TPU v7x, 32 devices: a whole 2x2x4 slice. The times are simulated.
32 devices in a mesh: dp: 8 (over y, x, core), mp: 4 (over z).
Axes of the slice: x: 2, y: 2, z: 4, core: 2. Of those that a mesh axis runs over, the one named last changes fastest.
Arguments:
- layer_input: bfloat16 [16384, 2048], P(('dp', 'mp')), may hold values from -6 to 6
- segments: int32 [16384], P('dp'), may hold values from 0 to 2, as said below
- padding: int32 [16384], P('dp'), may hold values from 0 to 1, as said below
- w_query: bfloat16 [2048, 2048], P('dp', 'mp'), may hold values from -0.125 to 0.125
- w_key: bfloat16 [2048, 2048], P('dp', 'mp'), may hold values from -0.125 to 0.125
- w_value: bfloat16 [2048, 2048], P('dp', 'mp'), may hold values from -0.125 to 0.125
- w_out: bfloat16 [2048, 2048], P('dp', 'mp'), may hold values from -2 to 2
- w_gate: bfloat16 [2048, 8192], P('dp', 'mp'), may hold values from -0.125 to 0.125
- w_up: bfloat16 [2048, 8192], P('dp', 'mp'), may hold values from -0.125 to 0.125
- w_down: bfloat16 [2048, 8192], P('dp', 'mp'), may hold values from -0.0625 to 0.0625
- cotangent: bfloat16 [16384, 2048], P(('dp', 'mp')), may hold values from -6 to 6
Outputs:
- output: bfloat16 [16384, 2048], P(('dp', 'mp'))
- d_input: float32 [16384, 2048], P(('dp', 'mp'))
- g_query: float32 [2048, 2048], P('dp', 'mp')
- g_key: float32 [2048, 2048], P('dp', 'mp')
- g_value: float32 [2048, 2048], P('dp', 'mp')
- g_out: float32 [2048, 2048], P('dp', 'mp')
- g_gate: float32 [2048, 8192], P('dp', 'mp')
- g_up: float32 [2048, 8192], P('dp', 'mp')
- g_down: float32 [2048, 8192], P('dp', 'mp')
Inputs may be any that keep to these rules, and one draw needn't show every extreme that they name: `segments`: each sequence holds three documents numbered 0, 1, 2 in order: the first and the last have 200 to 511 tokens each, the middle one the rest. `padding`: in each sequence the tokens with flag 1 form a nonempty tail lying within its last document.
All inputs are finite; a program needn't handle non-finite values.
Results may differ from a plain program's by a relative error of at most 0.023.
Values may be sent and summed in bfloat16 or wider, within the bound.
A program may use at most 256 MiB of HBM per device.

v0:
```python
import jax
import jax.numpy as jnp
from jax import lax
from jax.sharding import PartitionSpec as P

HD = 128
BLOCK = 512


eps = 1e-05


def layer_norm(tok_rows):
    average = jnp.mean(tok_rows, axis=-1, keepdims=True)
    centred = tok_rows - average
    variance = jnp.mean(centred * centred, axis=-1, keepdims=True)
    return centred * lax.rsqrt(variance + eps)


def swiglu(gate, up_lin):
    return jax.nn.silu(gate) * up_lin


def rope_tables(length, head_size):
    half_size = head_size // 2
    positions = jnp.arange(length).astype(jnp.float32)[:, None]
    frequency = 10000.0 ** (-jnp.arange(half_size).astype(jnp.float32) / half_size)
    angles = positions * frequency[None, :]
    return (jnp.cos(angles), jnp.sin(angles))


def rotate(per_head, cos_tab, sin_tab):
    half_size = per_head.shape[-1] // 2
    front_half = per_head[..., :half_size]
    back_half = per_head[..., half_size:]
    cos_part = cos_tab[:, None, :]
    sin_part = sin_tab[:, None, :]
    return jnp.concatenate(
        [
            front_half * cos_part - back_half * sin_part,
            back_half * cos_part + front_half * sin_part,
        ],
        axis=-1,
    )


def visible(segment, padding, offset, count):
    q_pos = offset + jnp.arange(count)
    k_pos = jnp.arange(segment.shape[0])
    seg_rows = lax.dynamic_slice_in_dim(segment, offset, count)
    causal = k_pos[None, :] <= q_pos[:, None]
    same_doc = seg_rows[:, None] == segment[None, :]
    real_key = (padding[None, :] == 0) | (k_pos[None, :] == q_pos[:, None])
    return causal & same_doc & real_key


def block_scores(q_blk, key_rows, allowed):
    raw = jnp.einsum("qhd,khd->hqk", q_blk, key_rows, preferred_element_type=jnp.float32) * HD ** (
        -0.5
    )
    return jnp.where(allowed[None], raw, -1e30)


def times_t(left, right):
    return lax.dot_general(
        left, right, (((1,), (1,)), ((), ())), preferred_element_type=jnp.float32
    )


def over_rows(left, right):
    return lax.dot_general(
        left, right, (((0,), (0,)), ((), ())), preferred_element_type=jnp.float32
    )


def body(
    layer_input, segments, padding, w_query, w_key, w_value, w_out, w_gate, w_up, w_down, cotangent
):
    att_mats = (
        lax.all_gather(w_query, "dp", axis=0, tiled=True),
        lax.all_gather(w_key, "dp", axis=0, tiled=True),
        lax.all_gather(w_value, "dp", axis=0, tiled=True),
        lax.all_gather(w_out, "dp", axis=0, tiled=True),
    )
    mlp_mats = (
        lax.all_gather(w_gate, "dp", axis=0, tiled=True),
        lax.all_gather(w_up, "dp", axis=0, tiled=True),
        lax.all_gather(w_down, "dp", axis=0, tiled=True),
    )
    full_query, full_key, full_value, full_out = att_mats
    full_gate, full_up, full_down = mlp_mats
    n_local = full_query.shape[1] // HD
    x_own = layer_input.astype(jnp.float32)
    norm1_own, norm1_pull = jax.vjp(layer_norm, x_own)
    norm1_low = norm1_own.astype(jnp.bfloat16)
    norm1_full = lax.all_gather(norm1_low, "mp", axis=0, tiled=True)
    length = norm1_full.shape[0]
    cos_tab, sin_tab = rope_tables(length, HD)
    q_lin = jnp.dot(norm1_full, full_query, preferred_element_type=jnp.float32).reshape(
        length, n_local, HD
    )
    k_lin = jnp.dot(norm1_full, full_key, preferred_element_type=jnp.float32).reshape(
        length, n_local, HD
    )
    values = (
        jnp.dot(norm1_full, full_value, preferred_element_type=jnp.float32)
        .astype(jnp.bfloat16)
        .reshape(length, n_local, HD)
    )
    queries = rotate(q_lin, cos_tab, sin_tab).astype(jnp.bfloat16)
    key_rows = rotate(k_lin, cos_tab, sin_tab).astype(jnp.bfloat16)
    offsets = jnp.arange(length // BLOCK) * BLOCK

    def forward_block(offset):
        q_blk = lax.dynamic_slice_in_dim(queries, offset, BLOCK, 0)
        scores = block_scores(q_blk, key_rows, visible(segments, padding, offset, BLOCK))
        row_max = jnp.max(scores, axis=-1, keepdims=True)
        weights = jnp.exp(scores - row_max)
        total = jnp.sum(weights, axis=-1, keepdims=True)
        prob_low = (weights / total).astype(jnp.bfloat16)
        block_out = jnp.einsum("hqk,khd->qhd", prob_low, values, preferred_element_type=jnp.float32)
        return (block_out.astype(jnp.bfloat16), (row_max + jnp.log(total))[..., 0])

    att_blocks, lse_blocks = lax.map(forward_block, offsets)
    attended = att_blocks.reshape(length, n_local * HD)
    attn_own = lax.psum_scatter(
        times_t(attended, full_out).astype(jnp.bfloat16), "mp", scatter_dimension=0, tiled=True
    ).astype(jnp.float32)
    hidden_own = x_own + attn_own
    norm2_own, norm2_pull = jax.vjp(layer_norm, hidden_own)
    norm2_low = norm2_own.astype(jnp.bfloat16)
    norm2_full = lax.all_gather(norm2_low, "mp", axis=0, tiled=True)
    gate = jnp.dot(norm2_full, full_gate, preferred_element_type=jnp.float32)
    up_lin = jnp.dot(norm2_full, full_up, preferred_element_type=jnp.float32)
    act, act_pull = jax.vjp(swiglu, gate, up_lin)
    act_low = act.astype(jnp.bfloat16)
    mlp_own = lax.psum_scatter(
        times_t(act_low, full_down).astype(jnp.bfloat16), "mp", scatter_dimension=0, tiled=True
    ).astype(jnp.float32)
    output = (hidden_own + mlp_own).astype(jnp.bfloat16)
    cot_full = lax.all_gather(cotangent, "mp", axis=0, tiled=True)
    d_act = jnp.dot(cot_full, full_down, preferred_element_type=jnp.float32)
    g_down = over_rows(cot_full, act_low)
    d_gate_f, d_up_f = act_pull(d_act)
    d_gate = d_gate_f.astype(jnp.bfloat16)
    d_up = d_up_f.astype(jnp.bfloat16)
    g_gate = over_rows(norm2_full, d_gate)
    g_up = over_rows(norm2_full, d_up)
    d_norm2 = lax.psum_scatter(
        (times_t(d_gate, full_gate) + times_t(d_up, full_up)).astype(jnp.bfloat16),
        "mp",
        scatter_dimension=0,
        tiled=True,
    ).astype(jnp.float32)
    d_hidden = cotangent.astype(jnp.float32) + norm2_pull(d_norm2)[0]
    d_hidden_low = d_hidden.astype(jnp.bfloat16)
    dh_full = lax.all_gather(d_hidden_low, "mp", axis=0, tiled=True)
    g_out = over_rows(dh_full, attended)
    d_attended = (
        jnp.dot(dh_full, full_out, preferred_element_type=jnp.float32)
        .astype(jnp.bfloat16)
        .reshape(length, n_local, HD)
    )

    def backward_block(running, element):
        d_keys, d_values = running
        offset, lse_blk = element
        q_blk = lax.dynamic_slice_in_dim(queries, offset, BLOCK, 0)
        grad_blk = lax.dynamic_slice_in_dim(d_attended, offset, BLOCK, 0)
        scores = block_scores(q_blk, key_rows, visible(segments, padding, offset, BLOCK))
        probs = jnp.exp(scores - lse_blk[..., None])
        prob_low = probs.astype(jnp.bfloat16)
        d_probs = jnp.einsum("qhd,khd->hqk", grad_blk, values, preferred_element_type=jnp.float32)
        d_values = d_values + jnp.einsum(
            "hqk,qhd->khd", prob_low, grad_blk, preferred_element_type=jnp.float32
        )
        row_dot = jnp.sum(probs * d_probs, axis=-1, keepdims=True)
        d_scores = (probs * (d_probs - row_dot)).astype(jnp.bfloat16)
        d_q_blk = jnp.einsum(
            "hqk,khd->qhd", d_scores, key_rows, preferred_element_type=jnp.float32
        ) * HD ** (-0.5)
        d_keys = d_keys + jnp.einsum(
            "hqk,qhd->khd", d_scores, q_blk, preferred_element_type=jnp.float32
        ) * HD ** (-0.5)
        return ((d_keys, d_values), d_q_blk)

    zero_heads = jnp.zeros((length, n_local, HD), jnp.float32)
    (d_keys, d_values), d_q_blocks = lax.scan(
        backward_block, (zero_heads, zero_heads), (offsets, lse_blocks)
    )
    d_queries = d_q_blocks.reshape(length, n_local, HD)
    d_q_lin = (
        rotate(d_queries, cos_tab, -sin_tab).reshape(length, n_local * HD).astype(jnp.bfloat16)
    )
    d_k_lin = rotate(d_keys, cos_tab, -sin_tab).reshape(length, n_local * HD).astype(jnp.bfloat16)
    d_v_lin = d_values.reshape(length, n_local * HD).astype(jnp.bfloat16)
    g_query = over_rows(norm1_full, d_q_lin)
    g_key = over_rows(norm1_full, d_k_lin)
    g_value = over_rows(norm1_full, d_v_lin)
    d_norm1 = lax.psum_scatter(
        (
            times_t(d_q_lin, full_query) + times_t(d_k_lin, full_key) + times_t(d_v_lin, full_value)
        ).astype(jnp.bfloat16),
        "mp",
        scatter_dimension=0,
        tiled=True,
    ).astype(jnp.float32)
    d_input = d_hidden + norm1_pull(d_norm1)[0]
    summed = (
        lax.psum_scatter(
            g_query.astype(jnp.bfloat16), "dp", scatter_dimension=0, tiled=True
        ).astype(jnp.float32),
        lax.psum_scatter(g_key.astype(jnp.bfloat16), "dp", scatter_dimension=0, tiled=True).astype(
            jnp.float32
        ),
        lax.psum_scatter(
            g_value.astype(jnp.bfloat16), "dp", scatter_dimension=0, tiled=True
        ).astype(jnp.float32),
        lax.psum_scatter(g_out.astype(jnp.bfloat16), "dp", scatter_dimension=0, tiled=True).astype(
            jnp.float32
        ),
        lax.psum_scatter(g_gate.astype(jnp.bfloat16), "dp", scatter_dimension=0, tiled=True).astype(
            jnp.float32
        ),
        lax.psum_scatter(g_up.astype(jnp.bfloat16), "dp", scatter_dimension=0, tiled=True).astype(
            jnp.float32
        ),
        lax.psum_scatter(g_down.astype(jnp.bfloat16), "dp", scatter_dimension=0, tiled=True).astype(
            jnp.float32
        ),
    )
    return (
        output,
        d_input,
        summed[0],
        summed[1],
        summed[2],
        summed[3],
        summed[4],
        summed[5],
        summed[6],
    )


def solution(mesh):
    placed = (
        P(("dp", "mp"), None),
        P("dp"),
        P("dp"),
        P("dp", "mp"),
        P("dp", "mp"),
        P("dp", "mp"),
        P("dp", "mp"),
        P("dp", "mp"),
        P("dp", "mp"),
        P("dp", "mp"),
        P(("dp", "mp"), None),
    )
    return jax.shard_map(
        body,
        mesh=mesh,
        in_specs=placed,
        out_specs=(
            P(("dp", "mp"), None),
            P(("dp", "mp"), None),
            P("dp", "mp"),
            P("dp", "mp"),
            P("dp", "mp"),
            P("dp", "mp"),
            P("dp", "mp"),
            P("dp", "mp"),
            P("dp", "mp"),
        ),
        check_vma=False,
    )
```

profile of v0, /device:TPU:1, one launch (start us, length us, event | category | flops | bytes accessed | tf_op | source)
XLA Modules:
  0.0 2092.3 jit_solution(6044259909673190893)
XLA Ops:
  22.8 17.5 all-gather.18.cloned.1.call-done
  40.3 151.6 %all-gather.12.cloned.1.call-done = bf16[2048,2048]{1,0:T(8,128)(2,1)} async-done(((bf16[512,2048]{1,0:T(8,128)(2,1)}), bf16[2048,2048]{1,0:T(8,128)(2,1)}) %all-gather.12.cloned.1.call-update) | async-done | bytes 8388624 | tf_op jit(solution)/shard_map/all_gather | solution.py:96
  203.0 17.2 all-gather.16.cloned.1.call-done
  236.1 13.8 all-gather.14.cloned.1.call-done
  277.1 87.2 %while.27 = (s32[]{:T(128)}, bf16[4,512,4,128]{3,2,1,0:T(4,128)(2,1)}, f32[4,4,512]{2,1,0:T(4,128)}, s32[4]{0:T(128)S(1)}, s32[2048]{0:T(1024)S(1)}, /*index=5*/...) while((s32[]{:T(128)}, ...), condition=%wide.region_5.6_spmd, body=%wide.region_2.5_spmd.sunk | while | flops 2204369408 | bytes 69302488 | solution.py:124
  376.1 143.2 %reduce-scatter.12.cloned.1.call-done = bf16[512,2048]{1,0:T(8,128)(2,1)} async-done(((bf16[2048,2048]{1,0:T(8,128)(2,1)}), bf16[512,2048]{1,0:T(8,128)(2,1)}) %reduce-scatter.12.cloned.1.call-update) | async-done | bytes 2097168 | tf_op jit(solution)/shard_map/reduce_scatter | solution.py:126
  527.9 48.9 %all-gather.26.cloned.1.call-done = bf16[2048,2048]{1,0:T(8,128)(2,1)} async-done(((bf16[256,2048]{1,0:T(8,128)(2,1)}), bf16[2048,2048]{1,0:T(8,128)(2,1)}) %all-gather.26.cloned.1.call-update) | async-done | bytes 8388624 | tf_op jit(solution)/shard_map/all_gather | solution.py:87
  576.9 151.6 %all-gather.22.cloned.1.call-done = bf16[2048,2048]{1,0:T(8,128)(2,1)} async-done(((bf16[512,2048]{1,0:T(8,128)(2,1)}), bf16[2048,2048]{1,0:T(8,128)(2,1)}) %all-gather.22.cloned.1.call-update) | async-done | bytes 8388624 | tf_op jit(solution)/shard_map/all_gather | solution.py:132
  728.5 24.3 %fusion.65 = f32[2048,2048]{1,0:T(8,128)} fusion(bf16[2048,2048]{1,0:T(8,128)(2,1)} %all-gather.22.cloned.1.call-done, bf16[2048,2048]{1,0:T(8,128)(2,1)} %all-gather.26.cloned.1.call-done), kind=kOutput, calls=%fused_computation.137 | convolution fusion | flops 17179869184 | bytes 33554432 | tf_op jit(solution)/shard_map/dot_general | solution.py:134
  752.8 30.4 %all-gather.24.cloned.1.call-done = bf16[2048,2048]{1,0:T(8,128)(2,1)} async-done(((bf16[256,2048]{1,0:T(8,128)(2,1)}), bf16[2048,2048]{1,0:T(8,128)(2,1)}) %all-gather.24.cloned.1.call-update) | async-done | bytes 8388624 | tf_op jit(solution)/shard_map/all_gather | solution.py:86
  783.2 24.1 %fusion.64 = f32[2048,2048]{1,0:T(8,128)} fusion(bf16[2048,2048]{1,0:T(8,128)(2,1)} %all-gather.22.cloned.1.call-done, bf16[2048,2048]{1,0:T(8,128)(2,1)} %all-gather.24.cloned.1.call-done), kind=kOutput, calls=%fused_computation.136 | convolution fusion | flops 17179869184 | bytes 33554432 | tf_op jit(solution)/shard_map/dot_general | solution.py:133
  807.4 126.7 %all-gather.30.cloned.1.call-done = bf16[2048,2048]{1,0:T(8,128)(2,1)} async-done(((bf16[512,2048]{1,0:T(8,128)(2,1)}), bf16[2048,2048]{1,0:T(8,128)(2,1)}) %all-gather.30.cloned.1.call-update) | async-done | bytes 8388624 | tf_op jit(solution)/shard_map/all_gather | solution.py:141
  934.1 54.7 %all-gather.28.cloned.1.call-done = bf16[2048,2048]{1,0:T(8,128)(2,1)} async-done(((bf16[256,2048]{1,0:T(8,128)(2,1)}), bf16[2048,2048]{1,0:T(8,128)(2,1)}) %all-gather.28.cloned.1.call-update) | async-done | bytes 8388624 | tf_op jit(solution)/shard_map/all_gather | solution.py:88
  988.9 34.9 %multiply_convert_fusion.1 = (bf16[2048,2048]{1,0:T(8,128)(2,1)}, bf16[2048,2048]{1,0:T(8,128)(2,1)}, bf16[2048,2048]{1,0:T(8,128)(2,1)}) fusion(f32[2048,2048]{1,0:T(8,128)} %fusion.64, f32[2048,2048]{1,0:T(8,128)} %fusion.65, bf16[2048,2048]{1,0:T(8,128)(2,1)} %all-gather.30.cloned.1.call-done, bf16[2048,2048]{1,0:T(8,128)(2,1)} %all-gather.28.cloned.1.call-done), kind=kOutput, calls=%fused_computation.59 | convolution fusion | flops 17246978048 | bytes 75497472 | tf_op jit(solution)/shard_map/dot_general | solution.py:142
  1023.8 24.3 %fusion.66 = f32[2048,2048]{1,0:T(8,128)} fusion(bf16[2048,2048]{1,0:T(8,128)(2,1)} %get-tuple-element.302, bf16[2048,2048]{1,0:T(8,128)(2,1)} %all-gather.24.cloned.1.call-done), kind=kOutput, calls=%fused_computation.138 | convolution fusion | flops 17179869184 | bytes 33554432 | tf_op jit(solution)/shard_map/dot_general | solution.py:65
  1048.1 25.7 %add_convert_fusion.1 = bf16[2048,2048]{1,0:T(8,128)(2,1)} fusion(f32[2048,2048]{1,0:T(8,128)} %fusion.66, bf16[2048,2048]{1,0:T(8,128)(2,1)} %get-tuple-element.301, bf16[2048,2048]{1,0:T(8,128)(2,1)} %all-gather.26.cloned.1.call-done), kind=kOutput, calls=%fused_computation.58 | convolution fusion | flops 17188257792 | bytes 41943040 | tf_op jit(solution)/shard_map/dot_general | solution.py:65
  1073.9 144.0 %reduce-scatter.16.cloned.1.call-done = bf16[512,2048]{1,0:T(8,128)(2,1)} async-done(((bf16[2048,2048]{1,0:T(8,128)(2,1)}), bf16[512,2048]{1,0:T(8,128)(2,1)}) %reduce-scatter.16.cloned.1.call-update) | async-done | bytes 2097168 | tf_op jit(solution)/shard_map/reduce_scatter | solution.py:149
  1226.5 24.2 %convert_bitcast_fusion = bf16[2048,2048]{0,1:T(8,128)(2,1)} fusion(bf16[2048,2048]{1,0:T(8,128)(2,1)} %get-tuple-element.303, bf16[2048,2048]{1,0:T(8,128)(2,1)} %all-gather.30.cloned.1.call-done), kind=kOutput, calls=%fused_computation.63 | convolution fusion | flops 17184063488 | bytes 25165824 | tf_op jit(solution)/shard_map/dot_general | solution.py:71
  1250.8 23.8 %convolution_convert_fusion = bf16[2048,2048]{1,0:T(8,128)(2,1)} fusion(bf16[2048,2048]{1,0:T(8,128)(2,1)} %all-gather.22.cloned.1.call-done, bf16[2048,2048]{1,0:T(8,128)(2,1)} %get-tuple-element.301), kind=kOutput, calls=%fused_computation.64 | convolution fusion | flops 17184063488 | bytes 25165824 | tf_op jit(solution)/shard_map/dot_general | solution.py:71
  1274.6 24.0 %convolution_convert_fusion.1 = bf16[2048,2048]{1,0:T(8,128)(2,1)} fusion(bf16[2048,2048]{1,0:T(8,128)(2,1)} %all-gather.22.cloned.1.call-done, bf16[2048,2048]{1,0:T(8,128)(2,1)} %get-tuple-element.302), kind=kOutput, calls=%fused_computation.65 | convolution fusion | flops 17184063488 | bytes 25165824 | tf_op jit(solution)/shard_map/dot_general | solution.py:71
  1298.8 78.6 %all-gather.32.cloned.1.call-done = bf16[2048,2048]{1,0:T(8,128)(2,1)} async-done(((bf16[512,2048]{1,0:T(8,128)(2,1)}), bf16[2048,2048]{1,0:T(8,128)(2,1)}) %all-gather.32.cloned.1.call-update) | async-done | bytes 8388624 | tf_op jit(solution)/shard_map/all_gather | solution.py:157
  1398.9 242.8 %while.28 = (s32[]{:T(128)}, f32[2048,4,128]{0,2,1:T(8,128)}, f32[2048,4,128]{0,2,1:T(8,128)}, f32[4,512,4,128]{3,1,0,2:T(8,128)}, s32[4]{0:T(128)S(1)}, /*index...) while((s32[]{:T(128)}, f32[2048,4,128]{0,2,1:T(8,128)}, ...), condition=%wide.region_15.16_spmd.clone, body=%wide.region_13.15_spmd.clone.sunk | while | flops 5443420672 | bytes 231823760 | solution.py:188
  1424.6 14.7 multiply_reduce_fusion.3
  1484.3 15.1 multiply_reduce_fusion.3
  1546.9 14.7 multiply_reduce_fusion.3
  1561.6 13.1 multiply_convert_fusion.5
  1606.6 14.9 multiply_reduce_fusion.3
  1705.2 13.1 fusion.67
  1726.7 17.3 add_convert_fusion
  1744.4 24.0 %convolution_convert_fusion.2 = bf16[2048,2048]{1,0:T(8,128)(2,1)} fusion(bf16[2048,2048]{1,0:T(8,128)(2,1)} %get-tuple-element.303, bf16[2048,2048]{1,0:T(8,128)(2,1)} %all-gather.28.cloned.1.call-done), kind=kOutput, calls=%fused_computation.66 | convolution fusion | flops 17184063488 | bytes 25165824 | tf_op jit(solution)/shard_map/dot_general | solution.py:65
  1784.6 145.0 %reduce-scatter.18.cloned.1.call-done = bf16[512,2048]{1,0:T(8,128)(2,1)} async-done(((bf16[2048,2048]{1,0:T(8,128)(2,1)}), bf16[512,2048]{1,0:T(8,128)(2,1)}) %reduce-scatter.18.cloned.1.call-update) | async-done | bytes 2097168 | tf_op jit(solution)/shard_map/reduce_scatter | solution.py:200
  1933.5 143.9 %reduce-scatter.14.cloned.1.call-done = bf16[512,2048]{1,0:T(8,128)(2,1)} async-done(((bf16[2048,2048]{1,0:T(8,128)(2,1)}), bf16[512,2048]{1,0:T(8,128)(2,1)}) %reduce-scatter.14.cloned.1.call-update) | async-done | bytes 2097168 | tf_op jit(solution)/shard_map/reduce_scatter | solution.py:137
  (325 shorter events, 460.7 us)
Async XLA Ops:
  7.2 33.2 %all-gather.18.cloned.1.call-start = ((), (), s32[]{:S(2)}) async-start(), calls=%async_computation.14 | async-start | bytes 2359296 | tf_op jit(solution)/shard_map/all_gather | solution.py:82
  7.9 184.0 %all-gather.12.cloned.1.call-start = ((), (), s32[]{:S(2)}) async-start(), calls=%async_computation.11 | async-start | bytes 10485760 | tf_op jit(solution)/shard_map/all_gather | solution.py:96
  15.3 204.9 %all-gather.16.cloned.1.call-start = ((), (), s32[]{:S(2)}) async-start(), calls=%async_computation.13 | async-start | bytes 2359296 | tf_op jit(solution)/shard_map/all_gather | solution.py:81
  16.0 233.9 %all-gather.14.cloned.1.call-start = ((), (), s32[]{:S(2)}) async-start(), calls=%async_computation.12 | async-start | bytes 2359296 | tf_op jit(solution)/shard_map/all_gather | solution.py:80
  16.6 347.8 %all-gather.20.cloned.1.call-start = ((), (), s32[]{:S(2)}) async-start(), calls=%async_computation.15 | async-start | bytes 2359296 | tf_op jit(solution)/shard_map/all_gather | solution.py:83
  17.2 502.1 %reduce-scatter.12.cloned.1.call-start = ((), (), s32[]{:S(2)}) async-start(), calls=%async_computation.16 | async-start | bytes 10485760 | tf_op jit(solution)/shard_map/reduce_scatter | solution.py:126
  22.8 243.0 %copy-start.15 = (f32[2048,64]{1,0:T(8,128)}, f32[2048,64]{1,0:T(8,128)S(1)}, u32[]{:S(2)}) copy-start(f32[2048,64]{1,0:T(8,128)S(1)} %get-tuple-element.324) | copy-start | bytes 1572868
  375.3 201.6 %all-gather.26.cloned.1.call-start = ((), (), s32[]{:S(2)}) async-start(), calls=%async_computation.19 | async-start | bytes 9437184 | tf_op jit(solution)/shard_map/all_gather | solution.py:87
  376.0 352.5 %all-gather.22.cloned.1.call-start = ((), (), s32[]{:S(2)}) async-start(), calls=%async_computation.17 | async-start | bytes 10485760 | tf_op jit(solution)/shard_map/all_gather | solution.py:132
  525.8 257.4 %all-gather.24.cloned.1.call-start = ((), (), s32[]{:S(2)}) async-start(), calls=%async_computation.18 | async-start | bytes 9437184 | tf_op jit(solution)/shard_map/all_gather | solution.py:86
  526.6 407.5 %all-gather.30.cloned.1.call-start = ((), (), s32[]{:S(2)}) async-start(), calls=%async_computation.22 | async-start | bytes 10485760 | tf_op jit(solution)/shard_map/all_gather | solution.py:141
  527.1 461.7 %all-gather.28.cloned.1.call-start = ((), (), s32[]{:S(2)}) async-start(), calls=%async_computation.20 | async-start | bytes 9437184 | tf_op jit(solution)/shard_map/all_gather | solution.py:88
  527.9 690.0 %reduce-scatter.16.cloned.1.call-start = ((), (), s32[]{:S(2)}) async-start(), calls=%async_computation.23 | async-start | bytes 10485760 | tf_op jit(solution)/shard_map/reduce_scatter | solution.py:149
  1073.8 147.5 %copy-start.30 = (f32[512]{0:T(512)S(1)}, f32[512]{0:T(512)}, u32[]{:S(2)}) copy-start(f32[512]{0:T(512)} %copy-done.29) | copy-start | bytes 6148
  1073.9 303.5 %all-gather.32.cloned.1.call-start = ((), (), s32[]{:S(2)}) async-start(), calls=%async_computation.24 | async-start | bytes 10485760 | tf_op jit(solution)/shard_map/all_gather | solution.py:157
  1226.5 542.0 %reduce-scatter.32.cloned.1.call-start = ((), (), s32[]{:S(2)}) async-start(), calls=%async_computation.32 | async-start | bytes 9437184 | tf_op jit(solution)/shard_map/reduce_scatter | solution.py:228
  1250.7 520.3 %reduce-scatter.30.cloned.1.call-start = ((), (), s32[]{:S(2)}) async-start(), calls=%async_computation.31 | async-start | bytes 9437184 | tf_op jit(solution)/shard_map/reduce_scatter | solution.py:225
  1274.6 499.4 %reduce-scatter.28.cloned.1.call-start = ((), (), s32[]{:S(2)}) async-start(), calls=%async_computation.30 | async-start | bytes 9437184 | tf_op jit(solution)/shard_map/reduce_scatter | solution.py:222
  1298.7 478.1 %reduce-scatter.26.cloned.1.call-start = ((), (), s32[]{:S(2)}) async-start(), calls=%async_computation.29 | async-start | bytes 2359296 | tf_op jit(solution)/shard_map/reduce_scatter | solution.py:219
  1386.9 391.8 %reduce-scatter.24.cloned.1.call-start = ((), (), s32[]{:S(2)}) async-start(), calls=%async_computation.28 | async-start | bytes 2359296 | tf_op jit(solution)/shard_map/reduce_scatter | solution.py:216
  1653.7 126.7 %reduce-scatter.22.cloned.1.call-start = ((), (), s32[]{:S(2)}) async-start(), calls=%async_computation.27 | async-start | bytes 2359296 | tf_op jit(solution)/shard_map/reduce_scatter | solution.py:213
  1686.2 96.7 %reduce-scatter.20.cloned.1.call-start = ((), (), s32[]{:S(2)}) async-start(), calls=%async_computation.26 | async-start | bytes 2359296 | tf_op jit(solution)/shard_map/reduce_scatter | solution.py:210
  1704.9 224.7 %reduce-scatter.18.cloned.1.call-start = ((), (), s32[]{:S(2)}) async-start(), calls=%async_computation.25 | async-start | bytes 10485760 | tf_op jit(solution)/shard_map/reduce_scatter | solution.py:200
  1744.0 333.4 %reduce-scatter.14.cloned.1.call-start = ((), (), s32[]{:S(2)}) async-start(), calls=%async_computation.21 | async-start | bytes 10485760 | tf_op jit(solution)/shard_map/reduce_scatter | solution.py:137
  1771.0 158.6 %copy-start.5 = (bf16[512,2048]{1,0:T(8,128)(2,1)S(1)}, bf16[512,2048]{1,0:T(8,128)(2,1)}, u32[]{:S(2)}) copy-start(bf16[512,2048]{1,0:T(8,128)(2,1)} %param.15) | copy-start | bytes 6291460
  1771.0 158.6 %copy-start.28 = (f32[512]{0:T(512)S(1)}, f32[512]{0:T(512)}, u32[]{:S(2)}) copy-start(f32[512]{0:T(512)} %copy-done.27) | copy-start | bytes 6148
  1776.8 155.4 %copy-start.39 = (f32[512]{0:T(512)S(1)}, f32[512]{0:T(512)}, u32[]{:S(2)}) copy-start(f32[512]{0:T(512)} %copy-done.38) | copy-start | bytes 6148
  1776.8 155.5 %copy-start.33 = (f32[512]{0:T(512)S(1)}, f32[512]{0:T(512)}, u32[]{:S(2)}) copy-start(f32[512]{0:T(512)} %copy-done.32) | copy-start | bytes 6148
  1784.6 292.7 %copy-start.26 = (f32[512]{0:T(512)S(1)}, f32[512]{0:T(512)}, u32[]{:S(2)}) copy-start(f32[512]{0:T(512)} %copy-done.24) | copy-start | bytes 6148
  1784.6 292.7 %copy-start.31 = (f32[512]{0:T(512)S(1)}, f32[512]{0:T(512)}, u32[]{:S(2)}) copy-start(f32[512]{0:T(512)} %copy-done.29) | copy-start | bytes 6148
  1784.6 292.7 %copy-start.35 = (f32[512]{0:T(512)S(1)}, f32[512]{0:T(512)}, u32[]{:S(2)}) copy-start(f32[512]{0:T(512)} %copy-done.34) | copy-start | bytes 6148
  1784.6 292.7 %copy-start.41 = (f32[512]{0:T(512)S(1)}, f32[512]{0:T(512)}, u32[]{:S(2)}) copy-start(f32[512]{0:T(512)} %copy-done.40) | copy-start | bytes 6148
  (54 other events, 1016.8 us)
Sparse Core Ops, SparseCore 0:
  9.9 30.3 all-gather.17
  42.5 149.4 all-gather.11
  193.8 26.3 all-gather.15
  222.0 27.8 all-gather.13
  251.6 27.8 all-gather.19
  375.4 143.8 reduce-scatter.11
  521.1 55.6 all-gather.25
  579.0 149.4 all-gather.21
  730.4 52.8 all-gather.23
  784.6 149.4 all-gather.29
  936.0 52.8 all-gather.27
  1074.0 143.8 reduce-scatter.15
  1226.6 150.7 all-gather.31
  1380.7 69.2 reduce-scatter.31
  1453.7 71.2 reduce-scatter.29
  1528.3 71.2 reduce-scatter.27
  1603.1 41.1 reduce-scatter.25
  1653.8 39.1 reduce-scatter.23
  1696.6 41.2 reduce-scatter.21
  1741.6 41.1 reduce-scatter.19
  1785.3 144.3 reduce-scatter.17
  1932.1 145.1 reduce-scatter.13
where the time goes:
time: 2100 us; the launch traced here: 2090 us
  waiting for transfers between devices  1270 us (60%)
  matrix products  562 us (27%)
  other arithmetic  172 us (8%)
  local copies, waits for them, and re-layouts  51.4 us (2%)
    all_gather x1, waiting for transfers between devices, body(): norm2_full = lax.all_gather(norm2_low, 'mp', axis=0, tiled=True)  152 us
    all_gather x1, waiting for transfers between devices, body(): norm1_full = lax.all_gather(norm1_low, 'mp', axis=0, tiled=True)  152 us
    reduce_scatter x1, waiting for transfers between devices, body(): lax.psum_scatter((times_t(d_q_lin, full_query) + times_t(d_k_lin, full_ke...  145 us
    reduce_scatter x1, waiting for transfers between devices, body(): lax.psum_scatter((times_t(d_gate, full_gate) + times_t(d_up, full_up)).as...  144 us
    reduce_scatter x1, waiting for transfers between devices, body(): lax.psum_scatter(times_t(act_low, full_down).astype(jnp.bfloat16), 'mp',...  144 us
    reduce_scatter x1, waiting for transfers between devices, body(): lax.psum_scatter(times_t(attended, full_out).astype(jnp.bfloat16), 'mp',...  143 us
    all_gather x1, waiting for transfers between devices, body(): cot_full = lax.all_gather(cotangent, 'mp', axis=0, tiled=True)  127 us
    dot_general x7, matrix products, times_t(): lax.dot_general(left, right, (((1,), (1,)), ((), ())), preferred_element_...  123 us
  transfers between devices with their start and end apart: 22, of which 15 were waited for; matrix products, arithmetic and copies ran while one was open for 32% of the time, Pallas kernels for 0%

commit v1 on v0

v1 whole, which is shorter than its diff:
```python
import functools
import jax
import jax.numpy as jnp
from jax import lax
from jax.experimental import pallas as pl
from jax.experimental.pallas import tpu as pltpu
from jax.sharding import Mesh, PartitionSpec as P

HD = 128
SCALE = HD ** (-0.5)
LOG2E = 1.4426950408889634
NEG = -1e30
eps = 1e-05
NT = (((1,), (1,)), ((), ()))
TN = (((0,), (0,)), ((), ()))


def layer_norm(tok_rows):
    average = jnp.mean(tok_rows, axis=-1, keepdims=True)
    centred = tok_rows - average
    variance = jnp.mean(centred * centred, axis=-1, keepdims=True)
    return centred * lax.rsqrt(variance + eps)


def swiglu(gate, up_lin):
    return jax.nn.silu(gate) * up_lin


def dot(left, right, dims=(((1,), (0,)), ((), ()))):
    return lax.dot_general(left, right, dims, preferred_element_type=jnp.float32)


def low(value):
    return value.astype(jnp.bfloat16)

def visit_lists(pos, end, blk):
    first = pos[::blk]
    most = jnp.max(end.reshape(-1, blk), axis=1)
    met = (first[None, :] <= first[:, None]) & (most[None, :] >= first[:, None])
    count = jnp.sum(met, axis=1, dtype=jnp.int32)
    keys = jnp.argsort(~met, axis=1, stable=True).astype(jnp.int32)
    total = jnp.sum(count, dtype=jnp.int32)
    pairs = jnp.argsort(~met.reshape(-1), stable=True).astype(jnp.int32)
    return first, count, keys.reshape(-1), total.reshape(1), pairs


def turned(value, cos_ref, sin_ref, sign):
    return value * cos_ref[...] + sign * pltpu.roll(value, HD // 2, 1) * sin_ref[...]


def allowed_of(first_q, first_k, end_row):
    blk = end_row.shape[1]
    t = first_q + lax.broadcasted_iota(jnp.int32, (blk, 1), 0)
    u = first_k + lax.broadcasted_iota(jnp.int32, (1, blk), 1)
    return (u <= t) & (t <= end_row)


def forward_kernel(
    hpg, first, count, keys, q_lin, k_lin, v_lin, cos_ref, sin_ref, end_ref,
    att_ref, lse_ref, q_ref, k_ref, v_ref
):
    n_k, blk = end_ref.shape
    for h in range(hpg):
        cols = slice(h * HD, (h + 1) * HD)
        q_ref[:, cols] = turned(q_lin[:, cols], cos_ref, sin_ref, 1.0).astype(jnp.bfloat16)
        k_ref[:, cols] = turned(k_lin[:, cols], cos_ref, sin_ref, 1.0).astype(jnp.bfloat16)
        v_ref[:, cols] = v_lin[:, cols].astype(jnp.bfloat16)

    @pl.loop(0, n_k)
    def _(i):
        rows = pl.ds(pl.multiple_of(i * blk, blk), blk)

        def step(n, carry):
            j = keys[i * n_k + n]
            spot = pl.ds(pl.multiple_of(j * blk, blk), blk)
            allowed = allowed_of(first[i], first[j], end_ref[pl.ds(j, 1), :])
            out = []
            for h in range(hpg):
                cols = slice(h * HD, (h + 1) * HD)
                top, total, acc = carry[h]
                scores = dot(q_ref[rows, cols], k_ref[spot, cols], NT)
                scores = jnp.where(allowed, scores * (SCALE * LOG2E), NEG)
                new_top = jnp.maximum(top, jnp.max(scores, axis=1, keepdims=True))
                weights = jnp.exp2(scores - new_top)
                shrink = jnp.exp2(top - new_top)
                total = total * shrink + jnp.sum(weights, axis=1, keepdims=True)
                acc = acc * shrink + dot(weights.astype(jnp.bfloat16), v_ref[spot, cols])
                out.append((new_top, total, acc))
            return tuple(out)

        start = tuple(
            (
                jnp.full((blk, 1), NEG, jnp.float32),
                jnp.zeros((blk, 1), jnp.float32),
                jnp.zeros((blk, HD), jnp.float32),
            )
            for _ in range(hpg)
        )
        done = lax.fori_loop(0, count[i], step, start)
        for h in range(hpg):
            cols = slice(h * HD, (h + 1) * HD)
            top, total, acc = done[h]
            att_ref[rows, cols] = low(acc / total)
            lse_ref[rows, cols] = jnp.broadcast_to(top + jnp.log2(total), (blk, HD))


def attend(qkv, cos, sin, end_rows, lists, heads, hpg):
    length = qkv.shape[0]
    first, count, keys, _, _ = lists
    groups = heads // hpg
    wide = hpg * HD
    col = lambda k: pl.BlockSpec((length, wide), lambda g, *_: (0, k * groups + g))
    whole = lambda a: pl.BlockSpec(a.shape, lambda g, *_: (0, 0))
    low = jax.ShapeDtypeStruct((length, heads * HD), jnp.bfloat16)
    return pl.pallas_call(
        functools.partial(forward_kernel, hpg),
        grid_spec=pltpu.PrefetchScalarGridSpec(
            num_scalar_prefetch=3,
            grid=(groups,),
            in_specs=[col(0), col(1), col(2), whole(cos), whole(sin), whole(end_rows)],
            out_specs=[col(0)] * 5,
        ),
        out_shape=[low, jax.ShapeDtypeStruct(low.shape, jnp.float32), low, low, low],
        compiler_params=pltpu.CompilerParams(vmem_limit_bytes=48 * 2**20),
        cost_estimate=pl.CostEstimate(
            flops=2 * length * length * HD * heads,
            bytes_accessed=length * heads * HD * 24,
            transcendentals=heads * length * length // 2,
        ),
    )(first, count, keys, qkv, qkv, qkv, cos, sin, end_rows)


def backward_kernel(
    hpg, first, total, pairs, q_ref, k_ref, v_ref, grad_ref, att_ref, lse_ref,
    cos_ref, sin_ref, end_ref, dq_ref, dk_ref, dv_ref, dq_acc, dk_acc, dv_acc, delta
):
    n_k, blk = end_ref.shape
    dq_acc[...] = jnp.zeros_like(dq_acc)
    dk_acc[...] = jnp.zeros_like(dk_acc)
    dv_acc[...] = jnp.zeros_like(dv_acc)
    for h in range(hpg):
        cols = slice(h * HD, (h + 1) * HD)
        prod = grad_ref[:, cols].astype(jnp.float32) * att_ref[:, cols].astype(jnp.float32)
        delta[:, cols] = jnp.broadcast_to(jnp.sum(prod, axis=1, keepdims=True), prod.shape)

    def step(n, carry):
        code = pairs[n]
        i, j = code // n_k, code % n_k
        rows = pl.ds(pl.multiple_of(i * blk, blk), blk)
        spot = pl.ds(pl.multiple_of(j * blk, blk), blk)
        allowed = allowed_of(first[i], first[j], end_ref[pl.ds(j, 1), :])
        for h in range(hpg):
            cols = slice(h * HD, (h + 1) * HD)
            q, k, v, grad = q_ref[rows, cols], k_ref[spot, cols], v_ref[spot, cols], grad_ref[rows, cols]
            scores = dot(q, k, NT) * (SCALE * LOG2E)
            lse = lse_ref[rows, h * HD : h * HD + 1]
            probs = jnp.where(allowed, jnp.exp2(scores - lse), 0.0)
            d_probs = dot(grad, v, NT)
            d_scores = (probs * (d_probs - delta[rows, h * HD : h * HD + 1])).astype(jnp.bfloat16)
            dv_acc[spot, cols] += dot(probs.astype(jnp.bfloat16), grad, TN)
            dk_acc[spot, cols] += dot(d_scores, q, TN)
            dq_acc[rows, cols] += dot(d_scores, k)
        return carry

    lax.fori_loop(0, total[0], step, 0)
    for h in range(hpg):
        cols = slice(h * HD, (h + 1) * HD)
        dq_ref[:, cols] = turned(dq_acc[:, cols] * SCALE, cos_ref, sin_ref, -1.0).astype(jnp.bfloat16)
        dk_ref[:, cols] = turned(dk_acc[:, cols] * SCALE, cos_ref, sin_ref, -1.0).astype(jnp.bfloat16)
        dv_ref[:, cols] = dv_acc[:, cols].astype(jnp.bfloat16)


def attend_back(q, k, v, grad, att, lse, cos, sin, end_rows, lists, heads, hpg):
    length = q.shape[0]
    first, _, _, total, pairs = lists
    groups = heads // hpg
    wide = hpg * HD
    col = pl.BlockSpec((length, wide), lambda g, *_: (0, g))
    whole = lambda a: pl.BlockSpec(a.shape, lambda g, *_: (0, 0))
    low = jax.ShapeDtypeStruct((length, heads * HD), jnp.bfloat16)
    return pl.pallas_call(
        functools.partial(backward_kernel, hpg),
        grid_spec=pltpu.PrefetchScalarGridSpec(
            num_scalar_prefetch=3,
            grid=(groups,),
            in_specs=[col] * 6 + [whole(cos), whole(sin), whole(end_rows)],
            out_specs=[col] * 3,
            scratch_shapes=[pltpu.VMEM((length, wide), jnp.float32)] * 4,
        ),
        out_shape=[low] * 3,
        compiler_params=pltpu.CompilerParams(vmem_limit_bytes=48 * 2**20),
        cost_estimate=pl.CostEstimate(
            flops=5 * length * length * HD * heads,
            bytes_accessed=length * heads * HD * 20,
            transcendentals=heads * length * length // 2,
        ),
    )(first, total, pairs, q, k, v, grad, att, lse, cos, sin, end_rows)


def flip(value, axis):
    return lax.ppermute(value, axis, [(0, 1), (1, 0)])


def body(places, x, segments, padding, w_query, w_key, w_value, w_out, w_gate, w_up, w_down, cot):
    rest, core, high, lower = places
    pair = (core, high)
    c, h = lax.axis_index(core), lax.axis_index(high)
    same = c == h
    first_core = c == 0

    def swap(value):
        return lax.ppermute(value, pair, [(0, 0), (1, 2), (2, 1), (3, 3)])

    def gather_low(value):
        parts = [value]
        for axis in lower:
            parts = parts + [flip(part, axis) for part in parts]
        return parts

    def gather(value):
        parts = gather_low(value)
        return jnp.concatenate([piece for part in parts for piece in (part, flip(part, core))])

    def scatter(product, n_parts):
        far = []
        for part in reversed(range(n_parts)):
            mine, other = product(part)
            far.insert(0, (mine, flip(other, core)))
        sums = [mine.astype(jnp.float32) + other.astype(jnp.float32) for mine, other in far]
        for axis in reversed(lower):
            half = len(sums) // 2
            sums = [sums[k] + flip(low(sums[half + k]), axis).astype(jnp.float32) for k in range(half)]
        return sums[0]

    def gather_weight(shard):
        to_far0 = lax.ppermute(shard, pair, [(0, 1), (1, 2)])
        to_far1 = lax.ppermute(shard, pair, [(2, 1), (3, 2)])
        near = lax.ppermute(shard, pair, [(2, 0), (1, 3)])
        s0 = jnp.where(same, jnp.where(first_core, shard, near), to_far0)
        s1 = jnp.where(same, jnp.where(first_core, near, shard), to_far1)
        return lax.all_gather(jnp.concatenate([s0, s1]), rest, axis=0, tiled=True)

    def scatter_weight(partial):
        both = lax.psum_scatter(partial, rest, scatter_dimension=0, tiled=True)
        rows = both.shape[0] // 2
        s0, s1 = both[:rows], both[rows:]
        near = lax.ppermute(jnp.where(first_core, s1, s0), pair, [(0, 2), (3, 1)])
        from0 = lax.ppermute(s0, pair, [(1, 0), (2, 1)])
        from1 = lax.ppermute(s1, pair, [(1, 2), (2, 3)])
        kept = jnp.where(same, jnp.where(first_core, s0, s1), near)
        far = jnp.where(first_core, from0, from1)
        return kept.astype(jnp.float32) + far.astype(jnp.float32)

    own = x.shape[0]
    n_parts = 2 ** len(lower)
    length = 2 * n_parts * own
    cols = w_query.shape[1]
    heads = cols // HD
    blk = min(512, own)

    spot = jnp.int32(0)
    for axis in lower:
        spot = spot * 2 + lax.axis_index(axis)
    quarters = []
    order = [0]
    for k in range(len(lower)):
        order = order + [part + 2 ** (len(lower) - 1 - k) for part in order]
    for part in order:
        for other in (0, 1):
            quarters.append((c ^ other) * n_parts + (spot ^ part))
    position = jnp.concatenate([q * own + jnp.arange(own, dtype=jnp.int32) for q in quarters])
    marks = jnp.stack([segments, padding])
    marks = jnp.where(same, marks, flip(marks, core))
    seg, pad = marks[0], marks[1]
    last = jnp.sum((seg[None, :] <= seg[:, None]).astype(jnp.int32), axis=1) - 1
    end = jnp.where(pad == 0, last, jnp.arange(length, dtype=jnp.int32))
    end = jnp.concatenate([lax.dynamic_slice_in_dim(end, q * own, own) for q in quarters])
    lists = visit_lists(position, end, blk)
    end_rows = end.reshape(-1, blk)
    frequency = 10000.0 ** (-jnp.arange(HD // 2).astype(jnp.float32) / (HD // 2))
    angles = position.astype(jnp.float32)[:, None] * frequency[None, :]
    cos, sin = jnp.cos(angles), jnp.sin(angles)
    cos = jnp.concatenate([cos, cos], axis=1)
    sin = jnp.concatenate([-sin, sin], axis=1)

    x_own = swap(x).astype(jnp.float32)
    norm1_own, norm1_pull = jax.vjp(layer_norm, x_own)
    w_qkv = gather_weight(jnp.concatenate([w_query, w_key, w_value], axis=1))
    norm1 = gather(low(norm1_own))
    full_out = gather_weight(w_out)
    full_gate = gather_weight(w_gate)
    full_up = gather_weight(w_up)
    cot_own = swap(cot)
    cots = gather(cot_own)
    full_down = gather_weight(w_down)

    qkv = dot(norm1, w_qkv)
    attended, lse, q, k, v = attend(qkv, cos, sin, end_rows, lists, heads, 1)

    def halves(product, values):
        def of(part):
            lo = part * 2 * own
            both = low(product(*(value[lo : lo + 2 * own] for value in values)))
            return both[:own], both[own:]

        return of

    hidden = x_own + scatter(halves(lambda a: dot(a, full_out, NT), (attended,)), n_parts)
    norm2_own, norm2_pull = jax.vjp(layer_norm, hidden)
    norm2 = gather(low(norm2_own))
    gate = dot(norm2, full_gate)
    up_lin = dot(norm2, full_up)
    act, act_pull = jax.vjp(swiglu, gate, up_lin)
    act_low = low(act)
    d_act = dot(cots, full_down)
    d_gate_f, d_up_f = act_pull(d_act)
    d_gate, d_up = low(d_gate_f), low(d_up_f)
    d_norm2 = scatter(
        halves(lambda a, b: dot(a, full_gate, NT) + dot(b, full_up, NT), (d_gate, d_up)), n_parts
    )
    d_hidden = cot_own.astype(jnp.float32) + norm2_pull(d_norm2)[0]
    d_hiddens = gather(low(d_hidden))

    mlp = scatter(halves(lambda a: dot(a, full_down, NT), (act_low,)), n_parts)
    output = swap(low(hidden + mlp))
    g_down = scatter_weight(low(dot(cots, act_low, TN)))
    g_gate = scatter_weight(low(dot(norm2, d_gate, TN)))
    g_up = scatter_weight(low(dot(norm2, d_up, TN)))

    d_attended = low(dot(d_hiddens, full_out))
    dq, dk, dv = attend_back(q, k, v, d_attended, attended, lse, cos, sin, end_rows, lists, heads, 1)
    d_qkv = jnp.concatenate([dq, dk, dv], axis=1)
    d_norm1 = scatter(halves(lambda a: dot(a, w_qkv, NT), (d_qkv,)), n_parts)
    d_input = swap(low(d_hidden + norm1_pull(d_norm1)[0])).astype(jnp.float32)
    g_out = scatter_weight(low(dot(d_hiddens, attended, TN)))
    g_qkv = scatter_weight(low(dot(norm1, d_qkv, TN)))
    return (
        output,
        d_input,
        g_qkv[:, :cols],
        g_qkv[:, cols : 2 * cols],
        g_qkv[:, 2 * cols :],
        g_out,
        g_gate,
        g_up,
        g_down,
    )


def solution(mesh):
    dp, mp = mesh.devices.shape
    n_dp, n_mp = dp.bit_length() - 1, mp.bit_length() - 1
    dp_axes = tuple("d%d" % k for k in range(n_dp))
    mp_axes = tuple("m%d" % k for k in range(n_mp))
    fine = Mesh(mesh.devices.reshape((2,) * (n_dp + n_mp)), dp_axes + mp_axes)
    places = (dp_axes[:-1], dp_axes[-1], mp_axes[0], mp_axes[1:])
    tokens = P(dp_axes + mp_axes, None)
    weight = P(dp_axes, mp_axes)
    return jax.shard_map(
        functools.partial(body, places),
        mesh=fine,
        in_specs=(tokens, P(dp_axes), P(dp_axes)) + (weight,) * 7 + (tokens,),
        out_specs=(tokens, tokens) + (weight,) * 7,
        check_vma=False,
    )
```

time: 2100 us -> 1420 us (0.68)
  waiting for transfers between devices: 1270 us -> 717 us
  matrix products: 562 us -> 327 us
  starting transfers between devices: 1.5 us -> 137 us
  Pallas kernels: 0 us -> 92 us
  other arithmetic: 172 us -> 81 us
    ppermute x0 -> x59, waiting for transfers between devices: none -> 717 us  [the longest x25 344 us: flip(): return lax.ppermute(value, axis, [(0, 1), (1, 0)])]
    all_gather x11 -> x5, waiting for transfers between devices: 691 us -> 0.01 us  [gather_weight(): return lax.all_gather(jnp.concatenate([s0, s1]), rest, axis=0, tiled=True)]
    reduce_scatter x11 -> x5, waiting for transfers between devices: 577 us -> 0.05 us  [scatter_weight(): both = lax.psum_scatter(partial, rest, scatter_dimension=0, tiled=True)]
    dot_general x49 -> x20, matrix products: 562 us -> 327 us  [dot(): lax.dot_general(left, right, dims, preferred_element_type=jnp.float32)]
    ppermute x0 -> x59, starting transfers between devices: none -> 125 us  [the longest x5 28.6 us: scatter_weight(): from0 = lax.ppermute(s0, pair, [(1, 0), (2, 1)])]
    pallas_call x0 -> x2, Pallas kernels: none -> 92 us  [the longest x1 52 us: attend_back(): pl.pallas_call(functools.partial(backward_kernel, hpg), grid_spec=pltpu.P...]
    convert_element_type x15 -> x10, other arithmetic: 73.3 us -> 21.9 us  [the longest x8 19.3 us: low(): return value.astype(jnp.bfloat16)]
  transfers between devices with their start and end apart: 22 -> 69, of which waited for: 15 -> 25; matrix products, arithmetic and copies ran while one was open for 32% -> 25% of each run, Pallas kernels for 0% -> 7%
where the time goes in v1:
time: 1420 us; the launch traced here: 1410 us
  waiting for transfers between devices  717 us (50%)
  matrix products  327 us (23%)
  starting transfers between devices  137 us (10%)
  Pallas kernels  92 us (6%)
  other arithmetic  81 us (6%)
  local copies, waits for them, and re-layouts  36 us (3%)
  between operations  15.8 us (1%)
    ppermute x25, waiting for transfers between devices, flip(): return lax.ppermute(value, axis, [(0, 1), (1, 0)])  344 us
    dot_general x20, matrix products, dot(): lax.dot_general(left, right, dims, preferred_element_type=jnp.float32)  327 us
    ppermute x5, waiting for transfers between devices, gather_weight(): to_far1 = lax.ppermute(shard, pair, [(2, 1), (3, 2)])  183 us
    ppermute x5, waiting for transfers between devices, scatter_weight(): from1 = lax.ppermute(s1, pair, [(1, 2), (2, 3)])  147 us
    pallas_call x1, Pallas kernels, attend_back(): pl.pallas_call(functools.partial(backward_kernel, hpg), grid_spec=pltpu.P...  52 us
    pallas_call x1, Pallas kernels, attend(): pl.pallas_call(functools.partial(forward_kernel, hpg), grid_spec=pltpu.Pr...  40 us
    ppermute x5, waiting for transfers between devices, gather_weight(): to_far0 = lax.ppermute(shard, pair, [(0, 1), (1, 2)])  30 us
    ppermute x5, starting transfers between devices, scatter_weight(): from0 = lax.ppermute(s0, pair, [(1, 0), (2, 1)])  28.6 us
  transfers between devices with their start and end apart: 69, of which 25 were waited for; matrix products, arithmetic and copies ran while one was open for 25% of the time, Pallas kernels for 7%

profile of v1, /device:TPU:1, one launch (start us, length us, event | category | flops | bytes accessed | tf_op | source)
XLA Modules:
  0.0 1406.0 jit_solution(17219573709588420787)
XLA Ops:
  19.5 27.9 %collective-permute-done.7 = bf16[256,1536]{1,0:T(8,128)(2,1)S(1)} collective-permute-done((bf16[256,1536]{1,0:T(8,128)(2,1)S(1)}, bf16[256,1536]{1,0:T(8,128)(2,1)S(1)}, u32[]{:S(2)}, u32[]{:S(2)}) %collective-permute-start.7) | collective-permute-done | bytes 786464 | tf_op jit(solution)/shard_map/ppermute | solution.py:237
  82.0 60.6 %collective-permute-done.22 = bf16[256,2048]{1,0:T(8,128)(2,1)S(1)} collective-permute-done((bf16[256,2048]{1,0:T(8,128)(2,1)S(1)}, bf16[256,2048]{1,0:T(8,128)(2,1)S(1)}, u32[]{:S(2)}, u32[]{:S(2)}) %collective-permute-start.22) | collective-permute-done | bytes 1048608 | tf_op jit(solution)/shard_map/ppermute | solution.py:237
  142.7 22.3 %collective-permute-done.25 = bf16[256,2048]{1,0:T(8,128)(2,1)S(1)} collective-permute-done((bf16[256,2048]{1,0:T(8,128)(2,1)S(1)}, bf16[256,2048]{1,0:T(8,128)(2,1)S(1)}, u32[]{:S(2)}, u32[]{:S(2)}) %collective-permute-start.25) | collective-permute-done | bytes 1048608 | tf_op jit(solution)/shard_map/ppermute | solution.py:237
  177.3 64.1 %collective-permute-done.19 = bf16[256,2048]{1,0:T(8,128)(2,1)S(1)} collective-permute-done((bf16[256,2048]{1,0:T(8,128)(2,1)S(1)}, bf16[256,2048]{1,0:T(8,128)(2,1)S(1)}, u32[]{:S(2)}, u32[]{:S(2)}) %collective-permute-start.19) | collective-permute-done | bytes 1048608 | tf_op jit(solution)/shard_map/ppermute | solution.py:237
  241.4 22.4 %collective-permute-done.18 = bf16[256,2048]{1,0:T(8,128)(2,1)S(1)} collective-permute-done((bf16[256,2048]{1,0:T(8,128)(2,1)S(1)}, bf16[256,2048]{1,0:T(8,128)(2,1)S(1)}, u32[]{:S(2)}, u32[]{:S(2)}) %collective-permute-start.18) | collective-permute-done | bytes 1048608 | tf_op jit(solution)/shard_map/ppermute | solution.py:236
  273.7 35.1 %collective-permute-done.3 = bf16[512,2048]{1,0:T(8,128)(2,1)} collective-permute-done((bf16[512,2048]{1,0:T(8,128)(2,1)}, bf16[512,2048]{1,0:T(8,128)(2,1)}, u32[]{:S(2)}, u32[]{:S(2)}) %collective-permute-start.3) | collective-permute-done | bytes 2097184 | tf_op jit(solution)/shard_map/ppermute | solution.py:201
  313.3 22.4 %fusion.36.q_lin.k_lin.v_lin = f32[2048,1536]{1,0:T(8,128)} fusion(bf16[2048,1536]{1,0:T(8,128)(2,1)} %all-gather.6.cloned.1.call-done, bf16[512,2048]{1,0:T(8,128)(2,1)} %collective-permute-done.4, bf16[512,2048]{1,0:T(8,128)(2,1)} %collective-permute-done.3, bf16[512,2048]{1,0:T(8,128)(2,1)} %collective-permute-done.2, bf16[512,2048]{1,0:T(8,128)(2,1)} %fusion.9), kind=kOutput, calls=%fused_computation.75 | convolution fusion | flops 12918456320 | bytes 27262976 | tf_op jit(solution)/shard_map/dot_general | solution.py:30
  335.7 40.0 %shard_map.178 = (bf16[2048,512]{1,0:T(8,128)(2,1)S(1)}, f32[2048,512]{1,0:T(8,128)}, bf16[2048,512]{1,0:T(8,128)(2,1)}, bf16[2048,512]{1,0:T(8,128)(2,1)}, bf16[2048,512]{1,0:T(8,128)(2,1)}) custom-call(s32[4]{0:T(128)S(1)} %slice.126.first, s32[4]{0:T(128)S(1)} %get-tuple-element.30.count, s32[16]{0:T(128)S(1)} %reshape.124.keys, ...), custom_call_target="tpu_custom_call" | custom-call | flops 4294967296 | bytes 25165824 | tf_op jit(solution)/shard_map/pallas_call | solution.py:115
  388.5 15.3 %collective-permute-start.11 = (bf16[512,2048]{1,0:T(8,128)(2,1)}, bf16[512,2048]{1,0:T(8,128)(2,1)}, u32[]{:S(2)}, u32[]{:S(2)}) collective-permute-start(bf16[512,2048]{1,0:T(8,128)(2,1)} %slice.171), channel_id=1, source_target_pairs={{0,4},{4,0},{1,5},{5,1},{2,6},{6,2},{3,7},{7,3},{8,12},{12,8},{9,1... | collective-permute-start | bytes 6291464 | tf_op jit(solution)/shard_map/ppermute | solution.py:201
  419.2 13.5 collective-permute-done.30
  432.7 43.2 %collective-permute-done.13 = bf16[512,2048]{1,0:T(8,128)(2,1)} collective-permute-done((bf16[512,2048]{1,0:T(8,128)(2,1)}, bf16[512,2048]{1,0:T(8,128)(2,1)}, u32[]{:S(2)}, u32[]{:S(2)}) %collective-permute-start.13) | collective-permute-done | bytes 2097184 | tf_op jit(solution)/shard_map/ppermute | solution.py:201
  484.9 35.9 %collective-permute-done.32 = bf16[512,2048]{1,0:T(8,128)(2,1)S(1)} collective-permute-done((bf16[512,2048]{1,0:T(8,128)(2,1)}, bf16[512,2048]{1,0:T(8,128)(2,1)S(1)}, u32[]{:S(2)}, u32[]{:S(2)}) %collective-permute-start.32) | collective-permute-done | bytes 2097184 | tf_op jit(solution)/shard_map/ppermute | solution.py:201
  521.7 44.2 %collective-permute-done.15 = bf16[512,2048]{1,0:T(8,128)(2,1)} collective-permute-done((bf16[512,2048]{1,0:T(8,128)(2,1)}, bf16[512,2048]{1,0:T(8,128)(2,1)}, u32[]{:S(2)}, u32[]{:S(2)}) %collective-permute-start.15) | collective-permute-done | bytes 2097184 | tf_op jit(solution)/shard_map/ppermute | solution.py:201
  574.2 27.7 %fusion.47 = f32[2048,2048]{1,0:T(8,128)} fusion(bf16[2048,2048]{1,0:T(8,128)(2,1)} %all-gather.12.cloned.1.call-done, bf16[512,2048]{1,0:T(8,128)(2,1)} %collective-permute-done.16, bf16[512,2048]{1,0:T(8,128)(2,1)} %collective-permute-done.15, bf16[512,2048]{1,0:T(8,128)(2,1)} %collective-permute-done.14, bf16[512,2048]{1,0:T(8,128)(2,1)} %multiply_convert_fusion.2), kind=kOutput, calls=%fused_computation.137 | convolution fusion | flops 17213423616 | bytes 33554432 | tf_op jit(solution)/shard_map/dot_general | solution.py:30
  601.9 27.6 %fusion.48 = f32[2048,2048]{1,0:T(8,128)} fusion(bf16[2048,2048]{1,0:T(8,128)(2,1)} %all-gather.10.cloned.1.call-done, bf16[512,2048]{1,0:T(8,128)(2,1)} %collective-permute-done.16, bf16[512,2048]{1,0:T(8,128)(2,1)} %collective-permute-done.15, bf16[512,2048]{1,0:T(8,128)(2,1)} %collective-permute-done.14, bf16[512,2048]{1,0:T(8,128)(2,1)} %multiply_convert_fusion.2), kind=kOutput, calls=%fused_computation.138 | convolution fusion | flops 17213423616 | bytes 33554432 | tf_op jit(solution)/shard_map/dot_general | solution.py:30
  629.5 35.0 %fusion.2 = (bf16[2048,2048]{1,0:T(8,128)(2,1)}, bf16[2048,2048]{1,0:T(8,128)(2,1)}, bf16[2048,2048]{1,0:T(8,128)(2,1)}) fusion(f32[2048,2048]{1,0:T(8,128)} %fusion.48, f32[2048,2048]{1,0:T(8,128)} %fusion.47, bf16[2048,2048]{1,0:T(8,128)(2,1)} %constant_dynamic-update-slice_fusion.3, bf16[2048,2048]{1,0:T(8,128)(2,1)} %all-gather.14.cloned.1.call-done), kind=kOutput, calls=%fused_computation.3 | convolution fusion | flops 17246978048 | bytes 75497472 | tf_op jit(solution)/shard_map/dot_general | solution.py:30
  678.9 13.7 fusion.11
  692.6 13.8 add_convert_fusion
  708.0 14.5 %fusion.15 = f32[1024,2048]{1,0:T(8,128)} fusion(bf16[2048,2048]{1,0:T(8,128)(2,1)} %all-gather.12.cloned.1.call-done, bf16[2048,2048]{1,0:T(8,128)(2,1)} %get-tuple-element.40), kind=kOutput, calls=%fused_computation.34 | convolution fusion | flops 8589934592 | bytes 20971520 | tf_op jit(solution)/shard_map/dot_general | solution.py:30
  722.5 14.1 add_convert_fusion.1
  761.7 26.1 %collective-permute-done.36 = bf16[512,2048]{1,0:T(8,128)(2,1)S(1)} collective-permute-done((bf16[512,2048]{1,0:T(8,128)(2,1)S(1)}, bf16[512,2048]{1,0:T(8,128)(2,1)S(1)}, u32[]{:S(2)}, u32[]{:S(2)}) %collective-permute-start.36) | collective-permute-done | bytes 2097184 | tf_op jit(solution)/shard_map/ppermute | solution.py:201
  789.1 43.8 %collective-permute-done.28 = bf16[512,2048]{1,0:T(8,128)(2,1)} collective-permute-done((bf16[512,2048]{1,0:T(8,128)(2,1)S(1)}, bf16[512,2048]{1,0:T(8,128)(2,1)}, u32[]{:S(2)}, u32[]{:S(2)}) %collective-permute-start.28) | collective-permute-done | bytes 2097184 | tf_op jit(solution)/shard_map/ppermute | solution.py:201
  843.8 44.9 %collective-permute-done.38 = bf16[512,2048]{1,0:T(8,128)(2,1)S(1)} collective-permute-done((bf16[512,2048]{1,0:T(8,128)(2,1)S(1)}, bf16[512,2048]{1,0:T(8,128)(2,1)S(1)}, u32[]{:S(2)}, u32[]{:S(2)}) %collective-permute-start.38) | collective-permute-done | bytes 2097184 | tf_op jit(solution)/shard_map/ppermute | solution.py:201
  901.7 23.8 %convolution_convert_fusion = bf16[2048,2048]{1,0:T(8,128)(2,1)} fusion(bf16[2048,2048]{1,0:T(8,128)(2,1)} %constant_dynamic-update-slice_fusion.3, bf16[2048,2048]{1,0:T(8,128)(2,1)} %get-tuple-element.41), kind=kOutput, calls=%fused_computation.14 | convolution fusion | flops 17184063488 | bytes 25165824 | tf_op jit(solution)/shard_map/dot_general | solution.py:30
  925.5 24.2 %convolution_convert_fusion.2 = bf16[2048,2048]{1,0:T(8,128)(2,1)} fusion(bf16[2048,2048]{1,0:T(8,128)(2,1)} %get-tuple-element.39, bf16[512,2048]{1,0:T(8,128)(2,1)} %collective-permute-done.16, bf16[512,2048]{1,0:T(8,128)(2,1)} %collective-permute-done.15, bf16[512,2048]{1,0:T(8,128)(2,1)} %collective-permute-done.14, ...), kind=kOutput, calls=%fused_computation.16 | convolution fusion | flops 17217617920 | bytes 25165824 | tf_op jit(solution)/shard_map/dot_general | solution.py:30
  949.8 24.2 %convolution_convert_fusion.1 = bf16[2048,2048]{1,0:T(8,128)(2,1)} fusion(bf16[2048,2048]{1,0:T(8,128)(2,1)} %get-tuple-element.40, bf16[512,2048]{1,0:T(8,128)(2,1)} %collective-permute-done.16, bf16[512,2048]{1,0:T(8,128)(2,1)} %collective-permute-done.15, bf16[512,2048]{1,0:T(8,128)(2,1)} %collective-permute-done.14, ...), kind=kOutput, calls=%fused_computation.15 | convolution fusion | flops 17217617920 | bytes 25165824 | tf_op jit(solution)/shard_map/dot_general | solution.py:30
  986.9 52.0 %shard_map.179 = (bf16[2048,512]{1,0:T(8,128)(2,1)S(1)}, bf16[2048,512]{1,0:T(8,128)(2,1)}, bf16[2048,512]{1,0:T(8,128)(2,1)}) custom-call(s32[4]{0:T(128)S(1)} %slice.126.first, s32[1]{0:T(128)} %bitcast.3.total, s32[16]{0:T(128)S(1)} %get-tuple-element.21.pairs, bf16[2048,512]{1,0:T(8,128)(2,1)} %get-tuple-element.22.q_ref, ...), custom_call_target="tpu_custom_call" | custom-call | flops 10737418240 | bytes 20971520 | tf_op jit(solution)/shard_map/pallas_call | solution.py:181
  1043.9 18.2 %convolution_convert_fusion.3 = bf16[2048,1536]{1,0:T(8,128)(2,1)} fusion(bf16[2048,1536]{1,0:T(8,128)(2,1)S(1)} %constant_dynamic-update-slice_fusion.7, bf16[512,2048]{1,0:T(8,128)(2,1)} %collective-permute-done.4, bf16[512,2048]{1,0:T(8,128)(2,1)} %collective-permute-done.3, bf16[512,2048]{1,0:T(8,128)(2,1)} %collective-permute-done.2, ...), kind=kOutput, calls=%fused_computation.17 | convolution fusion | flops 12921602048 | bytes 20971520 | tf_op jit(solution)/shard_map/dot_general | solution.py:30
  1086.8 66.4 %collective-permute-done.42 = bf16[512,2048]{1,0:T(8,128)(2,1)S(1)} collective-permute-done((bf16[512,2048]{1,0:T(8,128)(2,1)S(1)}, bf16[512,2048]{1,0:T(8,128)(2,1)S(1)}, u32[]{:S(2)}, u32[]{:S(2)}) %collective-permute-start.42) | collective-permute-done | bytes 2097184 | tf_op jit(solution)/shard_map/ppermute | solution.py:201
  1171.7 47.3 %collective-permute-done.49 = bf16[256,512]{1,0:T(8,128)(2,1)S(1)} collective-permute-done((bf16[256,512]{1,0:T(8,128)(2,1)S(1)}, bf16[256,512]{1,0:T(8,128)(2,1)S(1)}, u32[]{:S(2)}, u32[]{:S(2)}) %collective-permute-start.49) | collective-permute-done | bytes 262176 | tf_op jit(solution)/shard_map/ppermute | solution.py:249
  1252.2 38.0 %collective-permute-done.58 = bf16[256,2048]{1,0:T(8,128)(2,1)S(1)} collective-permute-done((bf16[256,2048]{1,0:T(8,128)(2,1)}, bf16[256,2048]{1,0:T(8,128)(2,1)S(1)}, u32[]{:S(2)}, u32[]{:S(2)}) %collective-permute-start.58) | collective-permute-done | bytes 1048608 | tf_op jit(solution)/shard_map/ppermute | solution.py:249
  1338.5 55.7 %collective-permute-done.46 = bf16[256,1536]{1,0:T(8,128)(2,1)S(1)} collective-permute-done((bf16[256,1536]{1,0:T(8,128)(2,1)S(1)}, bf16[256,1536]{1,0:T(8,128)(2,1)S(1)}, u32[]{:S(2)}, u32[]{:S(2)}) %collective-permute-start.46) | collective-permute-done | bytes 786464 | tf_op jit(solution)/shard_map/ppermute | solution.py:249
  (337 shorter events, 332.2 us)
Async XLA Ops:
  7.2 306.2 %all-gather.6.cloned.1.call-start = ((), (), s32[]{:S(2)}) async-start(), calls=%async_computation.5 | async-start | bytes 7864320 | tf_op jit(solution)/shard_map/all_gather | solution.py:241
  50.7 326.4 %all-gather.8.cloned.1.call-start = ((), (), s32[]{:S(2)}) async-start(), calls=%async_computation.6 | async-start | bytes 2621440 | tf_op jit(solution)/shard_map/all_gather | solution.py:241
  69.4 504.8 %all-gather.12.cloned.1.call-start = ((), (), s32[]{:S(2)}) async-start(), calls=%async_computation.8 | async-start | bytes 10485760 | tf_op jit(solution)/shard_map/all_gather | solution.py:241
  70.9 71.7 %collective-permute-start.22 = (bf16[256,2048]{1,0:T(8,128)(2,1)S(1)}, bf16[256,2048]{1,0:T(8,128)(2,1)S(1)}, u32[]{:S(2)}, u32[]{:S(2)}) collective-permute-start(bf16[256,2048]{1,0:T(8,128)(2,1)S(1)} %copy-done.22), channel_id=1, source_target_pairs={{4,2},{6,4},{5,3},{7,5},{12,10},{14,12},{13,11},{15,13},{20,18},{2... | collective-permute-start | bytes 3145736 | tf_op jit(solution)/shard_map/ppermute | solution.py:237
  72.8 69.9 %collective-permute-start.21 = (bf16[256,2048]{1,0:T(8,128)(2,1)S(1)}, bf16[256,2048]{1,0:T(8,128)(2,1)S(1)}, u32[]{:S(2)}, u32[]{:S(2)}) collective-permute-start(bf16[256,2048]{1,0:T(8,128)(2,1)S(1)} %copy-done.22), channel_id=1, source_target_pairs={{0,2},{2,4},{1,3},{3,5},{8,10},{10,12},{9,11},{11,13},{16,18},{18,... | collective-permute-start | bytes 3145736 | tf_op jit(solution)/shard_map/ppermute | solution.py:236
  74.1 68.6 %collective-permute-start.23 = (bf16[256,2048]{1,0:T(8,128)(2,1)S(1)}, bf16[256,2048]{1,0:T(8,128)(2,1)S(1)}, u32[]{:S(2)}, u32[]{:S(2)}) collective-permute-start(bf16[256,2048]{1,0:T(8,128)(2,1)S(1)} %copy-done.21), channel_id=1, source_target_pairs={{4,0},{2,6},{5,1},{3,7},{12,8},{10,14},{13,9},{11,15},{20,16},{18,... | collective-permute-start | bytes 3145736 | tf_op jit(solution)/shard_map/ppermute | solution.py:238
  76.3 88.7 %collective-permute-start.25 = (bf16[256,2048]{1,0:T(8,128)(2,1)S(1)}, bf16[256,2048]{1,0:T(8,128)(2,1)S(1)}, u32[]{:S(2)}, u32[]{:S(2)}) collective-permute-start(bf16[256,2048]{1,0:T(8,128)(2,1)S(1)} %copy-done.21), channel_id=1, source_target_pairs={{4,2},{6,4},{5,3},{7,5},{12,10},{14,12},{13,11},{15,13},{20,18},{2... | collective-permute-start | bytes 3145736 | tf_op jit(solution)/shard_map/ppermute | solution.py:237
  80.7 84.4 %collective-permute-start.24 = (bf16[256,2048]{1,0:T(8,128)(2,1)S(1)}, bf16[256,2048]{1,0:T(8,128)(2,1)S(1)}, u32[]{:S(2)}, u32[]{:S(2)}) collective-permute-start(bf16[256,2048]{1,0:T(8,128)(2,1)S(1)} %copy-done.21), channel_id=1, source_target_pairs={{0,2},{2,4},{1,3},{3,5},{8,10},{10,12},{9,11},{11,13},{16,18},{18,... | collective-permute-start | bytes 3145736 | tf_op jit(solution)/shard_map/ppermute | solution.py:236
  168.1 433.8 %all-gather.10.cloned.1.call-start = ((), (), s32[]{:S(2)}) async-start(), calls=%async_computation.7 | async-start | bytes 10485760 | tf_op jit(solution)/shard_map/all_gather | solution.py:241
  168.2 96.1 %collective-permute-start = (bf16[512,2048]{1,0:T(8,128)(2,1)}, bf16[512,2048]{1,0:T(8,128)(2,1)S(1)}, u32[]{:S(2)}, u32[]{:S(2)}) collective-permute-start(bf16[512,2048]{1,0:T(8,128)(2,1)} %param.11), channel_id=1, source_target_pairs={{0,0},{2,4},{4,2},{6,6},{1,1},{3,5},{5,3},{7,7},{8,8},{10,12},{12,... | collective-permute-start | bytes 6291464 | tf_op jit(solution)/shard_map/ppermute | solution.py:212
  171.5 70.0 %collective-permute-start.19 = (bf16[256,2048]{1,0:T(8,128)(2,1)S(1)}, bf16[256,2048]{1,0:T(8,128)(2,1)S(1)}, u32[]{:S(2)}, u32[]{:S(2)}) collective-permute-start(bf16[256,2048]{1,0:T(8,128)(2,1)S(1)} %copy-done.23), channel_id=1, source_target_pairs={{4,2},{6,4},{5,3},{7,5},{12,10},{14,12},{13,11},{15,13},{20,18},{2... | collective-permute-start | bytes 3145736 | tf_op jit(solution)/shard_map/ppermute | solution.py:237
  176.0 87.8 %collective-permute-start.18 = (bf16[256,2048]{1,0:T(8,128)(2,1)S(1)}, bf16[256,2048]{1,0:T(8,128)(2,1)S(1)}, u32[]{:S(2)}, u32[]{:S(2)}) collective-permute-start(bf16[256,2048]{1,0:T(8,128)(2,1)S(1)} %copy-done.23), channel_id=1, source_target_pairs={{0,2},{2,4},{1,3},{3,5},{8,10},{10,12},{9,11},{11,13},{16,18},{18,... | collective-permute-start | bytes 3145736 | tf_op jit(solution)/shard_map/ppermute | solution.py:236
  269.0 360.5 %all-gather.14.cloned.1.call-start = ((), (), s32[]{:S(2)}) async-start(), calls=%async_computation.9 | async-start | bytes 10485760 | tf_op jit(solution)/shard_map/all_gather | solution.py:241
  406.1 69.9 %collective-permute-start.13 = (bf16[512,2048]{1,0:T(8,128)(2,1)}, bf16[512,2048]{1,0:T(8,128)(2,1)}, u32[]{:S(2)}, u32[]{:S(2)}) collective-permute-start(bf16[512,2048]{1,0:T(8,128)(2,1)} %add_convert_fusion.7), channel_id=1, source_target_pairs={{0,1},{1,0},{2,3},{3,2},{4,5},{5,4},{6,7},{7,6},{8,9},{9,8},{10,11... | collective-permute-start | bytes 6291464 | tf_op jit(solution)/shard_map/ppermute | solution.py:201
  407.6 755.0 %reduce-scatter.8.cloned.1.call-start = ((), (), s32[]{:S(2)}) async-start(), calls=%async_computation.11 | async-start | bytes 2621440 | tf_op jit(solution)/shard_map/reduce_scatter | solution.py:244
  432.7 88.1 %collective-permute-start.32 = (bf16[512,2048]{1,0:T(8,128)(2,1)}, bf16[512,2048]{1,0:T(8,128)(2,1)S(1)}, u32[]{:S(2)}, u32[]{:S(2)}) collective-permute-start(bf16[512,2048]{1,0:T(8,128)(2,1)} %collective-permute-done.30), channel_id=1, source_target_pairs={{0,1},{1,0},{2,3},{3,2},{4,5},{5,4},{6,7},{7,6},{8,9},{9,8},{10,11... | collective-permute-start | bytes 6291464 | tf_op jit(solution)/shard_map/ppermute | solution.py:201
  483.9 81.9 %collective-permute-start.15 = (bf16[512,2048]{1,0:T(8,128)(2,1)}, bf16[512,2048]{1,0:T(8,128)(2,1)}, u32[]{:S(2)}, u32[]{:S(2)}) collective-permute-start(bf16[512,2048]{1,0:T(8,128)(2,1)} %multiply_convert_fusion.2), channel_id=1, source_target_pairs={{0,1},{1,0},{2,3},{3,2},{4,5},{5,4},{6,7},{7,6},{8,9},{9,8},{10,11... | collective-permute-start | bytes 6291464 | tf_op jit(solution)/shard_map/ppermute | solution.py:201
  483.9 85.7 %collective-permute-start.31 = (bf16[512,2048]{1,0:T(8,128)(2,1)}, bf16[512,2048]{1,0:T(8,128)(2,1)S(1)}, u32[]{:S(2)}, u32[]{:S(2)}) collective-permute-start(bf16[512,2048]{1,0:T(8,128)(2,1)} %collective-permute-done.30), channel_id=1, source_target_pairs={{0,4},{4,0},{1,5},{5,1},{2,6},{6,2},{3,7},{7,3},{8,12},{12,8},{9,1... | collective-permute-start | bytes 6291464 | tf_op jit(solution)/shard_map/ppermute | solution.py:201
  678.9 76.9 %collective-permute-start.27 = (bf16[512,2048]{1,0:T(8,128)(2,1)}, bf16[512,2048]{1,0:T(8,128)(2,1)}, u32[]{:S(2)}, u32[]{:S(2)}) collective-permute-start(bf16[512,2048]{1,0:T(8,128)(2,1)} %slice.179), channel_id=1, source_target_pairs={{0,4},{4,0},{1,5},{5,1},{2,6},{6,2},{3,7},{7,3},{8,12},{12,8},{9,1... | collective-permute-start | bytes 6291464 | tf_op jit(solution)/shard_map/ppermute | solution.py:201
  760.2 72.7 %collective-permute-start.28 = (bf16[512,2048]{1,0:T(8,128)(2,1)S(1)}, bf16[512,2048]{1,0:T(8,128)(2,1)}, u32[]{:S(2)}, u32[]{:S(2)}) collective-permute-start(bf16[512,2048]{1,0:T(8,128)(2,1)S(1)} %add_convert_fusion.6), channel_id=1, source_target_pairs={{0,1},{1,0},{2,3},{3,2},{4,5},{5,4},{6,7},{7,6},{8,9},{9,8},{10,11... | collective-permute-start | bytes 6291464 | tf_op jit(solution)/shard_map/ppermute | solution.py:201
  901.7 321.8 %reduce-scatter.14.cloned.1.call-start = ((), (), s32[]{:S(2)}) async-start(), calls=%async_computation.14 | async-start | bytes 10485760 | tf_op jit(solution)/shard_map/reduce_scatter | solution.py:244
  925.5 310.2 %reduce-scatter.10.cloned.1.call-start = ((), (), s32[]{:S(2)}) async-start(), calls=%async_computation.12 | async-start | bytes 10485760 | tf_op jit(solution)/shard_map/reduce_scatter | solution.py:244
  949.7 295.0 %reduce-scatter.12.cloned.1.call-start = ((), (), s32[]{:S(2)}) async-start(), calls=%async_computation.13 | async-start | bytes 10485760 | tf_op jit(solution)/shard_map/reduce_scatter | solution.py:244
  974.1 336.5 %reduce-scatter.6.cloned.1.call-start = ((), (), s32[]{:S(2)}) async-start(), calls=%async_computation.10 | async-start | bytes 7864320 | tf_op jit(solution)/shard_map/reduce_scatter | solution.py:244
  1083.4 69.9 %collective-permute-start.42 = (bf16[512,2048]{1,0:T(8,128)(2,1)S(1)}, bf16[512,2048]{1,0:T(8,128)(2,1)S(1)}, u32[]{:S(2)}, u32[]{:S(2)}) collective-permute-start(bf16[512,2048]{1,0:T(8,128)(2,1)S(1)} %add_convert_fusion.3), channel_id=1, source_target_pairs={{0,1},{1,0},{2,3},{3,2},{4,5},{5,4},{6,7},{7,6},{8,9},{9,8},{10,11... | collective-permute-start | bytes 6291464 | tf_op jit(solution)/shard_map/ppermute | solution.py:201
  1083.4 88.2 %collective-permute-start.29 = (bf16[512,2048]{1,0:T(8,128)(2,1)}, bf16[512,2048]{1,0:T(8,128)(2,1)}, u32[]{:S(2)}, u32[]{:S(2)}) collective-permute-start(bf16[512,2048]{1,0:T(8,128)(2,1)} %get-tuple-element.42), channel_id=1, source_target_pairs={{0,0},{2,4},{4,2},{6,6},{1,1},{3,5},{5,3},{7,7},{8,8},{10,12},{12,... | collective-permute-start | bytes 6291464 | tf_op jit(solution)/shard_map/ppermute | solution.py:212
  1160.7 60.3 %collective-permute-start.43 = (bf16[512,2048]{1,0:T(8,128)(2,1)}, bf16[512,2048]{1,0:T(8,128)(2,1)S(1)}, u32[]{:S(2)}, u32[]{:S(2)}) collective-permute-start(bf16[512,2048]{1,0:T(8,128)(2,1)} %add_convert_fusion.2), channel_id=1, source_target_pairs={{0,0},{2,4},{4,2},{6,6},{1,1},{3,5},{5,3},{7,7},{8,8},{10,12},{12,... | collective-permute-start | bytes 6291464 | tf_op jit(solution)/shard_map/ppermute | solution.py:212
  1228.1 62.2 %collective-permute-start.58 = (bf16[256,2048]{1,0:T(8,128)(2,1)}, bf16[256,2048]{1,0:T(8,128)(2,1)S(1)}, u32[]{:S(2)}, u32[]{:S(2)}) collective-permute-start(bf16[256,2048]{1,0:T(8,128)(2,1)} %get-tuple-element.44), channel_id=1, source_target_pairs={{2,4},{4,6},{3,5},{5,7},{10,12},{12,14},{11,13},{13,15},{18,20},{2... | collective-permute-start | bytes 3145736 | tf_op jit(solution)/shard_map/ppermute | solution.py:249
  1240.3 72.5 %collective-permute-start.52 = (bf16[256,2048]{1,0:T(8,128)(2,1)}, bf16[256,2048]{1,0:T(8,128)(2,1)}, u32[]{:S(2)}, u32[]{:S(2)}) collective-permute-start(bf16[256,2048]{1,0:T(8,128)(2,1)} %get-tuple-element.50), channel_id=1, source_target_pairs={{2,4},{4,6},{3,5},{5,7},{10,12},{12,14},{11,13},{13,15},{18,20},{2... | collective-permute-start | bytes 3145736 | tf_op jit(solution)/shard_map/ppermute | solution.py:249
  1248.1 66.0 %collective-permute-start.51 = (bf16[256,2048]{1,0:T(8,128)(2,1)}, bf16[256,2048]{1,0:T(8,128)(2,1)}, u32[]{:S(2)}, u32[]{:S(2)}) collective-permute-start(bf16[256,2048]{1,0:T(8,128)(2,1)} %get-tuple-element.51), channel_id=1, source_target_pairs={{2,0},{4,2},{3,1},{5,3},{10,8},{12,10},{11,9},{13,11},{18,16},{20,... | collective-permute-start | bytes 3145736 | tf_op jit(solution)/shard_map/ppermute | solution.py:248
  1314.1 80.1 %collective-permute-start.46 = (bf16[256,1536]{1,0:T(8,128)(2,1)S(1)}, bf16[256,1536]{1,0:T(8,128)(2,1)S(1)}, u32[]{:S(2)}, u32[]{:S(2)}) collective-permute-start(bf16[256,1536]{1,0:T(8,128)(2,1)S(1)} %get-tuple-element.62), channel_id=1, source_target_pairs={{2,4},{4,6},{3,5},{5,7},{10,12},{12,14},{11,13},{13,15},{18,20},{2... | collective-permute-start | bytes 2359304 | tf_op jit(solution)/shard_map/ppermute | solution.py:249
  1317.7 76.5 %collective-permute-start.45 = (bf16[256,1536]{1,0:T(8,128)(2,1)S(1)}, bf16[256,1536]{1,0:T(8,128)(2,1)S(1)}, u32[]{:S(2)}, u32[]{:S(2)}) collective-permute-start(bf16[256,1536]{1,0:T(8,128)(2,1)S(1)} %get-tuple-element.63), channel_id=1, source_target_pairs={{2,0},{4,2},{3,1},{5,3},{10,8},{12,10},{11,9},{13,11},{18,16},{20,... | collective-permute-start | bytes 2359304 | tf_op jit(solution)/shard_map/ppermute | solution.py:248
  (90 other events, 2258.6 us)
Sparse Core Ops, SparseCore 0:
  50.8 72.5 all-gather.5
  125.8 35.3 all-gather.7
  168.3 87.9 all-gather.11
  269.1 87.3 all-gather.9
  407.8 87.2 all-gather.13
  901.8 34.4 reduce-scatter.7
  939.6 86.3 reduce-scatter.13
  1029.1 86.3 reduce-scatter.9
  1118.9 86.3 reduce-scatter.11
  1208.2 70.2 reduce-scatter.5

commit v2 on v1

v2 whole, which is shorter than its diff:
```python
import functools
import jax
import jax.numpy as jnp
import numpy as np
from jax import lax
from jax.experimental import pallas as pl
from jax.experimental.pallas import tpu as pltpu
from jax.sharding import Mesh, PartitionSpec as P

HD = 128
SCALE = HD ** (-0.5)
LOG2E = 1.4426950408889634
NEG = -1e30
eps = 1e-05
NT = (((1,), (1,)), ((), ()))
TN = (((0,), (0,)), ((), ()))


def layer_norm(tok_rows):
    average = jnp.mean(tok_rows, axis=-1, keepdims=True)
    centred = tok_rows - average
    variance = jnp.mean(centred * centred, axis=-1, keepdims=True)
    return centred * lax.rsqrt(variance + eps)


def swiglu(gate, up_lin):
    return jax.nn.silu(gate) * up_lin


def dot(left, right, dims=(((1,), (0,)), ((), ()))):
    return lax.dot_general(left, right, dims, preferred_element_type=jnp.float32)


def low(value):
    return value.astype(jnp.bfloat16)

def visit_lists(pos, end, blk):
    first = pos[::blk]
    most = jnp.max(end.reshape(-1, blk), axis=1)
    met = (first[None, :] <= first[:, None]) & (most[None, :] >= first[:, None])
    count = jnp.sum(met, axis=1, dtype=jnp.int32)
    keys = jnp.argsort(~met, axis=1, stable=True).astype(jnp.int32)
    total = jnp.sum(count, dtype=jnp.int32)
    pairs = jnp.argsort(~met.reshape(-1), stable=True).astype(jnp.int32)
    return first, count, keys.reshape(-1), total.reshape(1), pairs


def turned(value, cos_ref, sin_ref, sign):
    return value * cos_ref[...] + sign * pltpu.roll(value, HD // 2, 1) * sin_ref[...]


def allowed_of(first_q, first_k, end_row):
    blk = end_row.shape[1]
    t = first_q + lax.broadcasted_iota(jnp.int32, (blk, 1), 0)
    u = first_k + lax.broadcasted_iota(jnp.int32, (1, blk), 1)
    return (u <= t) & (t <= end_row)


def backward_kernel(
    hpg, n_after, first, total, pairs, q_ref, k_ref, v_ref, grad_ref, att_ref, lse_ref,
    cos_ref, sin_ref, end_ref, *refs
):
    dq_ref, dk_ref, dv_ref, dq_acc, dk_acc, dv_acc, delta, lses = refs[n_after:]
    n_k, blk = end_ref.shape
    dq_acc[...] = jnp.zeros_like(dq_acc)
    dk_acc[...] = jnp.zeros_like(dk_acc)
    dv_acc[...] = jnp.zeros_like(dv_acc)
    lanes = lax.broadcasted_iota(jnp.int32, lse_ref.shape, 1)
    for h in range(hpg):
        cols = slice(h * HD, (h + 1) * HD)
        mine = jnp.where(lanes == pl.program_id(0) * hpg + h, lse_ref[...], 0.0)
        lses[:, cols] = jnp.broadcast_to(jnp.sum(mine, axis=1, keepdims=True), mine.shape)
        prod = grad_ref[:, cols].astype(jnp.float32) * att_ref[:, cols].astype(jnp.float32)
        delta[:, cols] = jnp.broadcast_to(jnp.sum(prod, axis=1, keepdims=True), prod.shape)

    def step(n, carry):
        code = pairs[n]
        i, j = code // n_k, code % n_k
        rows = pl.ds(pl.multiple_of(i * blk, blk), blk)
        spot = pl.ds(pl.multiple_of(j * blk, blk), blk)
        allowed = allowed_of(first[i], first[j], end_ref[pl.ds(j, 1), :])
        for h in range(hpg):
            cols = slice(h * HD, (h + 1) * HD)
            q, k, v, grad = q_ref[rows, cols], k_ref[spot, cols], v_ref[spot, cols], grad_ref[rows, cols]
            scores = dot(q, k, NT) * (SCALE * LOG2E)
            lse = lses[rows, h * HD : h * HD + 1]
            probs = jnp.where(allowed, jnp.exp2(scores - lse), 0.0)
            d_probs = dot(grad, v, NT)
            d_scores = (probs * (d_probs - delta[rows, h * HD : h * HD + 1])).astype(jnp.bfloat16)
            dv_acc[spot, cols] += dot(probs.astype(jnp.bfloat16), grad, TN)
            dk_acc[spot, cols] += dot(d_scores, q, TN)
            dq_acc[rows, cols] += dot(d_scores, k)
        return carry

    lax.fori_loop(0, total[0], step, 0)
    for h in range(hpg):
        cols = slice(h * HD, (h + 1) * HD)
        dq_ref[:, cols] = turned(dq_acc[:, cols] * SCALE, cos_ref, sin_ref, -1.0).astype(jnp.bfloat16)
        dk_ref[:, cols] = turned(dk_acc[:, cols] * SCALE, cos_ref, sin_ref, -1.0).astype(jnp.bfloat16)
        dv_ref[:, cols] = dv_acc[:, cols].astype(jnp.bfloat16)


def attend_back(q, k, v, grad, att, lse, cos, sin, end_rows, lists, heads, hpg, after=()):
    length = q.shape[0]
    first, _, _, total, pairs = lists
    groups = heads // hpg
    wide = hpg * HD
    col = pl.BlockSpec((length, wide), lambda g, *_: (0, g))
    whole = lambda a: pl.BlockSpec(a.shape, lambda g, *_: (0, 0))
    low = jax.ShapeDtypeStruct((length, heads * HD), jnp.bfloat16)
    return pl.pallas_call(
        functools.partial(backward_kernel, hpg, len(after)),
        grid_spec=pltpu.PrefetchScalarGridSpec(
            num_scalar_prefetch=3,
            grid=(groups,),
            in_specs=[col] * 5
            + [whole(lse), whole(cos), whole(sin), whole(end_rows)]
            + [pl.BlockSpec(memory_space=pl.ANY)] * len(after),
            out_specs=[col] * 3,
            scratch_shapes=[pltpu.VMEM((length, wide), jnp.float32)] * 5,
        ),
        out_shape=[low] * 3,
        compiler_params=pltpu.CompilerParams(vmem_limit_bytes=48 * 2**20),
        cost_estimate=pl.CostEstimate(
            flops=5 * length * length * HD * heads,
            bytes_accessed=length * heads * HD * 20,
            transcendentals=heads * length * length // 2,
        ),
    )(first, total, pairs, q, k, v, grad, att, lse, cos, sin, end_rows, *after)


MESH = pl.DeviceIdType.MESH
CHUNKS = 4
SEMS = 224
MATS = ("qkv", "out", "gate", "up", "down")


def flipped(bit, other):
    return bit + other - 2 * bit * other


class Links:
    def __init__(self, places, send, recv):
        self.rest, self.core, self.high, self.lower = places
        self.c, self.h = lax.axis_index(self.core), lax.axis_index(self.high)
        self.r = [lax.axis_index(axis) for axis in self.rest]
        self.low = [lax.axis_index(axis) for axis in self.lower]
        self.same = self.c == self.h
        self.n_parts = 2 ** len(self.lower)
        self.send, self.recv, self.used, self.unsent = send, recv, 0, []
        self.across = {self.core: 1 - self.c}

    def beside(self, k):
        return {self.lower[k]: 1 - self.low[k]}

    def over(self, k):
        return {self.rest[k]: 1 - self.r[k]}

    def group(self, mask):
        total = 0
        for k, bit in enumerate(self.r):
            total = total * 2 + (1 - bit if mask >> k & 1 else bit)
        return total

    def swap_piece(self, number):
        other, part = number % 2, number // 2
        return flipped(self.c, other) * self.n_parts + self.turn(part)

    def piece(self, quarter):
        other, part = flipped(self.c, quarter // self.n_parts), self.turn(quarter % self.n_parts)
        return part * 2 + other

    def turn(self, part):
        total = 0
        for k, bit in enumerate(self.low):
            digit = part // 2 ** (len(self.low) - 1 - k) % 2
            total = total * 2 + flipped(bit, digit)
        return total

    def greet(self):
        barrier = pltpu.get_barrier_semaphore()
        partners = [
            self.across,
            {self.high: 1 - self.h},
            {self.core: 1 - self.c, self.high: 1 - self.h},
        ]
        partners += [self.beside(k) for k in range(len(self.lower))]
        partners += [self.over(k) for k in range(len(self.rest))]
        for partner in partners:
            pl.semaphore_signal(barrier, inc=1, device_id=partner, device_id_type=MESH)
        pl.semaphore_wait(barrier, len(partners))

    def take(self, count=1):
        self.used += count
        return self.used - count

    def copy(self, src, dst, partner, spot=None, recv=None):
        spot = self.take() if spot is None else spot
        made = pltpu.make_async_remote_copy(
            src_ref=src, dst_ref=dst, send_sem=self.send.at[spot],
            recv_sem=self.recv.at[spot if recv is None else recv],
            device_id=partner, device_id_type=MESH,
        )
        return made

    def push(self, src, dst, partner):
        made = self.copy(src, dst, partner)
        made.start()
        self.unsent.append(made)
        return made


class Weight:
    def __init__(self, links, shard, full):
        self.links, self.shard, self.full = links, shard, full
        self.rows = shard.shape[0]
        self.arrive = links.take(2)
        self.near, self.far = links.take(), links.take()
        self.stages = []
        n = len(links.rest)
        for step in range(n):
            stage = []
            for half in range(2):
                order = list(range(n)) if half == 0 else list(reversed(range(n)))
                have = [0]
                for k in order[:step]:
                    have = have + [mask | 1 << k for mask in have]
                stage += [(half, mask, order[step], links.take()) for mask in have]
            self.stages.append(stage)

    def slot(self, mask, core):
        start = (self.links.group(mask) * 2 + core) * self.rows
        return self.full.at[pl.ds(pl.multiple_of(start, self.rows), self.rows)]

    def near_copy(self):
        links = self.links
        return links.copy(
            self.shard, self.slot(0, links.c), links.across, self.near, self.arrive + links.c
        )

    def far_copy(self):
        links = self.links
        return links.copy(
            self.shard, self.slot(0, links.c), {links.core: links.h, links.high: 1 - links.h},
            self.far, self.arrive + links.c,
        )

    def send_near(self):
        links = self.links

        @pl.when(links.same)
        def _():
            pltpu.make_async_copy(
                self.shard, self.slot(0, links.c), links.recv.at[self.arrive + links.c]
            ).start()

        @pl.when(~links.same)
        def _():
            self.near_copy().start()

    def send_far(self):
        self.far_copy().start()

    def stage_copies(self, step):
        for half, mask, axis, spot in self.stages[step]:
            block = self.slot(mask, half)
            yield self.links.copy(block, block, self.links.over(axis), spot)

    def event(self, step):
        if step == 0:
            for core in range(2):
                block = self.slot(0, core)
                pltpu.make_async_copy(block, block, self.links.recv.at[self.arrive + core]).wait()
        else:
            for copy in self.stage_copies(step - 1):
                copy.wait_recv()
        if step < len(self.stages):
            for copy in self.stage_copies(step):
                copy.start()

    def finish(self):
        @pl.when(~self.links.same)
        def _():
            self.near_copy().wait_send()

        self.far_copy().wait_send()
        for step in range(len(self.stages)):
            for copy in self.stage_copies(step):
                copy.wait_send()


class Spread:
    def __init__(self, links, full, own):
        self.links, self.full, self.own, self.chunk = links, full, own, own // CHUNKS
        self.moves = {}
        n = len(links.lower)
        for k in range(CHUNKS):
            have = [0]
            for step in range(n):
                value = 2 ** (n - 1 - step)
                for part in have:
                    self.moves[k, part, step] = (part | value, links.take())
                have = have + [part | value for part in have]
            for part in range(links.n_parts):
                self.moves[k, part, None] = (part, links.take())

    def rows(self, part, other, k):
        return pl.ds((part * 2 + other) * self.own + k * self.chunk, self.chunk)

    def made(self, k, part, step, src=None):
        goal, spot = self.moves[k, part, step]
        links = self.links
        partner = links.across if step is None else links.beside(step)
        src = self.full.at[self.rows(part, 0, k)] if src is None else src
        dst = self.full.at[self.rows(goal, 1 if step is None else 0, k)]
        return links.copy(src, dst, partner, spot)

    def first_step(self, part):
        n = len(self.links.lower)
        return [s for s in range(n) if (0, part, s) in self.moves]

    def own_ready(self, k):
        for step in self.first_step(0):
            self.made(k, 0, step).start()
        self.made(k, 0, None).start()

    def pass_on(self, k):
        n = len(self.links.lower)
        for step in range(n):
            value = 2 ** (n - 1 - step)
            for part in range(self.links.n_parts):
                if (k, part, step) in self.moves:
                    self.made(k, part, step).wait_recv()
                    goal = part | value
                    for later in self.first_step(goal):
                        self.made(k, goal, later).start()
                    self.made(k, goal, None).start()

    def wait_near(self):
        for k in range(CHUNKS):
            self.made(k, 0, None).wait_recv()

    def wait_far(self):
        for k in range(CHUNKS):
            for part in range(1, self.links.n_parts):
                self.made(k, part, None).wait_recv()

    def finish(self):
        for k, part, step in self.moves:
            self.made(k, part, step).wait_send()


def normed(value):
    average = jnp.mean(value, axis=-1, keepdims=True)
    centred = value - average
    variance = jnp.mean(centred * centred, axis=-1, keepdims=True)
    return centred * lax.rsqrt(variance + eps)


def spin(value, cos, sin):
    return value * cos + pltpu.roll(value, HD // 2, 1) * sin


def first_kernel(
    places, x, end_mine, cos_ref, sin_ref, w_qkv, w_out, w_gate, w_up, w_down, cot,
    norm1, qkv_all, out_all, gate_all, up_all, down_all, q_ref, k_ref, v_ref, att_ref, lse_ref, x_own, hidden,
    norm2, cot_own, norm1_v, qkv_v, out_v, end_other, p_mine, p_other, p_come, line, send, recv, local,
):
    links = Links(places, send, recv)
    own = x.shape[0]
    n_parts, n_pieces = links.n_parts, 2 * links.n_parts
    n_low = len(links.lower)
    chunk = own // CHUNKS
    heads = q_ref.shape[1] // HD
    width = heads * HD
    weights = {
        name: Weight(links, shard, full)
        for name, shard, full in zip(
            MATS,
            (w_qkv, w_out, w_gate, w_up, w_down),
            (qkv_v, out_v, gate_all, up_all, down_all),
        )
    }
    n_steps = len(links.rest)
    swap_spots = [links.take() for _ in range(CHUNKS)]
    cot_spot, end_spot = links.take(), links.take()
    trade = {links.core: links.h, links.high: links.c}

    def swap_copy(k):
        rows = pl.ds(k * chunk, chunk)
        return links.copy(x.at[rows], x_own.at[rows], trade, swap_spots[k])

    def swap_local(k):
        rows = pl.ds(k * chunk, chunk)
        return pltpu.make_async_copy(x.at[rows], x_own.at[rows], recv.at[swap_spots[k]])

    def cot_copy():
        return links.copy(cot, cot_own, trade, cot_spot)

    def cot_local():
        return pltpu.make_async_copy(cot, cot_own, recv.at[cot_spot])

    end_copy = links.copy(end_mine, end_other, links.across, end_spot)
    spread1 = Spread(links, norm1_v, own)
    norm2_v = norm1_v
    spread2 = Spread(links, norm2_v, own)
    across_spots = [links.take() for _ in range(n_parts)]
    line_spots = {
        (part, k): links.take() for part in range(1, n_parts) for k in range(CHUNKS)
    }

    links.greet()
    end_copy.start()
    weights["qkv"].send_near()
    weights["qkv"].send_far()

    @pl.when(links.same)
    def _():
        for k in range(CHUNKS):
            swap_local(k).start()

    @pl.when(~links.same)
    def _():
        for k in range(CHUNKS):
            swap_copy(k).start()

    for name in MATS[1:]:
        weights[name].send_near()

    def norm_chunk(k):
        rows = pl.ds(k * chunk, chunk)
        norm1_v[rows, :] = low(normed(x_own[rows, :].astype(jnp.float32)))
        spread1.own_ready(k)

    def run(name, *steps):
        for step in steps:
            weights[name].event(step)

    last = n_steps

    @pl.when(links.same)
    def _():
        for k in range(CHUNKS):
            swap_local(k).wait()
            norm_chunk(k)
        run("qkv", *range(last))
        run("out", *range(last))
        run("qkv", last)
        run("out", last)
        run("gate", 0)

    @pl.when(~links.same)
    def _():
        run("qkv", 0)
        for k in range(CHUNKS):
            swap_copy(k).wait_recv()
            norm_chunk(k)
            if k == 1:
                run("qkv", *range(1, last))
        run("qkv", last)

    weights["out"].send_far()
    end_copy.wait_recv()
    for k in range(CHUNKS):
        spread1.pass_on(k)

    keep = [pltpu.make_async_copy(qkv_v, qkv_all, local.at[0])]
    keep[0].start()

    def project(pieces):
        for section, goal in enumerate((q_ref, k_ref, v_ref)):
            for number in pieces:
                rows = slice(number * own, (number + 1) * own)
                spot = pl.ds(pl.multiple_of(links.swap_piece(number) * own, own), own)

                @pl.loop(0, heads // 2)
                def _(tile, section=section, goal=goal, rows=rows, spot=spot):
                    start = pl.multiple_of(tile * 2 * HD, 2 * HD)
                    made = dot(norm1_v[rows, :], qkv_v[:, pl.ds(section * width + start, 2 * HD)])
                    for k in range(2):
                        value = made[:, k * HD : (k + 1) * HD]
                        if section < 2:
                            value = spin(value, cos_ref[spot, :], sin_ref[spot, :])
                        goal[rows, pl.ds(pl.multiple_of(start + k * HD, HD), HD)] = low(value)

    spread1.wait_near()
    project((0, 1))
    weights["gate"].send_far()

    @pl.when(links.same)
    def _():
        run("gate", *range(1, last))

    @pl.when(~links.same)
    def _():
        run("out", 0)

    spread1.wait_far()
    project(range(2, n_pieces))
    keep.append(pltpu.make_async_copy(norm1_v, norm1, local.at[1]))
    keep[-1].start()
    weights["up"].send_far()

    @pl.when(links.same)
    def _():
        run("gate", last)
        run("up", 0)

    @pl.when(~links.same)
    def _():
        run("out", *range(1, last + 1))

    keep.append(pltpu.make_async_copy(out_v, out_all, local.at[2]))
    keep[-1].start()

    lanes = lax.broadcasted_iota(jnp.int32, (own, HD), 1)
    for head in range(heads):
        cols = slice(head * HD, (head + 1) * HD)

        @pl.loop(0, n_pieces)
        def _(i, head=head, cols=cols):
            rows = pl.ds(pl.multiple_of(i * own, own), own)
            quarter = links.swap_piece(i)

            def step(n, carry):
                top, total, acc = carry
                spot = pl.ds(pl.multiple_of(links.piece(n) * own, own), own)
                end = jnp.where(links.same, end_mine[pl.ds(n, 1), :], end_other[pl.ds(n, 1), :])
                allowed = allowed_of(quarter * own, n * own, end)
                scores = dot(q_ref[rows, cols], k_ref[spot, cols], NT)
                scores = jnp.where(allowed, scores * (SCALE * LOG2E), NEG)
                new_top = jnp.maximum(top, jnp.max(scores, axis=1, keepdims=True))
                grown = jnp.exp2(scores - new_top)
                shrink = jnp.exp2(top - new_top)
                total = total * shrink + jnp.sum(grown, axis=1, keepdims=True)
                return new_top, total, acc * shrink + dot(low(grown), v_ref[spot, cols])

            top, total, acc = lax.fori_loop(
                0, quarter + 1, step,
                (
                    jnp.full((own, 1), NEG, jnp.float32),
                    jnp.zeros((own, 1), jnp.float32),
                    jnp.zeros((own, HD), jnp.float32),
                ),
            )
            att_ref[rows, cols] = low(acc / total)
            lse = jnp.broadcast_to(top + jnp.log2(total), (own, HD))
            lse_ref[rows, :] = lse if head == 0 else jnp.where(lanes == head, lse, lse_ref[rows, :])

        if head == 0:
            weights["down"].send_far()

            @pl.when(links.same)
            def _():
                run("up", *range(1, last))

        if head == heads // 2 - 1:

            @pl.when(~links.same)
            def _():
                run("gate", 0)

        if head == heads // 2:

            @pl.when(links.same)
            def _():
                run("up", last)
                run("down", 0)

            @pl.when(~links.same)
            def _():
                run("gate", *range(1, last))

    @pl.when(links.same)
    def _():
        cot_local().start()
        run("down", *range(1, last))

    @pl.when(~links.same)
    def _():
        cot_copy().start()
        run("gate", last)

    keep.pop(1).wait()
    spread1.finish()

    def across_copy(part):
        return links.copy(p_other.at[part], p_come.at[part], links.across, across_spots[part])

    def line_copy(part, k):
        rows = pl.ds(k * chunk, chunk)
        step = n_low - part.bit_length()
        return links.copy(
            p_mine.at[part, rows], line.at[part - 1, rows], links.beside(step), line_spots[part, k]
        )

    def out_rows(number, goal):
        rows = slice(number * own, (number + 1) * own)
        tile = 512

        @pl.loop(0, out_v.shape[0] // tile)
        def _(n):
            start = pl.multiple_of(n * tile, tile)
            goal[:, pl.ds(start, tile)] = low(
                dot(att_ref[rows, :], out_v[pl.ds(start, tile), :], NT)
            )

    for part in reversed(range(n_parts)):
        out_rows(part * 2 + 1, p_other.at[part])
        across_copy(part).start()
        out_rows(part * 2, p_mine.at[part])
        across_copy(part).wait_recv()
        for k in range(CHUNKS):
            rows = pl.ds(k * chunk, chunk)
            total = p_mine[part, rows, :].astype(jnp.float32) + p_come[part, rows, :].astype(jnp.float32)
            if part == 0:
                hidden[rows, :] = x_own[rows, :].astype(jnp.float32) + total
            else:
                step = part.bit_length() - 1
                for high in range(step + 1, n_low):
                    more = part | 1 << high
                    line_copy(more, k).wait_recv()
                    total = total + line[more - 1, rows, :].astype(jnp.float32)
                p_mine[part, rows, :] = low(total)
                line_copy(part, k).start()

    @pl.when(links.same)
    def _():
        run("down", last)

    @pl.when(~links.same)
    def _():
        run("up", *range(last))

    for k in range(CHUNKS):
        rows = pl.ds(k * chunk, chunk)
        total = hidden[rows, :]
        for step in range(n_low):
            line_copy(1 << step, k).wait_recv()
            total = total + line[(1 << step) - 1, rows, :].astype(jnp.float32)
        hidden[rows, :] = total
        norm2_v[rows, :] = low(normed(total))
        spread2.own_ready(k)

    @pl.when(~links.same)
    def _():
        run("up", last)
        run("down", *range(last))

    for k in range(CHUNKS):
        spread2.pass_on(k)
    spread2.wait_near()
    spread2.wait_far()
    keep.append(pltpu.make_async_copy(norm2_v, norm2, local.at[3]))
    keep[-1].start()

    @pl.when(links.same)
    def _():
        cot_local().wait()

    @pl.when(~links.same)
    def _():
        run("down", last)
        cot_copy().wait()
        for k in range(CHUNKS):
            swap_copy(k).wait_send()

    end_copy.wait_send()
    spread2.finish()
    for weight in weights.values():
        weight.finish()
    for part in range(n_parts):
        across_copy(part).wait_send()
    for part, k in line_spots:
        line_copy(part, k).wait_send()
    for made in keep:
        made.wait()


def first_half(places, x, end_mine, cos, sin, mats, cot):
    own, model = x.shape
    n_parts = 2 ** len(places[3])
    length = 2 * n_parts * own
    groups = 2 ** len(places[0])
    width = mats[1].shape[1]
    shape = lambda *dims: jax.ShapeDtypeStruct(dims, jnp.bfloat16)
    wide = lambda *dims: jax.ShapeDtypeStruct(dims, jnp.float32)
    here, there = pl.BlockSpec(memory_space=pltpu.VMEM), pl.BlockSpec(memory_space=pl.ANY)
    fulls = [shape(2 * groups * mat.shape[0], mat.shape[1]) for mat in mats]
    bf = lambda *dims: pltpu.VMEM(dims, jnp.bfloat16)
    return pl.pallas_call(
        functools.partial(first_kernel, places),
        in_specs=[there, here, here, here] + [there] * 6,
        out_specs=[there] * 6 + [here] * 7 + [there] * 2,
        out_shape=[shape(length, model)]
        + fulls
        + [shape(length, width)] * 4
        + [wide(length, HD), shape(own, model), wide(own, model)]
        + [shape(length, model), shape(own, model)],
        scratch_shapes=[
            bf(length, model),
            bf(*fulls[0].shape),
            bf(*fulls[1].shape),
            pltpu.VMEM(end_mine.shape, jnp.int32),
            bf(n_parts, own, model),
            bf(n_parts, own, model),
            bf(n_parts, own, model),
            bf(max(n_parts - 1, 1), own, model),
            pltpu.SemaphoreType.DMA((SEMS,)),
            pltpu.SemaphoreType.DMA((SEMS,)),
            pltpu.SemaphoreType.DMA((4,)),
        ],
        compiler_params=pltpu.CompilerParams(
            collective_id=0, has_side_effects=True, vmem_limit_bytes=61 * 2**20
        ),
        cost_estimate=pl.CostEstimate(
            flops=8 * length * model * width,
            bytes_accessed=100 * 2**20,
            transcendentals=length * length * 4,
        ),
    )(x, end_mine, cos, sin, *mats, cot)


def hold(value, *after):
    return lax.optimization_barrier((value,) + after)[0]


def turn_tables(length):
    frequency = 10000.0 ** (-np.arange(HD // 2, dtype=np.float32) / np.float32(HD // 2))
    angles = np.arange(length, dtype=np.float32)[:, None] * frequency.astype(np.float32)[None, :]
    cos, sin = np.cos(angles), np.sin(angles)
    return (
        jnp.asarray(np.concatenate([cos, cos], axis=1), jnp.float32),
        jnp.asarray(np.concatenate([-sin, sin], axis=1), jnp.float32),
    )


def flip(value, axis):
    return lax.ppermute(value, axis, [(0, 1), (1, 0)])


def body(places, x, segments, padding, w_query, w_key, w_value, w_out, w_gate, w_up, w_down, cot):
    rest, core, high, lower = places
    pair = (core, high)
    c, h = lax.axis_index(core), lax.axis_index(high)
    same = c == h
    first_core = c == 0

    def swap(value):
        return lax.ppermute(value, pair, [(0, 0), (1, 2), (2, 1), (3, 3)])

    def gather_low(value):
        parts = [value]
        for axis in reversed(lower):
            parts = parts + [flip(part, axis) for part in parts]
        return parts

    def gather(value):
        parts = gather_low(value)
        return jnp.concatenate([piece for part in parts for piece in (part, flip(part, core))])

    def scatter(product, n_parts, after=None):
        far = []
        for part in reversed(range(n_parts)):
            mine, other = product(part)
            far.insert(0, (mine, flip(other, core)))
        sums = [mine.astype(jnp.float32) + other.astype(jnp.float32) for mine, other in far]
        for axis in lower:
            half = len(sums) // 2
            come = [flip(low(sums[half + k]), axis) for k in range(half)]
            if after is not None and axis == lower[-1]:
                come = [hold(part, *after) for part in come]
            sums = [sums[k] + come[k].astype(jnp.float32) for k in range(half)]
        return sums[0]

    def scatter_weight(partial):
        both = lax.psum_scatter(partial, rest, scatter_dimension=0, tiled=True)
        rows = both.shape[0] // 2
        s0, s1 = both[:rows], both[rows:]
        near = lax.ppermute(jnp.where(first_core, s1, s0), pair, [(0, 2), (3, 1)])
        from0 = lax.ppermute(s0, pair, [(1, 0), (2, 1)])
        from1 = lax.ppermute(s1, pair, [(1, 2), (2, 3)])
        kept = jnp.where(same, jnp.where(first_core, s0, s1), near)
        far = jnp.where(first_core, from0, from1)
        return kept.astype(jnp.float32) + far.astype(jnp.float32)

    own = x.shape[0]
    n_parts = 2 ** len(lower)
    length = 2 * n_parts * own
    cols = w_query.shape[1]
    heads = cols // HD
    blk = min(512, own)

    spot = jnp.int32(0)
    for axis in lower:
        spot = spot * 2 + lax.axis_index(axis)
    quarters = []
    for part in range(n_parts):
        for other in (0, 1):
            quarters.append((c ^ other) * n_parts + (spot ^ part))
    position = jnp.concatenate([q * own + jnp.arange(own, dtype=jnp.int32) for q in quarters])
    counts = [jnp.sum(segments <= number, dtype=jnp.int32) for number in range(3)]
    last = jnp.where(segments == 0, counts[0], jnp.where(segments == 1, counts[1], counts[2])) - 1
    end_own = jnp.where(padding == 0, last, jnp.arange(length, dtype=jnp.int32))
    end = jnp.where(same, end_own, flip(end_own, core))
    end = jnp.concatenate([lax.dynamic_slice_in_dim(end, q * own, own) for q in quarters])
    lists = visit_lists(position, end, blk)
    end_rows = end.reshape(-1, blk)
    cos_all, sin_all = turn_tables(length)
    cos = jnp.concatenate([lax.dynamic_slice_in_dim(cos_all, q * own, own) for q in quarters])
    sin = jnp.concatenate([lax.dynamic_slice_in_dim(sin_all, q * own, own) for q in quarters])
    mats = (jnp.concatenate([w_query, w_key, w_value], axis=1), w_out, w_gate, w_up, w_down)
    (norm1, w_qkv, full_out, full_gate, full_up, full_down, q, k, v, attended, lse, x_low, hidden, norm2,
     cot_own) = first_half(places, x, end_own.reshape(-1, own), cos_all, sin_all, mats, cot)
    x_own = x_low.astype(jnp.float32)
    norm1_pull = jax.vjp(layer_norm, x_own)[1]
    norm2_pull = jax.vjp(layer_norm, hidden)[1]
    cots = gather(cot_own)

    def halves(product, values):
        def of(part):
            lo = part * 2 * own
            both = low(product(*(value[lo : lo + 2 * own] for value in values)))
            return both[:own], both[own:]

        return of

    gate = dot(norm2, full_gate)
    up_lin = dot(norm2, full_up)
    act, act_pull = jax.vjp(swiglu, gate, up_lin)
    act_low = low(act)
    d_act = dot(cots, full_down)
    d_gate_f, d_up_f = act_pull(d_act)
    d_gate, d_up = low(d_gate_f), low(d_up_f)
    p_down = low(dot(cots, act_low, TN))
    p_mlp = [halves(lambda a: dot(a, full_down, NT), (act_low,))(part) for part in range(n_parts)]
    d_norm2 = scatter(
        halves(lambda a, b: dot(a, full_gate, NT) + dot(b, full_up, NT), (d_gate, d_up)),
        n_parts,
        [p_down] + [half for part in p_mlp for half in part],
    )
    d_hidden = cot_own.astype(jnp.float32) + norm2_pull(d_norm2)[0]
    p_gate = low(dot(norm2, d_gate, TN))
    p_up = low(dot(norm2, d_up, TN))
    d_hiddens = hold(gather(low(d_hidden)), p_gate, p_up)

    mlp = scatter(lambda part: p_mlp[part], n_parts)
    output = swap(low(hidden + mlp))
    g_down, g_gate, g_up = scatter_weight(p_down), scatter_weight(p_gate), scatter_weight(p_up)

    d_attended = low(dot(d_hiddens, full_out))
    dq, dk, dv = attend_back(q, k, v, d_attended, attended, lse, cos, sin, end_rows, lists, heads, 1)
    d_qkv = jnp.concatenate([dq, dk, dv], axis=1)
    d_norm1 = scatter(halves(lambda a: dot(a, w_qkv, NT), (d_qkv,)), n_parts)
    d_input = swap(low(d_hidden + norm1_pull(d_norm1)[0])).astype(jnp.float32)
    g_out = scatter_weight(low(dot(d_hiddens, attended, TN)))
    g_qkv = scatter_weight(low(dot(norm1, d_qkv, TN)))
    return (
        output,
        d_input,
        g_qkv[:, :cols],
        g_qkv[:, cols : 2 * cols],
        g_qkv[:, 2 * cols :],
        g_out,
        g_gate,
        g_up,
        g_down,
    )


def solution(mesh):
    dp, mp = mesh.devices.shape
    n_dp, n_mp = dp.bit_length() - 1, mp.bit_length() - 1
    dp_axes = tuple("d%d" % k for k in range(n_dp))
    mp_axes = tuple("m%d" % k for k in range(n_mp))
    fine = Mesh(mesh.devices.reshape((2,) * (n_dp + n_mp)), dp_axes + mp_axes)
    places = (dp_axes[:-1], dp_axes[-1], mp_axes[0], mp_axes[1:])
    tokens = P(dp_axes + mp_axes, None)
    weight = P(dp_axes, mp_axes)
    return jax.shard_map(
        functools.partial(body, places),
        mesh=fine,
        in_specs=(tokens, P(dp_axes), P(dp_axes)) + (weight,) * 7 + (tokens,),
        out_specs=(tokens, tokens) + (weight,) * 7,
        check_vma=False,
    )
```

time: 1420 us -> 1230 us (0.87)
  waiting for transfers between devices: 717 us -> 349 us
  Pallas kernels: 92 us -> 418 us
  starting transfers between devices: 137 us -> 59.7 us
  matrix products: 327 us -> 283 us
  other arithmetic: 81 us -> 66 us
    pallas_call x2, Pallas kernels: 92 us -> 418 us  [the longest x1 365 us: first_half(): pl.pallas_call(functools.partial(first_kernel, places), in_specs=[there,...]
    ppermute x15 -> x0, waiting for transfers between devices: 213 us -> none  [the longest x5 183 us: gather_weight(): to_far1 = lax.ppermute(shard, pair, [(2, 1), (3, 2)])]
    ppermute x25 -> x16, waiting for transfers between devices: 344 us -> 171 us  [flip(): return lax.ppermute(value, axis, [(0, 1), (1, 0)])]
    dot_general x20 -> x17, matrix products: 327 us -> 283 us  [dot(): lax.dot_general(left, right, dims, preferred_element_type=jnp.float32)]
    reduce_scatter x5, waiting for transfers between devices: 0.05 us -> 41.7 us  [scatter_weight(): both = lax.psum_scatter(partial, rest, scatter_dimension=0, tiled=True)]
    ppermute x15 -> x0, starting transfers between devices: 33.4 us -> none  [the longest x5 18.3 us: gather_weight(): to_far1 = lax.ppermute(shard, pair, [(2, 1), (3, 2)])]
    ppermute x5, waiting for transfers between devices: 147 us -> 117 us  [scatter_weight(): from1 = lax.ppermute(s1, pair, [(1, 2), (2, 3)])]
    ppermute x5, waiting for transfers between devices: 0.01 us -> 17.6 us  [scatter_weight(): from0 = lax.ppermute(s0, pair, [(1, 0), (2, 1)])]
  transfers between devices with their start and end apart: 69 -> 38, of which waited for: 25 -> 11; matrix products, arithmetic and copies ran while one was open for 25% -> 22% of each run, Pallas kernels for 7% -> 4%
where the time goes in v2:
time: 1230 us
  Pallas kernels  418 us (34%)
  waiting for transfers between devices  349 us (28%)
  matrix products  283 us (23%)
  other arithmetic  66 us (5%)
  starting transfers between devices  59.7 us (5%)
  local copies, waits for them, and re-layouts  36.8 us (3%)
  between operations  14.6 us (1%)
    pallas_call x1, Pallas kernels, first_half(): pl.pallas_call(functools.partial(first_kernel, places), in_specs=[there,...  365 us
    dot_general x17, matrix products, dot(): lax.dot_general(left, right, dims, preferred_element_type=jnp.float32)  283 us
    ppermute x16, waiting for transfers between devices, flip(): return lax.ppermute(value, axis, [(0, 1), (1, 0)])  171 us
    ppermute x5, waiting for transfers between devices, scatter_weight(): from1 = lax.ppermute(s1, pair, [(1, 2), (2, 3)])  117 us
    pallas_call x1, Pallas kernels, attend_back(): pl.pallas_call(functools.partial(backward_kernel, hpg, len(after)), grid_...  53 us
    reduce_scatter x5, waiting for transfers between devices, scatter_weight(): both = lax.psum_scatter(partial, rest, scatter_dimension=0, tiled=True)  41.7 us
  transfers between devices with their start and end apart: 38, of which 11 were waited for; matrix products, arithmetic and copies ran while one was open for 22% of the time, Pallas kernels for 4%

profile of v2, /device:TPU:1, one launch (start us, length us, event | category | flops | bytes accessed | tf_op | source)
XLA Modules:
  0.0 1227.9 jit_solution(9092962159358046767)
XLA Ops:
  14.5 365.4 %shard_map.196 = (bf16[2048,2048]{1,0:T(8,128)(2,1)}, bf16[2048,1536]{1,0:T(8,128)(2,1)}, bf16[2048,512]{1,0:T(8,128)(2,1)}, bf16[2048,2048]{1,0:T(8,128)(2,1)},...) custom-call(bf16[512,2048]{1,0:T(8,128)(2,1)} %x.1, ...), custom_call_target="tpu_custom_call" | custom-call | flops 17179869184 | bytes 104857600 | tf_op jit(solution)/shard_map/pallas_call | solution.py:691
  383.8 24.7 %fusion.42 = f32[2048,2048]{1,0:T(8,128)} fusion(bf16[2048,2048]{1,0:T(8,128)(2,1)} %get-tuple-element.31, bf16[2048,2048]{1,0:T(8,128)(2,1)} %get-tuple-element.33), kind=kOutput, calls=%fused_computation.112 | convolution fusion | flops 17179869184 | bytes 33554432 | tf_op jit(solution)/shard_map/dot_general | solution.py:31
  408.5 21.3 %collective-permute-done.5 = bf16[512,2048]{1,0:T(8,128)(2,1)} collective-permute-done((bf16[512,2048]{1,0:T(8,128)(2,1)}, bf16[512,2048]{1,0:T(8,128)(2,1)}, u32[]{:S(2)}, u32[]{:S(2)}) %collective-permute-start.5) | collective-permute-done | bytes 2097184 | tf_op jit(solution)/shard_map/ppermute | solution.py:739
  430.7 20.5 %fusion.41 = f32[2048,2048]{1,0:T(8,128)} fusion(bf16[2048,2048]{1,0:T(8,128)(2,1)S(1)} %copy-done.28, bf16[2048,2048]{1,0:T(8,128)(2,1)S(1)} %copy-done.29), kind=kOutput, calls=%fused_computation.111 | convolution fusion | flops 17179869184 | bytes 33554432 | tf_op jit(solution)/shard_map/dot_general | solution.py:31
  465.4 35.0 %fusion.2 = (bf16[2048,2048]{1,0:T(8,128)(2,1)}, bf16[2048,2048]{1,0:T(8,128)(2,1)}, bf16[2048,2048]{1,0:T(8,128)(2,1)}) fusion(f32[2048,2048]{1,0:T(8,128)} %fusion.41, f32[2048,2048]{1,0:T(8,128)} %fusion.42, bf16[2048,2048]{1,0:T(8,128)(2,1)} %constant_dynamic-update-slice_fusion, bf16[2048,2048]{1,0:T(8,128)(2,1)} %get-tuple-element.34), kind=kOutput, calls=%fused_computation.3 | convolution fusion | flops 17246978048 | bytes 75497472 | tf_op jit(solution)/shard_map/dot_general | solution.py:31
  500.4 14.8 %fusion.13 = f32[1024,2048]{1,0:T(8,128)} fusion(bf16[2048,2048]{1,0:T(8,128)(2,1)} %get-tuple-element.33, bf16[2048,2048]{1,0:T(8,128)(2,1)} %get-tuple-element.63), kind=kOutput, calls=%fused_computation.28 | convolution fusion | flops 8589934592 | bytes 20971520 | tf_op jit(solution)/shard_map/dot_general | solution.py:31
  515.2 13.5 %fusion.9 = f32[1024,2048]{1,0:T(8,128)} fusion(bf16[2048,2048]{1,0:T(8,128)(2,1)} %get-tuple-element.33, bf16[2048,2048]{1,0:T(8,128)(2,1)S(1)} %copy-done.27), kind=kOutput, calls=%fused_computation.24 | convolution fusion | flops 8589934592 | bytes 20971520 | tf_op jit(solution)/shard_map/dot_general | solution.py:31
  528.7 12.6 %fusion.24 = bf16[1024,2048]{1,0:T(8,128)(2,1)S(1)} fusion(bf16[2048,2048]{1,0:T(8,128)(2,1)} %get-tuple-element.34, bf16[2048,2048]{1,0:T(8,128)(2,1)} %get-tuple-element.64), kind=kOutput, calls=%fused_computation.49 | convolution fusion | flops 8592031744 | bytes 16777216 | tf_op jit(solution)/shard_map/dot_general | solution.py:31
  542.8 13.8 %add_convert_fusion.1 = bf16[1024,2048]{1,0:T(8,128)(2,1)S(1)} fusion(f32[1024,2048]{1,0:T(8,128)} %fusion.13, bf16[2048,2048]{1,0:T(8,128)(2,1)} %get-tuple-element.32, bf16[2048,2048]{1,0:T(8,128)(2,1)} %get-tuple-element.62), kind=kOutput, calls=%fused_computation.10 | convolution fusion | flops 8594128896 | bytes 25165824 | tf_op jit(solution)/shard_map/dot_general | solution.py:31
  558.6 15.3 %add_convert_fusion = bf16[1024,2048]{1,0:T(8,128)(2,1)} fusion(f32[1024,2048]{1,0:T(8,128)} %fusion.9, bf16[2048,2048]{1,0:T(8,128)(2,1)} %get-tuple-element.32, bf16[2048,2048]{1,0:T(8,128)(2,1)} %get-tuple-element.62), kind=kOutput, calls=%fused_computation.9 | convolution fusion | flops 8594128896 | bytes 25165824 | tf_op jit(solution)/shard_map/dot_general | solution.py:31
  577.3 12.6 %fusion.21 = bf16[1024,2048]{1,0:T(8,128)(2,1)S(1)} fusion(bf16[2048,2048]{1,0:T(8,128)(2,1)} %get-tuple-element.34, bf16[2048,2048]{1,0:T(8,128)(2,1)} %get-tuple-element.64), kind=kOutput, calls=%fused_computation.48 | convolution fusion | flops 8592031744 | bytes 16777216 | tf_op jit(solution)/shard_map/dot_general | solution.py:31
  598.4 24.2 %convolution_convert_fusion.2 = bf16[2048,2048]{1,0:T(8,128)(2,1)} fusion(bf16[2048,2048]{1,0:T(8,128)(2,1)} %constant_dynamic-update-slice_fusion, bf16[2048,2048]{1,0:T(8,128)(2,1)} %get-tuple-element.64), kind=kOutput, calls=%fused_computation.13 | convolution fusion | flops 17184063488 | bytes 25165824 | tf_op jit(solution)/shard_map/dot_general | solution.py:31
  622.6 63.4 %collective-permute-done.9 = bf16[512,2048]{1,0:T(8,128)(2,1)} collective-permute-done((bf16[512,2048]{1,0:T(8,128)(2,1)}, bf16[512,2048]{1,0:T(8,128)(2,1)}, u32[]{:S(2)}, u32[]{:S(2)}) %collective-permute-start.9) | collective-permute-done | bytes 2097184 | tf_op jit(solution)/shard_map/ppermute | solution.py:739
  691.2 6.1 fusion.38
  700.8 22.3 %convolution_convert_fusion = bf16[2048,2048]{1,0:T(8,128)(2,1)} fusion(bf16[2048,2048]{1,0:T(8,128)(2,1)} %get-tuple-element.31, bf16[2048,2048]{1,0:T(8,128)(2,1)S(1)} %bitcast.30), kind=kOutput, calls=%fused_computation.11 | convolution fusion | flops 17184063488 | bytes 25165824 | tf_op jit(solution)/shard_map/dot_general | solution.py:31
  724.5 21.0 %collective-permute-done.12 = bf16[512,2048]{1,0:T(8,128)(2,1)} collective-permute-done((bf16[512,2048]{1,0:T(8,128)(2,1)S(1)}, bf16[512,2048]{1,0:T(8,128)(2,1)}, u32[]{:S(2)}, u32[]{:S(2)}) %collective-permute-start.12) | collective-permute-done | bytes 2097184 | tf_op jit(solution)/shard_map/ppermute | solution.py:739
  747.5 23.7 %convolution_convert_fusion.1 = bf16[2048,2048]{1,0:T(8,128)(2,1)} fusion(bf16[2048,2048]{1,0:T(8,128)(2,1)} %get-tuple-element.31, bf16[2048,2048]{1,0:T(8,128)(2,1)} %get-tuple-element.62), kind=kOutput, calls=%fused_computation.12 | convolution fusion | flops 17184063488 | bytes 25165824 | tf_op jit(solution)/shard_map/dot_general | solution.py:31
  778.4 5.7 convolution_convert_fusion.6
  790.0 10.0 convolution_convert_fusion.7.grad_ref
  800.0 53.0 %shard_map.197 = (bf16[2048,512]{1,0:T(8,128)(2,1)S(1)}, bf16[2048,512]{1,0:T(8,128)(2,1)}, bf16[2048,512]{1,0:T(8,128)(2,1)}) custom-call(s32[4]{0:T(128)S(1)} %slice.116.first, s32[1]{0:T(128)} %bitcast.total, s32[16]{0:T(128)S(1)} %get-tuple-element.37.pairs, bf16[2048,512]{1,0:T(8,128)(2,1)} %get-tuple-element.38.q_ref, ...), custom_call_target="tpu_custom_call" | custom-call | flops 10737418240 | bytes 20971520 | tf_op jit(solution)/shard_map/pallas_call | solution.py:111
  858.3 15.7 %convolution_convert_fusion.3 = bf16[2048,1536]{1,0:T(8,128)(2,1)} fusion(bf16[2048,2048]{1,0:T(8,128)(2,1)S(1)} %bitcast.32, bf16[2048,1536]{1,0:T(8,128)(2,1)S(1)} %constant_dynamic-update-slice_fusion.4), kind=kOutput, calls=%fused_computation.14 | convolution fusion | flops 12888047616 | bytes 20971520 | tf_op jit(solution)/shard_map/dot_general | solution.py:31
  874.1 10.0 convolution_convert_fusion.4
  884.5 9.0 convolution_convert_fusion.5
  900.0 64.9 %collective-permute-done.16 = bf16[512,2048]{1,0:T(8,128)(2,1)S(1)} collective-permute-done((bf16[512,2048]{1,0:T(8,128)(2,1)S(1)}, bf16[512,2048]{1,0:T(8,128)(2,1)S(1)}, u32[]{:S(2)}, u32[]{:S(2)}) %collective-permute-start.16) | collective-permute-done | bytes 2097184 | tf_op jit(solution)/shard_map/ppermute | solution.py:739
  982.5 17.6 %collective-permute-done.22 = bf16[256,512]{1,0:T(8,128)(2,1)S(1)} collective-permute-done((bf16[256,512]{1,0:T(8,128)(2,1)S(1)}, bf16[256,512]{1,0:T(8,128)(2,1)S(1)}, u32[]{:S(2)}, u32[]{:S(2)}) %collective-permute-start.22) | collective-permute-done | bytes 262176 | tf_op jit(solution)/shard_map/ppermute | solution.py:781
  1000.1 33.5 %collective-permute-done.23 = bf16[256,512]{1,0:T(8,128)(2,1)S(1)} collective-permute-done((bf16[256,512]{1,0:T(8,128)(2,1)S(1)}, bf16[256,512]{1,0:T(8,128)(2,1)S(1)}, u32[]{:S(2)}, u32[]{:S(2)}) %collective-permute-start.23) | collective-permute-done | bytes 262176 | tf_op jit(solution)/shard_map/ppermute | solution.py:782
  1051.2 7.0 collective-permute-start.28
  1058.2 28.5 %reduce-scatter.10.cloned.1.call-done = bf16[512,2048]{1,0:T(8,128)(2,1)} async-done(((bf16[2048,2048]{1,0:T(8,128)(2,1)}), bf16[512,2048]{1,0:T(8,128)(2,1)}) %reduce-scatter.10.cloned.1.call-update) | async-done | bytes 2097168 | tf_op jit(solution)/shard_map/reduce_scatter | solution.py:777
  1095.4 42.6 %collective-permute-done.32 = bf16[256,2048]{1,0:T(8,128)(2,1)} collective-permute-done((bf16[256,2048]{1,0:T(8,128)(2,1)}, bf16[256,2048]{1,0:T(8,128)(2,1)}, u32[]{:S(2)}, u32[]{:S(2)}) %collective-permute-start.32) | collective-permute-done | bytes 1048608 | tf_op jit(solution)/shard_map/ppermute | solution.py:782
  1146.6 13.2 %reduce-scatter.6.cloned.1.call-done = bf16[512,1536]{1,0:T(8,128)(2,1)} async-done(((bf16[2048,1536]{1,0:T(8,128)(2,1)}), bf16[512,1536]{1,0:T(8,128)(2,1)}) %reduce-scatter.6.cloned.1.call-update) | async-done | bytes 1572880 | tf_op jit(solution)/shard_map/reduce_scatter | solution.py:777
  1172.3 27.5 %collective-permute-done.26 = bf16[256,2048]{1,0:T(8,128)(2,1)} collective-permute-done((bf16[256,2048]{1,0:T(8,128)(2,1)}, bf16[256,2048]{1,0:T(8,128)(2,1)}, u32[]{:S(2)}, u32[]{:S(2)}) %collective-permute-start.26) | collective-permute-done | bytes 1048608 | tf_op jit(solution)/shard_map/ppermute | solution.py:782
  1203.0 13.6 %collective-permute-done.20 = bf16[256,1536]{1,0:T(8,128)(2,1)S(1)} collective-permute-done((bf16[256,1536]{1,0:T(8,128)(2,1)S(1)}, bf16[256,1536]{1,0:T(8,128)(2,1)S(1)}, u32[]{:S(2)}, u32[]{:S(2)}) %collective-permute-start.20) | collective-permute-done | bytes 786464 | tf_op jit(solution)/shard_map/ppermute | solution.py:782
  (208 shorter events, 151.5 us)
Async XLA Ops:
  7.2 966.9 %reduce-scatter.8.cloned.1.call-start = ((), (), s32[]{:S(2)}) async-start(), calls=%async_computation.6 | async-start | bytes 2621440 | tf_op jit(solution)/shard_map/reduce_scatter | solution.py:777
  379.9 76.0 %collective-permute-start.4 = (bf16[512,2048]{1,0:T(8,128)(2,1)}, bf16[512,2048]{1,0:T(8,128)(2,1)}, u32[]{:S(2)}, u32[]{:S(2)}) collective-permute-start(bf16[512,2048]{1,0:T(8,128)(2,1)} %get-tuple-element.35), channel_id=1, source_target_pairs={{0,4},{4,0},{1,5},{5,1},{2,6},{6,2},{3,7},{7,3},{8,12},{12,8},{9,1... | collective-permute-start | bytes 6291464 | tf_op jit(solution)/shard_map/ppermute | solution.py:739
  380.0 49.8 %collective-permute-start.5 = (bf16[512,2048]{1,0:T(8,128)(2,1)}, bf16[512,2048]{1,0:T(8,128)(2,1)}, u32[]{:S(2)}, u32[]{:S(2)}) collective-permute-start(bf16[512,2048]{1,0:T(8,128)(2,1)} %get-tuple-element.35), channel_id=1, source_target_pairs={{0,1},{1,0},{2,3},{3,2},{4,5},{5,4},{6,7},{7,6},{8,9},{9,8},{10,11... | collective-permute-start | bytes 6291464 | tf_op jit(solution)/shard_map/ppermute | solution.py:739
  429.8 32.5 %collective-permute-start.6 = (bf16[512,2048]{1,0:T(8,128)(2,1)}, bf16[512,2048]{1,0:T(8,128)(2,1)}, u32[]{:S(2)}, u32[]{:S(2)}) collective-permute-start(bf16[512,2048]{1,0:T(8,128)(2,1)} %collective-permute-done.5), channel_id=1, source_target_pairs={{0,4},{4,0},{1,5},{5,1},{2,6},{6,2},{3,7},{7,3},{8,12},{12,8},{9,1... | collective-permute-start | bytes 6291464 | tf_op jit(solution)/shard_map/ppermute | solution.py:739
  542.7 48.9 %collective-permute-start.1 = (bf16[512,2048]{1,0:T(8,128)(2,1)}, bf16[512,2048]{1,0:T(8,128)(2,1)S(1)}, u32[]{:S(2)}, u32[]{:S(2)}) collective-permute-start(bf16[512,2048]{1,0:T(8,128)(2,1)} %slice.141), channel_id=1, source_target_pairs={{0,4},{4,0},{1,5},{5,1},{2,6},{6,2},{3,7},{7,3},{8,12},{12,8},{9,1... | collective-permute-start | bytes 6291464 | tf_op jit(solution)/shard_map/ppermute | solution.py:739
  558.1 127.9 %collective-permute-start.7 = (bf16[512,2048]{1,0:T(8,128)(2,1)}, bf16[512,2048]{1,0:T(8,128)(2,1)S(1)}, u32[]{:S(2)}, u32[]{:S(2)}) collective-permute-start(bf16[512,2048]{1,0:T(8,128)(2,1)} %slice.145), channel_id=1, source_target_pairs={{0,4},{4,0},{1,5},{5,1},{2,6},{6,2},{3,7},{7,3},{8,12},{12,8},{9,1... | collective-permute-start | bytes 6291464 | tf_op jit(solution)/shard_map/ppermute | solution.py:739
  591.4 99.7 %collective-permute-start = (bf16[512,2048]{1,0:T(8,128)(2,1)}, bf16[512,2048]{1,0:T(8,128)(2,1)}, u32[]{:S(2)}, u32[]{:S(2)}) collective-permute-start(bf16[512,2048]{1,0:T(8,128)(2,1)} %slice.138), channel_id=1, source_target_pairs={{0,4},{4,0},{1,5},{5,1},{2,6},{6,2},{3,7},{7,3},{8,12},{12,8},{9,1... | collective-permute-start | bytes 6291464 | tf_op jit(solution)/shard_map/ppermute | solution.py:739
  593.8 97.4 %collective-permute-start.2 = (bf16[512,2048]{1,0:T(8,128)(2,1)}, bf16[512,2048]{1,0:T(8,128)(2,1)}, u32[]{:S(2)}, u32[]{:S(2)}) collective-permute-start(bf16[512,2048]{1,0:T(8,128)(2,1)} %add_convert_fusion.6), channel_id=1, source_target_pairs={{0,1},{1,0},{2,3},{3,2},{4,5},{5,4},{6,7},{7,6},{8,9},{9,8},{10,11... | collective-permute-start | bytes 6291464 | tf_op jit(solution)/shard_map/ppermute | solution.py:739
  597.3 88.7 %collective-permute-start.9 = (bf16[512,2048]{1,0:T(8,128)(2,1)}, bf16[512,2048]{1,0:T(8,128)(2,1)}, u32[]{:S(2)}, u32[]{:S(2)}) collective-permute-start(bf16[512,2048]{1,0:T(8,128)(2,1)} %add_convert_fusion.4), channel_id=1, source_target_pairs={{0,1},{1,0},{2,3},{3,2},{4,5},{5,4},{6,7},{7,6},{8,9},{9,8},{10,11... | collective-permute-start | bytes 6291464 | tf_op jit(solution)/shard_map/ppermute | solution.py:739
  699.3 46.1 %collective-permute-start.12 = (bf16[512,2048]{1,0:T(8,128)(2,1)S(1)}, bf16[512,2048]{1,0:T(8,128)(2,1)}, u32[]{:S(2)}, u32[]{:S(2)}) collective-permute-start(bf16[512,2048]{1,0:T(8,128)(2,1)S(1)} %fusion.33), channel_id=1, source_target_pairs={{0,1},{1,0},{2,3},{3,2},{4,5},{5,4},{6,7},{7,6},{8,9},{9,8},{10,11... | collective-permute-start | bytes 6291464 | tf_op jit(solution)/shard_map/ppermute | solution.py:739
  723.1 48.1 %collective-permute-start.11 = (bf16[512,2048]{1,0:T(8,128)(2,1)S(1)}, bf16[512,2048]{1,0:T(8,128)(2,1)}, u32[]{:S(2)}, u32[]{:S(2)}) collective-permute-start(bf16[512,2048]{1,0:T(8,128)(2,1)S(1)} %fusion.33), channel_id=1, source_target_pairs={{0,4},{4,0},{1,5},{5,1},{2,6},{6,2},{3,7},{7,3},{8,12},{12,8},{9,1... | collective-permute-start | bytes 6291464 | tf_op jit(solution)/shard_map/ppermute | solution.py:739
  745.5 25.7 %collective-permute-start.13 = (bf16[512,2048]{1,0:T(8,128)(2,1)}, bf16[512,2048]{1,0:T(8,128)(2,1)}, u32[]{:S(2)}, u32[]{:S(2)}) collective-permute-start(bf16[512,2048]{1,0:T(8,128)(2,1)} %collective-permute-done.12), channel_id=1, source_target_pairs={{0,4},{4,0},{1,5},{5,1},{2,6},{6,2},{3,7},{7,3},{8,12},{12,8},{9,1... | collective-permute-start | bytes 6291464 | tf_op jit(solution)/shard_map/ppermute | solution.py:739
  784.1 253.9 %reduce-scatter.14.cloned.1.call-start = ((), (), s32[]{:S(2)}) async-start(), calls=%async_computation.9 | async-start | bytes 10485760 | tf_op jit(solution)/shard_map/reduce_scatter | solution.py:777
  784.9 261.7 %reduce-scatter.12.cloned.1.call-start = ((), (), s32[]{:S(2)}) async-start(), calls=%async_computation.8 | async-start | bytes 10485760 | tf_op jit(solution)/shard_map/reduce_scatter | solution.py:777
  785.7 301.1 %reduce-scatter.10.cloned.1.call-start = ((), (), s32[]{:S(2)}) async-start(), calls=%async_computation.7 | async-start | bytes 10485760 | tf_op jit(solution)/shard_map/reduce_scatter | solution.py:777
  786.2 373.6 %reduce-scatter.6.cloned.1.call-start = ((), (), s32[]{:S(2)}) async-start(), calls=%async_computation.5 | async-start | bytes 7864320 | tf_op jit(solution)/shard_map/reduce_scatter | solution.py:777
  895.1 69.8 %collective-permute-start.16 = (bf16[512,2048]{1,0:T(8,128)(2,1)S(1)}, bf16[512,2048]{1,0:T(8,128)(2,1)S(1)}, u32[]{:S(2)}, u32[]{:S(2)}) collective-permute-start(bf16[512,2048]{1,0:T(8,128)(2,1)S(1)} %add_convert_fusion.3), channel_id=1, source_target_pairs={{0,1},{1,0},{2,3},{3,2},{4,5},{5,4},{6,7},{7,6},{8,9},{9,8},{10,11... | collective-permute-start | bytes 6291464 | tf_op jit(solution)/shard_map/ppermute | solution.py:739
  897.0 85.5 %collective-permute-start.3 = (bf16[512,2048]{1,0:T(8,128)(2,1)}, bf16[512,2048]{1,0:T(8,128)(2,1)}, u32[]{:S(2)}, u32[]{:S(2)}) collective-permute-start(bf16[512,2048]{1,0:T(8,128)(2,1)} %get-tuple-element.65), channel_id=1, source_target_pairs={{0,0},{2,4},{4,2},{6,6},{1,1},{3,5},{5,3},{7,7},{8,8},{10,12},{12,... | collective-permute-start | bytes 6291464 | tf_op jit(solution)/shard_map/ppermute | solution.py:750
  971.7 63.8 %collective-permute-start.17 = (bf16[512,2048]{1,0:T(8,128)(2,1)}, bf16[512,2048]{1,0:T(8,128)(2,1)S(1)}, u32[]{:S(2)}, u32[]{:S(2)}) collective-permute-start(bf16[512,2048]{1,0:T(8,128)(2,1)} %add_convert_fusion.2), channel_id=1, source_target_pairs={{0,0},{2,4},{4,2},{6,6},{1,1},{3,5},{5,3},{7,7},{8,8},{10,12},{12,... | collective-permute-start | bytes 6291464 | tf_op jit(solution)/shard_map/ppermute | solution.py:750
  980.6 53.0 %collective-permute-start.23 = (bf16[256,512]{1,0:T(8,128)(2,1)S(1)}, bf16[256,512]{1,0:T(8,128)(2,1)S(1)}, u32[]{:S(2)}, u32[]{:S(2)}) collective-permute-start(bf16[256,512]{1,0:T(8,128)(2,1)S(1)} %get-tuple-element.90), channel_id=1, source_target_pairs={{2,4},{4,6},{3,5},{5,7},{10,12},{12,14},{11,13},{13,15},{18,20},{2... | collective-permute-start | bytes 786440 | tf_op jit(solution)/shard_map/ppermute | solution.py:782
  1041.5 48.6 %collective-permute-start.30 = (bf16[256,2048]{1,0:T(8,128)(2,1)}, bf16[256,2048]{1,0:T(8,128)(2,1)S(1)}, u32[]{:S(2)}, u32[]{:S(2)}) collective-permute-start(bf16[256,2048]{1,0:T(8,128)(2,1)} %get-tuple-element.66), channel_id=1, source_target_pairs={{0,4},{6,2},{1,5},{7,3},{8,12},{14,10},{9,13},{15,11},{16,20},{22,... | collective-permute-start | bytes 3145736 | tf_op jit(solution)/shard_map/ppermute | solution.py:780
  1042.8 51.3 %collective-permute-start.31 = (bf16[256,2048]{1,0:T(8,128)(2,1)}, bf16[256,2048]{1,0:T(8,128)(2,1)S(1)}, u32[]{:S(2)}, u32[]{:S(2)}) collective-permute-start(bf16[256,2048]{1,0:T(8,128)(2,1)} %get-tuple-element.68), channel_id=1, source_target_pairs={{2,0},{4,2},{3,1},{5,3},{10,8},{12,10},{11,9},{13,11},{18,16},{20,... | collective-permute-start | bytes 3145736 | tf_op jit(solution)/shard_map/ppermute | solution.py:781
  1044.7 93.4 %collective-permute-start.32 = (bf16[256,2048]{1,0:T(8,128)(2,1)}, bf16[256,2048]{1,0:T(8,128)(2,1)}, u32[]{:S(2)}, u32[]{:S(2)}) collective-permute-start(bf16[256,2048]{1,0:T(8,128)(2,1)} %get-tuple-element.67), channel_id=1, source_target_pairs={{2,4},{4,6},{3,5},{5,7},{10,12},{12,14},{11,13},{13,15},{18,20},{2... | collective-permute-start | bytes 3145736 | tf_op jit(solution)/shard_map/ppermute | solution.py:782
  1050.0 94.8 %collective-permute-start.27 = (bf16[256,2048]{1,0:T(8,128)(2,1)}, bf16[256,2048]{1,0:T(8,128)(2,1)S(1)}, u32[]{:S(2)}, u32[]{:S(2)}) collective-permute-start(bf16[256,2048]{1,0:T(8,128)(2,1)} %get-tuple-element.69), channel_id=1, source_target_pairs={{0,4},{6,2},{1,5},{7,3},{8,12},{14,10},{9,13},{15,11},{16,20},{22,... | collective-permute-start | bytes 3145736 | tf_op jit(solution)/shard_map/ppermute | solution.py:780
  1051.2 110.1 %collective-permute-start.28 = (bf16[256,2048]{1,0:T(8,128)(2,1)}, bf16[256,2048]{1,0:T(8,128)(2,1)}, u32[]{:S(2)}, u32[]{:S(2)}) collective-permute-start(bf16[256,2048]{1,0:T(8,128)(2,1)} %get-tuple-element.71), channel_id=1, source_target_pairs={{2,0},{4,2},{3,1},{5,3},{10,8},{12,10},{11,9},{13,11},{18,16},{20,... | collective-permute-start | bytes 3145736 | tf_op jit(solution)/shard_map/ppermute | solution.py:781
  1090.1 72.7 %collective-permute-start.29 = (bf16[256,2048]{1,0:T(8,128)(2,1)}, bf16[256,2048]{1,0:T(8,128)(2,1)}, u32[]{:S(2)}, u32[]{:S(2)}) collective-permute-start(bf16[256,2048]{1,0:T(8,128)(2,1)} %get-tuple-element.70), channel_id=1, source_target_pairs={{2,4},{4,6},{3,5},{5,7},{10,12},{12,14},{11,13},{13,15},{18,20},{2... | collective-permute-start | bytes 3145736 | tf_op jit(solution)/shard_map/ppermute | solution.py:782
  1094.1 73.4 %collective-permute-start.24 = (bf16[256,2048]{1,0:T(8,128)(2,1)}, bf16[256,2048]{1,0:T(8,128)(2,1)}, u32[]{:S(2)}, u32[]{:S(2)}) collective-permute-start(bf16[256,2048]{1,0:T(8,128)(2,1)} %get-tuple-element.72), channel_id=1, source_target_pairs={{0,4},{6,2},{1,5},{7,3},{8,12},{14,10},{9,13},{15,11},{16,20},{22,... | collective-permute-start | bytes 3145736 | tf_op jit(solution)/shard_map/ppermute | solution.py:780
  1138.1 34.2 %collective-permute-start.25 = (bf16[256,2048]{1,0:T(8,128)(2,1)}, bf16[256,2048]{1,0:T(8,128)(2,1)}, u32[]{:S(2)}, u32[]{:S(2)}) collective-permute-start(bf16[256,2048]{1,0:T(8,128)(2,1)} %get-tuple-element.74), channel_id=1, source_target_pairs={{2,0},{4,2},{3,1},{5,3},{10,8},{12,10},{11,9},{13,11},{18,16},{20,... | collective-permute-start | bytes 3145736 | tf_op jit(solution)/shard_map/ppermute | solution.py:781
  1144.7 55.1 %collective-permute-start.26 = (bf16[256,2048]{1,0:T(8,128)(2,1)}, bf16[256,2048]{1,0:T(8,128)(2,1)}, u32[]{:S(2)}, u32[]{:S(2)}) collective-permute-start(bf16[256,2048]{1,0:T(8,128)(2,1)} %get-tuple-element.73), channel_id=1, source_target_pairs={{2,4},{4,6},{3,5},{5,7},{10,12},{12,14},{11,13},{13,15},{18,20},{2... | collective-permute-start | bytes 3145736 | tf_op jit(solution)/shard_map/ppermute | solution.py:782
  1161.4 41.6 %collective-permute-start.18 = (bf16[256,1536]{1,0:T(8,128)(2,1)S(1)}, bf16[256,1536]{1,0:T(8,128)(2,1)S(1)}, u32[]{:S(2)}, u32[]{:S(2)}) collective-permute-start(bf16[256,1536]{1,0:T(8,128)(2,1)S(1)} %get-tuple-element.78), channel_id=1, source_target_pairs={{0,4},{6,2},{1,5},{7,3},{8,12},{14,10},{9,13},{15,11},{16,20},{22,... | collective-permute-start | bytes 2359304 | tf_op jit(solution)/shard_map/ppermute | solution.py:780
  1162.8 40.2 %collective-permute-start.19 = (bf16[256,1536]{1,0:T(8,128)(2,1)S(1)}, bf16[256,1536]{1,0:T(8,128)(2,1)S(1)}, u32[]{:S(2)}, u32[]{:S(2)}) collective-permute-start(bf16[256,1536]{1,0:T(8,128)(2,1)S(1)} %get-tuple-element.80), channel_id=1, source_target_pairs={{2,0},{4,2},{3,1},{5,3},{10,8},{12,10},{11,9},{13,11},{18,16},{20,... | collective-permute-start | bytes 2359304 | tf_op jit(solution)/shard_map/ppermute | solution.py:781
  1167.5 49.1 %collective-permute-start.20 = (bf16[256,1536]{1,0:T(8,128)(2,1)S(1)}, bf16[256,1536]{1,0:T(8,128)(2,1)S(1)}, u32[]{:S(2)}, u32[]{:S(2)}) collective-permute-start(bf16[256,1536]{1,0:T(8,128)(2,1)S(1)} %get-tuple-element.79), channel_id=1, source_target_pairs={{2,4},{4,6},{3,5},{5,7},{10,12},{12,14},{11,13},{13,15},{18,20},{2... | collective-permute-start | bytes 2359304 | tf_op jit(solution)/shard_map/ppermute | solution.py:782
  (42 other events, 854.8 us)
Sparse Core Ops, SparseCore 0:
  784.3 33.5 reduce-scatter.7
  821.2 86.3 reduce-scatter.13
  910.7 86.3 reduce-scatter.11
  1000.3 86.4 reduce-scatter.9
  1089.6 70.2 reduce-scatter.5

commit v3 on v2

--- a/solution.py
+++ b/solution.py
@@ -12,121 +12,23 @@
 LOG2E = 1.4426950408889634
 NEG = -1e30
 eps = 1e-05
+NN = (((1,), (0,)), ((), ()))
 NT = (((1,), (1,)), ((), ()))
 TN = (((0,), (0,)), ((), ()))
 
 
-def layer_norm(tok_rows):
-    average = jnp.mean(tok_rows, axis=-1, keepdims=True)
-    centred = tok_rows - average
-    variance = jnp.mean(centred * centred, axis=-1, keepdims=True)
-    return centred * lax.rsqrt(variance + eps)
-
-
-def swiglu(gate, up_lin):
-    return jax.nn.silu(gate) * up_lin
-
-
 def dot(left, right, dims=(((1,), (0,)), ((), ()))):
     return lax.dot_general(left, right, dims, preferred_element_type=jnp.float32)
 
 
 def low(value):
     return value.astype(jnp.bfloat16)
-
-def visit_lists(pos, end, blk):
-    first = pos[::blk]
-    most = jnp.max(end.reshape(-1, blk), axis=1)
-    met = (first[None, :] <= first[:, None]) & (most[None, :] >= first[:, None])
-    count = jnp.sum(met, axis=1, dtype=jnp.int32)
-    keys = jnp.argsort(~met, axis=1, stable=True).astype(jnp.int32)
-    total = jnp.sum(count, dtype=jnp.int32)
-    pairs = jnp.argsort(~met.reshape(-1), stable=True).astype(jnp.int32)
-    return first, count, keys.reshape(-1), total.reshape(1), pairs
-
-
-def turned(value, cos_ref, sin_ref, sign):
-    return value * cos_ref[...] + sign * pltpu.roll(value, HD // 2, 1) * sin_ref[...]
-
 
 def allowed_of(first_q, first_k, end_row):
     blk = end_row.shape[1]
     t = first_q + lax.broadcasted_iota(jnp.int32, (blk, 1), 0)
     u = first_k + lax.broadcasted_iota(jnp.int32, (1, blk), 1)
     return (u <= t) & (t <= end_row)
-
-
-def backward_kernel(
-    hpg, n_after, first, total, pairs, q_ref, k_ref, v_ref, grad_ref, att_ref, lse_ref,
-    cos_ref, sin_ref, end_ref, *refs
-):
-    dq_ref, dk_ref, dv_ref, dq_acc, dk_acc, dv_acc, delta, lses = refs[n_after:]
-    n_k, blk = end_ref.shape
-    dq_acc[...] = jnp.zeros_like(dq_acc)
-    dk_acc[...] = jnp.zeros_like(dk_acc)
-    dv_acc[...] = jnp.zeros_like(dv_acc)
-    lanes = lax.broadcasted_iota(jnp.int32, lse_ref.shape, 1)
-    for h in range(hpg):
-        cols = slice(h * HD, (h + 1) * HD)
-        mine = jnp.where(lanes == pl.program_id(0) * hpg + h, lse_ref[...], 0.0)
-        lses[:, cols] = jnp.broadcast_to(jnp.sum(mine, axis=1, keepdims=True), mine.shape)
-        prod = grad_ref[:, cols].astype(jnp.float32) * att_ref[:, cols].astype(jnp.float32)
-        delta[:, cols] = jnp.broadcast_to(jnp.sum(prod, axis=1, keepdims=True), prod.shape)
-
-    def step(n, carry):
-        code = pairs[n]
-        i, j = code // n_k, code % n_k
-        rows = pl.ds(pl.multiple_of(i * blk, blk), blk)
-        spot = pl.ds(pl.multiple_of(j * blk, blk), blk)
-        allowed = allowed_of(first[i], first[j], end_ref[pl.ds(j, 1), :])
-        for h in range(hpg):
-            cols = slice(h * HD, (h + 1) * HD)
-            q, k, v, grad = q_ref[rows, cols], k_ref[spot, cols], v_ref[spot, cols], grad_ref[rows, cols]
-            scores = dot(q, k, NT) * (SCALE * LOG2E)
-            lse = lses[rows, h * HD : h * HD + 1]
-            probs = jnp.where(allowed, jnp.exp2(scores - lse), 0.0)
-            d_probs = dot(grad, v, NT)
-            d_scores = (probs * (d_probs - delta[rows, h * HD : h * HD + 1])).astype(jnp.bfloat16)
-            dv_acc[spot, cols] += dot(probs.astype(jnp.bfloat16), grad, TN)
-            dk_acc[spot, cols] += dot(d_scores, q, TN)
-            dq_acc[rows, cols] += dot(d_scores, k)
-        return carry
-
-    lax.fori_loop(0, total[0], step, 0)
-    for h in range(hpg):
-        cols = slice(h * HD, (h + 1) * HD)
-        dq_ref[:, cols] = turned(dq_acc[:, cols] * SCALE, cos_ref, sin_ref, -1.0).astype(jnp.bfloat16)
-        dk_ref[:, cols] = turned(dk_acc[:, cols] * SCALE, cos_ref, sin_ref, -1.0).astype(jnp.bfloat16)
-        dv_ref[:, cols] = dv_acc[:, cols].astype(jnp.bfloat16)
-
-
-def attend_back(q, k, v, grad, att, lse, cos, sin, end_rows, lists, heads, hpg, after=()):
-    length = q.shape[0]
-    first, _, _, total, pairs = lists
-    groups = heads // hpg
-    wide = hpg * HD
-    col = pl.BlockSpec((length, wide), lambda g, *_: (0, g))
-    whole = lambda a: pl.BlockSpec(a.shape, lambda g, *_: (0, 0))
-    low = jax.ShapeDtypeStruct((length, heads * HD), jnp.bfloat16)
-    return pl.pallas_call(
-        functools.partial(backward_kernel, hpg, len(after)),
-        grid_spec=pltpu.PrefetchScalarGridSpec(
-            num_scalar_prefetch=3,
-            grid=(groups,),
-            in_specs=[col] * 5
-            + [whole(lse), whole(cos), whole(sin), whole(end_rows)]
-            + [pl.BlockSpec(memory_space=pl.ANY)] * len(after),
-            out_specs=[col] * 3,
-            scratch_shapes=[pltpu.VMEM((length, wide), jnp.float32)] * 5,
-        ),
-        out_shape=[low] * 3,
-        compiler_params=pltpu.CompilerParams(vmem_limit_bytes=48 * 2**20),
-        cost_estimate=pl.CostEstimate(
-            flops=5 * length * length * HD * heads,
-            bytes_accessed=length * heads * HD * 20,
-            transcendentals=heads * length * length // 2,
-        ),
-    )(first, total, pairs, q, k, v, grad, att, lse, cos, sin, end_rows, *after)
 
 
 MESH = pl.DeviceIdType.MESH
@@ -721,8 +623,619 @@
     )(x, end_mine, cos, sin, *mats, cot)
 
 
-def hold(value, *after):
-    return lax.optimization_barrier((value,) + after)[0]
+def matmul(kind, left, right, out, rows, cols):
+    depth = left.shape[0] if kind == TN else left.shape[1]
+
+    def tile(a, b, made):
+        made[...] = low(dot(a[...], b[...], kind))
+
+    a_spec = (
+        pl.BlockSpec((depth, rows), lambda i, j: (0, i))
+        if kind == TN
+        else pl.BlockSpec((rows, depth), lambda i, j: (i, 0))
+    )
+    b_spec = (
+        pl.BlockSpec((cols, depth), lambda i, j: (j, 0))
+        if kind == NT
+        else pl.BlockSpec((depth, cols), lambda i, j: (0, j))
+    )
+    pltpu.emit_pipeline(
+        tile,
+        grid=(out.shape[0] // rows, out.shape[1] // cols),
+        in_specs=[a_spec, b_spec],
+        out_specs=[pl.BlockSpec((rows, cols), lambda i, j: (i, j))],
+    )(left, right, out)
+
+
+def two_products(left1, right1, left2, right2, out, cols):
+    def tile(a, b, c, d, made):
+        made[...] = low(dot(a[...], b[...], NT) + dot(c[...], d[...], NT))
+
+    rows, depth = left1.shape
+    held = pl.BlockSpec((rows, depth), lambda j: (0, 0))
+    moving = pl.BlockSpec((cols, depth), lambda j: (j, 0))
+    pltpu.emit_pipeline(
+        tile,
+        grid=(out.shape[1] // cols,),
+        in_specs=[held, moving, held, moving],
+        out_specs=[pl.BlockSpec((rows, cols), lambda j: (0, j))],
+    )(left1, right1, left2, right2, out)
+
+
+def by_rows(make, rows, ins, outs):
+    spec = lambda ref: pl.BlockSpec((rows, ref.shape[1]), lambda i: (i, 0))
+    pltpu.emit_pipeline(
+        make,
+        grid=(outs[0].shape[0] // rows,),
+        in_specs=[spec(ref) for ref in ins],
+        out_specs=[spec(ref) for ref in outs],
+    )(*ins, *outs)
+
+
+def gated(norm, cots, w_gate, w_up, w_down, act, d_gate, d_up, rows, cols):
+    def tile(n, c, wg, wu, wd, act_t, gate_t, up_t):
+        gate, up = dot(n[...], wg[...]), dot(n[...], wu[...])
+        d_act = dot(c[...], wd[...])
+        s = 1.0 / (1.0 + jnp.exp(-gate))
+        silu = gate * s
+        act_t[...] = low(silu * up)
+        gate_t[...] = low(d_act * up * s * (1.0 + gate * (1.0 - s)))
+        up_t[...] = low(d_act * silu)
+
+    depth = norm.shape[1]
+    row = pl.BlockSpec((rows, depth), lambda i, j: (i, 0))
+    col = pl.BlockSpec((depth, cols), lambda i, j: (0, j))
+    made = pl.BlockSpec((rows, cols), lambda i, j: (i, j))
+    pltpu.emit_pipeline(
+        tile,
+        grid=(act.shape[0] // rows, act.shape[1] // cols),
+        in_specs=[row, row, col, col, col],
+        out_specs=[made] * 3,
+    )(norm, cots, w_gate, w_up, w_down, act, d_gate, d_up)
+
+
+def norm_back(value, grad):
+    average = jnp.mean(value, axis=-1, keepdims=True)
+    centred = value - average
+    r = lax.rsqrt(jnp.mean(centred * centred, axis=-1, keepdims=True) + eps)
+    n = centred * r
+    return r * (
+        grad - jnp.mean(grad, axis=-1, keepdims=True) - n * jnp.mean(grad * n, axis=-1, keepdims=True)
+    )
+
+
+class Sums:
+    def __init__(self, links, mine, other, come, ready, line):
+        self.links, self.mine, self.other = links, mine, other
+        self.come, self.ready, self.line = come, ready, line
+        n_parts, self.own, _ = mine.shape
+        self.chunk = self.own // CHUNKS
+        self.spots = [links.take() for _ in range(n_parts)]
+        self.line_spots = {
+            (part, k): links.take() for part in range(1, n_parts) for k in range(CHUNKS)
+        }
+
+    def across(self, part):
+        links = self.links
+        return links.copy(self.other.at[part], self.come.at[part], links.across, self.spots[part])
+
+    def along(self, part, k):
+        links = self.links
+        rows = pl.ds(k * self.chunk, self.chunk)
+        step = len(links.lower) - part.bit_length()
+        return links.copy(
+            self.ready.at[part - 1, rows], self.line.at[part - 1, rows], links.beside(step),
+            self.line_spots[part, k],
+        )
+
+    def more(self, part):
+        return [part | 1 << k for k in range(part.bit_length(), len(self.links.lower))]
+
+    def far(self, part):
+        self.across(part).wait_recv()
+        ins = [self.mine.at[part], self.come.at[part]]
+        for number in self.more(part):
+            for k in range(CHUNKS):
+                self.along(number, k).wait_recv()
+            ins.append(self.line.at[number - 1])
+
+        def make(*refs):
+            total = refs[0][...].astype(jnp.float32)
+            for ref in refs[1:-1]:
+                total = total + ref[...].astype(jnp.float32)
+            refs[-1][...] = low(total)
+
+        by_rows(make, self.chunk, ins, [self.ready.at[part - 1]])
+        for k in range(CHUNKS):
+            self.along(part, k).start()
+
+    def arrived(self, k):
+        if k == 0:
+            self.across(0).wait_recv()
+        for number in self.more(0):
+            self.along(number, k).wait_recv()
+
+    def terms(self, rows):
+        return [self.mine.at[0, rows], self.come.at[0, rows]] + [
+            self.line.at[number - 1, rows] for number in self.more(0)
+        ]
+
+    def finish(self):
+        for part in range(self.mine.shape[0]):
+            self.across(part).wait_send()
+        for part, k in self.line_spots:
+            self.along(part, k).wait_send()
+
+
+class Gradient:
+    def __init__(self, links, partial, come, stage, stage_sems, near, far):
+        self.links, self.partial, self.come, self.stage = links, partial, come, stage
+        self.stage_sems, self.near, self.far = stage_sems, near, far
+        self.rows = near.shape[0]
+        n = len(links.rest)
+        self.n = n
+        self.kept, self.sent, self.place, self.spots = {}, {}, {}, {}
+        for half in range(2):
+            order = list(reversed(range(n))) if half == 0 else list(range(n))
+            have = list(range(2**n))
+            for step, axis in enumerate(order):
+                self.sent[half, step] = (axis, [mask for mask in have if mask >> axis & 1])
+                have = [mask for mask in have if not mask >> axis & 1]
+                self.kept[half, step] = have
+                for mask in have:
+                    self.place[half, step, mask] = len(self.place)
+                    self.spots[half, step, mask] = links.take()
+        self.near_spot, self.far_spot = links.take(), links.take()
+        self.out_spots = [links.take(), links.take()]
+
+    def slot(self, mask, half):
+        start = (self.links.group(mask) * 2 + half) * self.rows
+        return self.partial.at[pl.ds(pl.multiple_of(start, self.rows), self.rows)]
+
+    def block(self, half, step, mask):
+        return self.come.at[self.place[half, step, mask]]
+
+    def copies(self, step):
+        for half in range(2):
+            axis, masks = self.sent[half, step]
+            for mask in masks:
+                goal = mask & ~(1 << axis)
+                src = self.slot(mask, half) if step == 0 else self.block(half, step - 1, mask)
+                yield self.links.copy(
+                    src, self.block(half, step, goal), self.links.over(axis), self.spots[half, step, goal]
+                )
+
+    def loads(self):
+        number = 0
+        for half in range(2):
+            for mask in self.kept[half, 0]:
+                yield pltpu.make_async_copy(
+                    self.slot(mask, half), self.stage.at[number], self.stage_sems.at[number]
+                )
+                number += 1
+
+    def start(self):
+        for copy in self.copies(0):
+            copy.start()
+        for load in self.loads():
+            load.start()
+
+    def step(self, step):
+        for copy in self.copies(step):
+            copy.wait_recv()
+        if step == 0:
+            for load in self.loads():
+                load.wait()
+        number = 0
+        for half in range(2):
+            for mask in self.kept[half, step]:
+                goal = self.block(half, step, mask)
+                add = self.stage.at[number] if step == 0 else self.block(half, step - 1, mask)
+                number += 1
+                rows = min(64, self.rows)
+
+                @pl.loop(0, self.rows // rows)
+                def _(i, goal=goal, add=add):
+                    spot = pl.ds(pl.multiple_of(i * rows, rows), rows)
+                    goal[spot, :] = low(
+                        goal[spot, :].astype(jnp.float32) + add[spot, :].astype(jnp.float32)
+                    )
+
+        if step + 1 < self.n:
+            for copy in self.copies(step + 1):
+                copy.start()
+        else:
+            self.hand()
+
+    def total(self, half):
+        first, second = (self.place[k, self.n - 1, 0] for k in range(2))
+        return self.come.at[first + half * (second - first)]
+
+    def near_local(self):
+        links = self.links
+        return pltpu.make_async_copy(self.total(links.c), self.near, links.recv.at[self.near_spot])
+
+    def near_copy(self):
+        links = self.links
+        return links.copy(self.total(1 - links.c), self.near, links.across, self.near_spot)
+
+    def far_copy(self, half):
+        links = self.links
+        return links.copy(
+            self.total(half), self.far, {links.core: half, links.high: links.c},
+            self.out_spots[half], self.far_spot,
+        )
+
+    def hand(self):
+        links = self.links
+
+        @pl.when(links.same)
+        def _():
+            self.near_local().start()
+            self.near_copy().start()
+
+        @pl.when(~links.same)
+        def _():
+            for half in range(2):
+                self.far_copy(half).start()
+
+    def finish(self):
+        links = self.links
+        for step in range(self.n):
+            for copy in self.copies(step):
+                copy.wait_send()
+
+        @pl.when(links.same)
+        def _():
+            self.near_local().wait()
+            self.near_copy().wait_send()
+
+        @pl.when(~links.same)
+        def _():
+            self.near_copy().wait_recv()
+            for half in range(2):
+                self.far_copy(half).wait_send()
+
+        self.far_copy(0).wait_recv()
+
+
+def attention_back(links, q, k, v, grad, att, lse_ref, cos_ref, sin_ref, end_ref, d_q, d_k, d_v, heads, start):
+    length = q.shape[0]
+    n_pieces, own = end_ref.shape
+
+    def scoped(dq_acc, dk_acc, dv_acc, delta, lses):
+        def one(q_ref, k_ref, v_ref, grad_ref, att_ref, dq_ref, dk_ref, dv_ref):
+            head = pl.program_id(0) + start
+            dq_acc[...] = jnp.zeros_like(dq_acc)
+            dk_acc[...] = jnp.zeros_like(dk_acc)
+            dv_acc[...] = jnp.zeros_like(dv_acc)
+            lanes = lax.broadcasted_iota(jnp.int32, lse_ref.shape, 1)
+            mine = jnp.where(lanes == head, lse_ref[...], 0.0)
+            lses[...] = jnp.broadcast_to(jnp.sum(mine, axis=1, keepdims=True), mine.shape)
+            prod = grad_ref[...].astype(jnp.float32) * att_ref[...].astype(jnp.float32)
+            delta[...] = jnp.broadcast_to(jnp.sum(prod, axis=1, keepdims=True), prod.shape)
+
+            @pl.loop(0, n_pieces)
+            def _(i):
+                rows = pl.ds(pl.multiple_of(i * own, own), own)
+                quarter = links.swap_piece(i)
+
+                def step(n, carry):
+                    spot = pl.ds(pl.multiple_of(links.piece(n) * own, own), own)
+                    allowed = allowed_of(quarter * own, n * own, end_ref[pl.ds(n, 1), :])
+                    qb, kb, vb, gb = q_ref[rows, :], k_ref[spot, :], v_ref[spot, :], grad_ref[rows, :]
+                    scores = dot(qb, kb, NT) * (SCALE * LOG2E)
+                    probs = jnp.where(allowed, jnp.exp2(scores - lses[rows, 0:1]), 0.0)
+                    d_probs = dot(gb, vb, NT)
+                    d_scores = low(probs * (d_probs - delta[rows, 0:1]))
+                    dv_acc[spot, :] += dot(low(probs), gb, TN)
+                    dk_acc[spot, :] += dot(d_scores, qb, TN)
+                    dq_acc[rows, :] += dot(d_scores, kb)
+                    return carry
+
+                lax.fori_loop(0, quarter + 1, step, 0)
+
+            for number in range(n_pieces):
+                rows = slice(number * own, (number + 1) * own)
+                spot = pl.ds(pl.multiple_of(links.swap_piece(number) * own, own), own)
+                cos, sin = cos_ref[spot, :], sin_ref[spot, :]
+                dq_ref[rows, :] = low(spin(dq_acc[rows, :] * SCALE, cos, -sin))
+                dk_ref[rows, :] = low(spin(dk_acc[rows, :] * SCALE, cos, -sin))
+            dv_ref[...] = low(dv_acc[...])
+
+        col = pl.BlockSpec((length, HD), lambda g: (0, g + start))
+        pltpu.emit_pipeline(
+            one, grid=(heads,), in_specs=[col] * 5, out_specs=[col] * 3
+        )(q, k, v, grad, att, d_q, d_k, d_v)
+
+    wide = pltpu.VMEM((length, HD), jnp.float32)
+    pl.run_scoped(scoped, wide, wide, wide, wide, wide)
+
+
+def second_kernel(
+    places, norm2, cot, w_gate, w_up, w_down, w_out, w_qkv, norm1, q, k, v, att, hidden, x_own,
+    lse_ref, cos_ref, sin_ref, end_ref,
+    out_low, d_input, near_down, near_gate, near_up, near_out, near_qkv,
+    far_down, far_gate, far_up, far_out, far_qkv,
+    cots, act, d_gate, d_up, p_down, p_gate, p_up, p_out, p_qkv, dh, d_hidden, d_att, d_qkv,
+    mine2, other2, come2, ready2, line2, mine3, other3, come3, ready3, line3,
+    mine1, other1, come1, ready1, line1, out_mine, d_mine,
+    come_down, come_gate, come_up, come_out, come_qkv, stage0, stage1, stage_out, send, recv, local, stage_sems,
+):
+    links = Links(places, send, recv)
+    own, model = cot.shape
+    n_parts = links.n_parts
+    width = q.shape[1]
+    heads = width // HD
+    chunk = own // CHUNKS
+    trade = {links.core: links.h, links.high: links.c}
+    spread_c, spread_d = Spread(links, cots, own), Spread(links, dh, own)
+    sums2 = Sums(links, mine2, other2, come2, ready2, line2)
+    sums3 = Sums(links, mine3, other3, come3, ready3, line3)
+    sums1 = Sums(links, mine1, other1, come1, ready1, line1)
+    swap_spots = [links.take() for _ in range(CHUNKS)]
+    out_spot = links.take()
+    grad = lambda partial, come, stage, sems, near, far: Gradient(
+        links, partial, come, stage, stage_sems.at[sems], near, far
+    )
+    g_down = grad(p_down, come_down, stage0, 0, near_down, far_down)
+    g_gate = grad(p_gate, come_gate, stage1, 1, near_gate, far_gate)
+    g_up = grad(p_up, come_up, stage0, 0, near_up, far_up)
+    g_out = grad(p_out, come_out, stage_out, 2, near_out, far_out)
+    g_qkv = grad(p_qkv, come_qkv, stage1.at[:, :, pl.ds(0, 3 * width)], 1, near_qkv, far_qkv)
+
+    def piece(ref, part, other):
+        return ref.at[pl.ds((part * 2 + other) * own, own)]
+
+    near, rest = pl.ds(0, 2 * own), pl.ds(2 * own, 2 * own * (n_parts - 1))
+
+    def trade_start(src, dst, spot):
+        @pl.when(links.same)
+        def _():
+            pltpu.make_async_copy(src, dst, recv.at[spot]).start()
+
+        @pl.when(~links.same)
+        def _():
+            links.copy(src, dst, trade, spot).start()
+
+    def trade_wait(src, dst, spot):
+        @pl.when(links.same)
+        def _():
+            pltpu.make_async_copy(src, dst, recv.at[spot]).wait()
+
+        @pl.when(~links.same)
+        def _():
+            links.copy(src, dst, trade, spot).wait()
+
+    links.greet()
+    first = pltpu.make_async_copy(cot, piece(cots, 0, 0), local.at[0])
+    first.start()
+    first.wait()
+    for k_ in range(CHUNKS):
+        spread_c.own_ready(k_)
+    spread_c.wait_near()
+
+    def feed_forward(rows):
+        gated(
+            norm2.at[rows], cots.at[rows], w_gate, w_up, w_down, act.at[rows], d_gate.at[rows],
+            d_up.at[rows], min(512, 2 * own), 256,
+        )
+
+    feed_forward(near)
+    for k_ in range(CHUNKS):
+        spread_c.pass_on(k_)
+    spread_c.wait_far()
+    feed_forward(rest)
+    matmul(TN, cots, act, p_down, 1024, 512)
+    g_down.start()
+
+    def partials2(part, other, goal):
+        two_products(
+            piece(d_gate, part, other), w_gate, piece(d_up, part, other), w_up, goal.at[part], 512
+        )
+
+    def each_part(sums, make):
+        for part in reversed(range(n_parts)):
+            make(part, 1, sums.other)
+            sums.across(part).start()
+            make(part, 0, sums.mine)
+            if part:
+                sums.far(part)
+
+    each_part(sums2, partials2)
+    g_down.step(0)
+    matmul(TN, norm2, d_gate, p_gate, 1024, 512)
+    g_gate.start()
+    g_down.step(1)
+    for step in range(2, g_down.n):
+        g_down.step(step)
+
+    def hidden_back(hid, c, *refs):
+        *terms, wide_out, low_out = refs
+        total = terms[0][...].astype(jnp.float32)
+        for term in terms[1:]:
+            total = total + term[...].astype(jnp.float32)
+        made = c[...].astype(jnp.float32) + norm_back(hid[...], total)
+        wide_out[...] = made
+        low_out[...] = low(made)
+
+    for k_ in range(CHUNKS):
+        rows = pl.ds(k_ * chunk, chunk)
+        sums2.arrived(k_)
+        by_rows(
+            hidden_back, chunk // 2, [hidden.at[rows], cot.at[rows]] + sums2.terms(rows),
+            [d_hidden.at[rows], dh.at[rows]],
+        )
+        spread_d.own_ready(k_)
+
+    matmul(TN, norm2, d_up, p_up, 1024, 512)
+    g_up.start()
+
+    def partials3(part, other, goal):
+        matmul(NT, piece(act, part, other), w_down, goal.at[part], own, 512)
+
+    for part in reversed(range(n_parts)):
+        partials3(part, 1, other3)
+        sums3.across(part).start()
+        partials3(part, 0, mine3)
+    for k_ in range(CHUNKS):
+        spread_d.pass_on(k_)
+    g_gate.step(0)
+    spread_d.wait_near()
+    spread_d.wait_far()
+    matmul(NN, dh, w_out, d_att, own, width)
+    for part in reversed(range(1, n_parts)):
+        sums3.far(part)
+    matmul(TN, dh, att, p_out, 1024, width)
+    g_out.start()
+    d_q, d_k, d_v = (d_qkv.at[:, pl.ds(s * width, width)] for s in range(3))
+    half = heads // 2
+    attention_back(
+        links, q, k, v, d_att, att, lse_ref, cos_ref, sin_ref, end_ref, d_q, d_k, d_v, half, 0
+    )
+    for step in range(1, g_gate.n):
+        g_gate.step(step)
+    attention_back(
+        links, q, k, v, d_att, att, lse_ref, cos_ref, sin_ref, end_ref, d_q, d_k, d_v, heads - half, half
+    )
+
+    def partials1(part, other, goal):
+        matmul(NT, piece(d_qkv, part, other), w_qkv, goal.at[part], own, 512)
+
+    each_part(sums1, partials1)
+
+    def finish_out(hid, *refs):
+        *terms, made = refs
+        total = hid[...]
+        for term in terms:
+            total = total + term[...].astype(jnp.float32)
+        made[...] = low(total)
+
+    g_up.step(0)
+    for k_ in range(CHUNKS):
+        sums3.arrived(k_)
+    by_rows(finish_out, chunk, [hidden] + sums3.terms(pl.ds(0, own)), [out_mine])
+    matmul(TN, norm1, d_qkv, p_qkv, 1024, width)
+    g_qkv.start()
+    for step in range(1, g_up.n):
+        g_up.step(step)
+    g_out.step(0)
+
+    def input_back(x, d, *refs):
+        *terms, made = refs
+        total = terms[0][...].astype(jnp.float32)
+        for term in terms[1:]:
+            total = total + term[...].astype(jnp.float32)
+        made[...] = low(d[...] + norm_back(x[...].astype(jnp.float32), total))
+
+    for k_ in range(CHUNKS):
+        rows = pl.ds(k_ * chunk, chunk)
+        sums1.arrived(k_)
+        by_rows(
+            input_back, chunk // 2, [x_own.at[rows], d_hidden.at[rows]] + sums1.terms(rows),
+            [d_mine.at[rows]],
+        )
+        trade_start(d_mine.at[rows], d_input.at[rows], swap_spots[k_])
+    trade_start(out_mine, out_low, out_spot)
+    for step in range(1, g_out.n):
+        g_out.step(step)
+    for step in range(g_qkv.n):
+        g_qkv.step(step)
+    for k_ in range(CHUNKS):
+        rows = pl.ds(k_ * chunk, chunk)
+        trade_wait(d_mine.at[rows], d_input.at[rows], swap_spots[k_])
+    trade_wait(out_mine, out_low, out_spot)
+    for thing in (spread_c, spread_d, sums1, sums2, sums3, g_down, g_gate, g_up, g_out, g_qkv):
+        thing.finish()
+
+
+def second_half(places, norm2, cot, fulls, norm1, q, k, v, att, hidden, x_own, lse, cos, sin, end):
+    own, model = cot.shape
+    length, width = q.shape
+    w_qkv, w_out, w_gate, w_up, w_down = fulls
+    ff = w_gate.shape[1]
+    groups = 2 ** len(places[0])
+    n_parts = 2 ** len(places[3])
+    rows = model // (2 * groups)
+    shape = lambda *dims: jax.ShapeDtypeStruct(dims, jnp.bfloat16)
+    wide = lambda *dims: jax.ShapeDtypeStruct(dims, jnp.float32)
+    here, there = pl.BlockSpec(memory_space=pltpu.VMEM), pl.BlockSpec(memory_space=pl.ANY)
+    pieces = [shape(rows, cols) for cols in (ff, ff, ff, width, 3 * width)]
+    sums = [shape(n_parts, own, model)] * 3 + [shape(n_parts - 1, own, model)] * 2
+    out_shape = (
+        [shape(own, model)] * 2
+        + pieces * 2
+        + [shape(length, model)]
+        + [shape(length, ff)] * 3
+        + [shape(model, cols) for cols in (ff, ff, ff, width, 3 * width)]
+        + [shape(length, model), wide(own, model), shape(length, width), shape(length, 3 * width)]
+        + sums * 3
+        + [shape(own, model)] * 2
+    )
+    bf = lambda *dims: pltpu.VMEM(dims, jnp.bfloat16)
+    blocks = 2 * (groups - 1)
+    made = pl.pallas_call(
+        functools.partial(second_kernel, places),
+        in_specs=[there] * 14 + [here] * 4,
+        out_specs=[there] * len(out_shape),
+        out_shape=out_shape,
+        scratch_shapes=[
+            bf(blocks, rows, ff),
+            bf(blocks, rows, ff),
+            bf(blocks, rows, ff),
+            bf(blocks, rows, width),
+            bf(blocks, rows, 3 * width),
+            bf(groups, rows, ff),
+            bf(groups, rows, max(ff, 3 * width)),
+            bf(groups, rows, width),
+            pltpu.SemaphoreType.DMA((SEMS,)),
+            pltpu.SemaphoreType.DMA((SEMS,)),
+            pltpu.SemaphoreType.DMA((2,)),
+            pltpu.SemaphoreType.DMA((3, groups)),
+        ],
+        compiler_params=pltpu.CompilerParams(
+            collective_id=1, has_side_effects=True, vmem_limit_bytes=61 * 2**20
+        ),
+        cost_estimate=pl.CostEstimate(
+            flops=18 * length * model * ff, bytes_accessed=300 * 2**20, transcendentals=length * length * 4
+        ),
+    )(
+        norm2, cot, w_gate, w_up, w_down, w_out, w_qkv, norm1, q, k, v, att, hidden, x_own, lse, cos, sin, end
+    )
+    grads = [
+        a.astype(jnp.float32) + b.astype(jnp.float32) for a, b in zip(made[2:7], made[7:12])
+    ]
+    return made[0], made[1], grads
+
+
+def body(places, x, segments, padding, w_query, w_key, w_value, w_out, w_gate, w_up, w_down, cot):
+    own = x.shape[0]
+    length = segments.shape[0]
+    cols = w_query.shape[1]
+    same = lax.axis_index(places[1]) == lax.axis_index(places[2])
+    counts = [jnp.sum(segments <= number, dtype=jnp.int32) for number in range(3)]
+    last = jnp.where(segments == 0, counts[0], jnp.where(segments == 1, counts[1], counts[2])) - 1
+    end_own = jnp.where(padding == 0, last, jnp.arange(length, dtype=jnp.int32)).reshape(-1, own)
+    end = jnp.where(same, end_own, lax.ppermute(end_own, places[1], [(0, 1), (1, 0)]))
+    cos, sin = turn_tables(length)
+    mats = (jnp.concatenate([w_query, w_key, w_value], axis=1), w_out, w_gate, w_up, w_down)
+    norm1, *fulls, q, k, v, att, lse, x_own, hidden, norm2, cot_own = first_half(
+        places, x, end_own, cos, sin, mats, cot
+    )
+    output, d_input, (g_down, g_gate, g_up, g_out, g_qkv) = second_half(
+        places, norm2, cot_own, fulls, norm1, q, k, v, att, hidden, x_own, lse, cos, sin, end
+    )
+    return (
+        output,
+        d_input.astype(jnp.float32),
+        g_qkv[:, :cols],
+        g_qkv[:, cols : 2 * cols],
+        g_qkv[:, 2 * cols :],
+        g_out,
+        g_gate,
+        g_up,
+        g_down,
+    )
 
 
 def turn_tables(length):
@@ -732,139 +1245,6 @@
     return (
         jnp.asarray(np.concatenate([cos, cos], axis=1), jnp.float32),
         jnp.asarray(np.concatenate([-sin, sin], axis=1), jnp.float32),
-    )
-
-
-def flip(value, axis):
-    return lax.ppermute(value, axis, [(0, 1), (1, 0)])
-
-
-def body(places, x, segments, padding, w_query, w_key, w_value, w_out, w_gate, w_up, w_down, cot):
-    rest, core, high, lower = places
-    pair = (core, high)
-    c, h = lax.axis_index(core), lax.axis_index(high)
-    same = c == h
-    first_core = c == 0
-
-    def swap(value):
-        return lax.ppermute(value, pair, [(0, 0), (1, 2), (2, 1), (3, 3)])
-
-    def gather_low(value):
-        parts = [value]
-        for axis in reversed(lower):
-            parts = parts + [flip(part, axis) for part in parts]
-        return parts
-
-    def gather(value):
-        parts = gather_low(value)
-        return jnp.concatenate([piece for part in parts for piece in (part, flip(part, core))])
-
-    def scatter(product, n_parts, after=None):
-        far = []
-        for part in reversed(range(n_parts)):
-            mine, other = product(part)
-            far.insert(0, (mine, flip(other, core)))
-        sums = [mine.astype(jnp.float32) + other.astype(jnp.float32) for mine, other in far]
-        for axis in lower:
-            half = len(sums) // 2
-            come = [flip(low(sums[half + k]), axis) for k in range(half)]
-            if after is not None and axis == lower[-1]:
-                come = [hold(part, *after) for part in come]
-            sums = [sums[k] + come[k].astype(jnp.float32) for k in range(half)]
-        return sums[0]
-
-    def scatter_weight(partial):
-        both = lax.psum_scatter(partial, rest, scatter_dimension=0, tiled=True)
-        rows = both.shape[0] // 2
-        s0, s1 = both[:rows], both[rows:]
-        near = lax.ppermute(jnp.where(first_core, s1, s0), pair, [(0, 2), (3, 1)])
-        from0 = lax.ppermute(s0, pair, [(1, 0), (2, 1)])
-        from1 = lax.ppermute(s1, pair, [(1, 2), (2, 3)])
-        kept = jnp.where(same, jnp.where(first_core, s0, s1), near)
-        far = jnp.where(first_core, from0, from1)
-        return kept.astype(jnp.float32) + far.astype(jnp.float32)
-
-    own = x.shape[0]
-    n_parts = 2 ** len(lower)
-    length = 2 * n_parts * own
-    cols = w_query.shape[1]
-    heads = cols // HD
-    blk = min(512, own)
-
-    spot = jnp.int32(0)
-    for axis in lower:
-        spot = spot * 2 + lax.axis_index(axis)
-    quarters = []
-    for part in range(n_parts):
-        for other in (0, 1):
-            quarters.append((c ^ other) * n_parts + (spot ^ part))
-    position = jnp.concatenate([q * own + jnp.arange(own, dtype=jnp.int32) for q in quarters])
-    counts = [jnp.sum(segments <= number, dtype=jnp.int32) for number in range(3)]
-    last = jnp.where(segments == 0, counts[0], jnp.where(segments == 1, counts[1], counts[2])) - 1
-    end_own = jnp.where(padding == 0, last, jnp.arange(length, dtype=jnp.int32))
-    end = jnp.where(same, end_own, flip(end_own, core))
-    end = jnp.concatenate([lax.dynamic_slice_in_dim(end, q * own, own) for q in quarters])
-    lists = visit_lists(position, end, blk)
-    end_rows = end.reshape(-1, blk)
-    cos_all, sin_all = turn_tables(length)
-    cos = jnp.concatenate([lax.dynamic_slice_in_dim(cos_all, q * own, own) for q in quarters])
-    sin = jnp.concatenate([lax.dynamic_slice_in_dim(sin_all, q * own, own) for q in quarters])
-    mats = (jnp.concatenate([w_query, w_key, w_value], axis=1), w_out, w_gate, w_up, w_down)
-    (norm1, w_qkv, full_out, full_gate, full_up, full_down, q, k, v, attended, lse, x_low, hidden, norm2,
-     cot_own) = first_half(places, x, end_own.reshape(-1, own), cos_all, sin_all, mats, cot)
-    x_own = x_low.astype(jnp.float32)
-    norm1_pull = jax.vjp(layer_norm, x_own)[1]
-    norm2_pull = jax.vjp(layer_norm, hidden)[1]
-    cots = gather(cot_own)
-
-    def halves(product, values):
-        def of(part):
-            lo = part * 2 * own
-            both = low(product(*(value[lo : lo + 2 * own] for value in values)))
-            return both[:own], both[own:]
-
-        return of
-
-    gate = dot(norm2, full_gate)
-    up_lin = dot(norm2, full_up)
-    act, act_pull = jax.vjp(swiglu, gate, up_lin)
-    act_low = low(act)
-    d_act = dot(cots, full_down)
-    d_gate_f, d_up_f = act_pull(d_act)
-    d_gate, d_up = low(d_gate_f), low(d_up_f)
-    p_down = low(dot(cots, act_low, TN))
-    p_mlp = [halves(lambda a: dot(a, full_down, NT), (act_low,))(part) for part in range(n_parts)]
-    d_norm2 = scatter(
-        halves(lambda a, b: dot(a, full_gate, NT) + dot(b, full_up, NT), (d_gate, d_up)),
-        n_parts,
-        [p_down] + [half for part in p_mlp for half in part],
-    )
-    d_hidden = cot_own.astype(jnp.float32) + norm2_pull(d_norm2)[0]
-    p_gate = low(dot(norm2, d_gate, TN))
-    p_up = low(dot(norm2, d_up, TN))
-    d_hiddens = hold(gather(low(d_hidden)), p_gate, p_up)
-
-    mlp = scatter(lambda part: p_mlp[part], n_parts)
-    output = swap(low(hidden + mlp))
-    g_down, g_gate, g_up = scatter_weight(p_down), scatter_weight(p_gate), scatter_weight(p_up)
-
-    d_attended = low(dot(d_hiddens, full_out))
-    dq, dk, dv = attend_back(q, k, v, d_attended, attended, lse, cos, sin, end_rows, lists, heads, 1)
-    d_qkv = jnp.concatenate([dq, dk, dv], axis=1)
-    d_norm1 = scatter(halves(lambda a: dot(a, w_qkv, NT), (d_qkv,)), n_parts)
-    d_input = swap(low(d_hidden + norm1_pull(d_norm1)[0])).astype(jnp.float32)
-    g_out = scatter_weight(low(dot(d_hiddens, attended, TN)))
-    g_qkv = scatter_weight(low(dot(norm1, d_qkv, TN)))
-    return (
-        output,
-        d_input,
-        g_qkv[:, :cols],
-        g_qkv[:, cols : 2 * cols],
-        g_qkv[:, 2 * cols :],
-        g_out,
-        g_gate,
-        g_up,
-        g_down,
     )
 
 

time: 1230 us -> 1080 us (0.88)
  Pallas kernels: 418 us -> 1060 us
  waiting for transfers between devices: 349 us -> 0.01 us
  matrix products: 283 us -> 0 us
  starting transfers between devices: 59.7 us -> 0.12 us
  other arithmetic: 66 us -> 17 us
  local copies, waits for them, and re-layouts: 36.8 us -> 4.19 us
  between operations: 14.6 us -> 1.01 us
    pallas_call x1, Pallas kernels: 53 us -> 692 us  [second_half(): pl.pallas_call(functools.partial(second_kernel, places), in_specs=[there]...]
    ppermute x33 -> x1, waiting for transfers between devices: 305 us -> 0.01 us  [body(): lax.ppermute(end_own, places[1], [(0, 1), (1, 0)])]
    dot_general x17 -> x0, matrix products: 283 us -> none  [dot(): lax.dot_general(left, right, dims, preferred_element_type=jnp.float32)]
    ppermute x33 -> x1, starting transfers between devices: 59.5 us -> 0.12 us  [body(): lax.ppermute(end_own, places[1], [(0, 1), (1, 0)])]
    reduce_scatter x5 -> x0, waiting for transfers between devices: 41.7 us -> none  [scatter_weight(): both = lax.psum_scatter(partial, rest, scatter_dimension=0, tiled=True)]
    unnamed x78 -> x25, local copies, waits for them, and re-layouts: 23.1 us -> 4.18 us
    reduce_sum x7 -> x0, other arithmetic: 18.7 us -> none  [the longest x2 8.18 us: layer_norm(): centred = tok_rows - average]
  transfers between devices with their start and end apart: 38 -> 1, of which waited for: 11 -> 0; matrix products, arithmetic and copies ran while one was open for 22% -> 0% of each run, Pallas kernels for 4% -> 34%
where the time goes in v3:
time: 1080 us
  Pallas kernels  1060 us (98%)
  other arithmetic  17 us (2%)
    pallas_call x1, Pallas kernels, second_half(): pl.pallas_call(functools.partial(second_kernel, places), in_specs=[there]...  692 us
    pallas_call x1, Pallas kernels, first_half(): pl.pallas_call(functools.partial(first_kernel, places), in_specs=[there,...  366 us
  transfers between devices with their start and end apart: 1, of which 0 were waited for; matrix products, arithmetic and copies ran while one was open for 0% of the time, Pallas kernels for 34%

profile of v3, /device:TPU:1, one launch (start us, length us, event | category | flops | bytes accessed | tf_op | source)
XLA Modules:
  0.0 1079.8 jit_solution(11618557716630194328)
XLA Ops:
  0.6 1.4 convert_reduce_fusion.2
  2.0 2.7 iota_select_fusion
  4.7 0.0 copy-start.11
  4.7 0.1 collective-permute-start
  4.8 2.0 pad_maximum_fusion.w_qkv
  6.9 0.0 copy-done.11
  6.9 365.6 %shard_map.196 = (bf16[2048,2048]{1,0:T(8,128)(2,1)}, bf16[2048,1536]{1,0:T(8,128)(2,1)}, bf16[2048,512]{1,0:T(8,128)(2,1)}, bf16[2048,2048]{1,0:T(8,128)(2,1)},...) custom-call(bf16[512,2048]{1,0:T(8,128)(2,1)} %x.1, ...), custom_call_target="tpu_custom_call" | custom-call | flops 17179869184 | bytes 104857600 | tf_op jit(solution)/shard_map/pallas_call | solution.py:593
  372.5 0.0 collective-permute-done
  372.5 0.6 broadcast_select_fusion.end_ref
  373.1 691.8 %shard_map.197 = (bf16[512,2048]{1,0:T(8,128)(2,1)}, bf16[512,2048]{1,0:T(8,128)(2,1)}, bf16[256,2048]{1,0:T(8,128)(2,1)}, bf16[256,2048]{1,0:T(8,128)(2,1)}, bf...) custom-call(bf16[2048,2048]{1,0:T(8,128)(2,1)} %get-tuple-element.36, ...), custom_call_target="tpu_custom_call" | custom-call | flops 154618822656 | bytes 314572800 | tf_op jit(solution)/shard_map/pallas_call | solution.py:1177
  1064.9 0.0 copy-start.7
  1064.9 0.0 copy-start.8
  1065.0 4.2 convert_element_type.45
  1069.2 0.0 copy-start.1
  1069.2 0.0 copy-done.7
  1069.2 0.0 copy-done.8
  1069.2 0.2 convert_add_fusion.3
  1069.4 1.0 copy-done.1
  1070.4 0.3 copy-done.2
  1070.7 1.7 convert_add_fusion.2
  1072.4 0.0 copy-done.9
  1072.4 0.0 copy-done.10
  1072.4 0.0 copy-start.5
  1072.5 0.0 copy-start.6
  1072.5 1.4 fusion
  1073.9 0.4 copy-done.3
  1074.3 0.5 copy-done.4
  1074.7 0.3 copy-done.5
  1075.1 0.3 copy-done.6
  1075.4 2.8 convert_add_fusion
  1078.2 0.0 copy-done
  1078.2 1.3 copy.23
  (7 shorter events, 0.0 us)
Async XLA Ops:
  4.7 2.2 copy-start.11
  4.7 367.8 %collective-permute-start = (s32[4,512]{1,0:T(4,128)S(1)}, s32[4,512]{1,0:T(4,128)S(1)}, u32[]{:S(2)}, u32[]{:S(2)}) collective-permute-start(s32[4,512]{1,0:T(4,128)S(1)} %reshape.21.end_mine), channel_id=1, source_target_pairs={{0,4},{4,0},{1,5},{5,1},{2,6},{6,2},{3,7},{7,3},{8,12},{12,8},{9,1... | collective-permute-start | bytes 24584 | tf_op jit(solution)/shard_map/ppermute | solution.py:1219
  1064.9 4.3 copy-start.7
  1064.9 4.3 copy-start.8
  1069.2 1.2 copy-start.1
  1069.2 1.5 copy-start.2
  1070.7 1.7 copy-start.9
  1070.7 1.7 copy-start.10
  1072.4 1.8 copy-start.3
  1072.4 2.3 copy-start.4
  1072.4 2.6 copy-start.5
  1072.5 2.9 copy-start.6
  1075.4 2.8 copy-start

commit v4 on v3

--- a/solution.py
+++ b/solution.py
@@ -147,21 +147,17 @@
             self.far, self.arrive + links.c,
         )
 
-    def send_near(self):
+    def keep_near(self, src):
         links = self.links
-
-        @pl.when(links.same)
-        def _():
-            pltpu.make_async_copy(
-                self.shard, self.slot(0, links.c), links.recv.at[self.arrive + links.c]
-            ).start()
-
-        @pl.when(~links.same)
-        def _():
-            self.near_copy().start()
+        pltpu.make_async_copy(
+            src, self.slot(0, links.c), links.recv.at[self.arrive + links.c]
+        ).start()
 
     def send_far(self):
         self.far_copy().start()
+
+    def sent_far(self):
+        self.far_copy().wait_send()
 
     def stage_copies(self, step):
         for half, mask, axis, spot in self.stages[step]:
@@ -185,7 +181,6 @@
         def _():
             self.near_copy().wait_send()
 
-        self.far_copy().wait_send()
         for step in range(len(self.stages)):
             for copy in self.stage_copies(step):
                 copy.wait_send()
@@ -221,10 +216,10 @@
         n = len(self.links.lower)
         return [s for s in range(n) if (0, part, s) in self.moves]
 
-    def own_ready(self, k):
+    def own_ready(self, k, src=None):
         for step in self.first_step(0):
-            self.made(k, 0, step).start()
-        self.made(k, 0, None).start()
+            self.made(k, 0, step, src).start()
+        self.made(k, 0, None, src).start()
 
     def pass_on(self, k):
         n = len(self.links.lower)
@@ -300,7 +295,7 @@
         return links.copy(cot, cot_own, trade, cot_spot)
 
     def cot_local():
-        return pltpu.make_async_copy(cot, cot_own, recv.at[cot_spot])
+        return pltpu.make_async_copy(p_mine.at[0], cot_own, recv.at[cot_spot])
 
     end_copy = links.copy(end_mine, end_other, links.across, end_spot)
     spread1 = Spread(links, norm1_v, own)
@@ -311,23 +306,32 @@
         (part, k): links.take() for part in range(1, n_parts) for k in range(CHUNKS)
     }
 
+    rest = []
+    for number, name in enumerate(MATS[2:]):
+        shard = weights[name].shard
+        rows, cols = shard.shape
+        hold = p_other.at[number // 2, pl.ds(number % 2 * rows, rows), pl.ds(0, cols)]
+        rest.append((name, hold, pltpu.make_async_copy(shard, hold, local.at[number])))
+    cot_load = pltpu.make_async_copy(cot, p_mine.at[0], local.at[3])
+
     links.greet()
     end_copy.start()
-    weights["qkv"].send_near()
     weights["qkv"].send_far()
 
     @pl.when(links.same)
     def _():
         for k in range(CHUNKS):
             swap_local(k).start()
+        for name in MATS[:2]:
+            weights[name].keep_near(weights[name].shard)
+        for _, _, load in rest:
+            load.start()
+        cot_load.start()
 
     @pl.when(~links.same)
     def _():
-        for k in range(CHUNKS):
-            swap_copy(k).start()
-
-    for name in MATS[1:]:
-        weights[name].send_near()
+        for name in MATS:
+            weights[name].near_copy().start()
 
     def norm_chunk(k):
         rows = pl.ds(k * chunk, chunk)
@@ -345,16 +349,27 @@
         for k in range(CHUNKS):
             swap_local(k).wait()
             norm_chunk(k)
-        run("qkv", *range(last))
-        run("out", *range(last))
-        run("qkv", last)
-        run("out", last)
-        run("gate", 0)
+        for name, hold, load in rest:
+            load.wait()
+            weights[name].keep_near(hold)
+        cot_load.wait()
+        cot_local().start()
+        run("qkv", *range(last + 1))
+        run("out", *range(last + 1))
+        weights["qkv"].sent_far()
+        run("gate", *range(last + 1))
+        run("up", 0)
 
     @pl.when(~links.same)
     def _():
+        weights["qkv"].sent_far()
+        for k in range(2):
+            swap_copy(k).start()
         run("qkv", 0)
         for k in range(CHUNKS):
+            swap_copy(k).wait_send()
+            if k + 2 < CHUNKS:
+                swap_copy(k + 2).start()
             swap_copy(k).wait_recv()
             norm_chunk(k)
             if k == 1:
@@ -366,7 +381,7 @@
     for k in range(CHUNKS):
         spread1.pass_on(k)
 
-    keep = [pltpu.make_async_copy(qkv_v, qkv_all, local.at[0])]
+    keep = [pltpu.make_async_copy(qkv_v, qkv_all, local.at[4])]
     keep[0].start()
 
     def project(pieces):
@@ -385,13 +400,13 @@
                             value = spin(value, cos_ref[spot, :], sin_ref[spot, :])
                         goal[rows, pl.ds(pl.multiple_of(start + k * HD, HD), HD)] = low(value)
 
+    weights["gate"].send_far()
     spread1.wait_near()
     project((0, 1))
-    weights["gate"].send_far()
 
     @pl.when(links.same)
     def _():
-        run("gate", *range(1, last))
+        run("up", *range(1, last))
 
     @pl.when(~links.same)
     def _():
@@ -399,20 +414,19 @@
 
     spread1.wait_far()
     project(range(2, n_pieces))
-    keep.append(pltpu.make_async_copy(norm1_v, norm1, local.at[1]))
+    keep.append(pltpu.make_async_copy(norm1_v, norm1, local.at[5]))
     keep[-1].start()
-    weights["up"].send_far()
 
     @pl.when(links.same)
     def _():
-        run("gate", last)
-        run("up", 0)
+        run("up", last)
+        run("down", 0)
 
     @pl.when(~links.same)
     def _():
         run("out", *range(1, last + 1))
 
-    keep.append(pltpu.make_async_copy(out_v, out_all, local.at[2]))
+    keep.append(pltpu.make_async_copy(out_v, out_all, local.at[6]))
     keep[-1].start()
 
     lanes = lax.broadcasted_iota(jnp.int32, (own, HD), 1)
@@ -450,38 +464,23 @@
             lse_ref[rows, :] = lse if head == 0 else jnp.where(lanes == head, lse, lse_ref[rows, :])
 
         if head == 0:
-            weights["down"].send_far()
 
             @pl.when(links.same)
             def _():
-                run("up", *range(1, last))
+                run("down", *range(1, last))
 
         if head == heads // 2 - 1:
-
-            @pl.when(~links.same)
-            def _():
-                run("gate", 0)
-
-        if head == heads // 2:
-
-            @pl.when(links.same)
-            def _():
-                run("up", last)
-                run("down", 0)
-
-            @pl.when(~links.same)
-            def _():
-                run("gate", *range(1, last))
+            weights["gate"].sent_far()
+            weights["up"].send_far()
 
     @pl.when(links.same)
     def _():
-        cot_local().start()
-        run("down", *range(1, last))
+        cot_local().wait()
+        run("down", last)
 
     @pl.when(~links.same)
     def _():
-        cot_copy().start()
-        run("gate", last)
+        run("gate", 0)
 
     keep.pop(1).wait()
     spread1.finish()
@@ -524,57 +523,79 @@
                     line_copy(more, k).wait_recv()
                     total = total + line[more - 1, rows, :].astype(jnp.float32)
                 p_mine[part, rows, :] = low(total)
-                line_copy(part, k).start()
-
-    @pl.when(links.same)
-    def _():
-        run("down", last)
+                if k < 2 or part & (part - 1):
+                    line_copy(part, k).start()
 
     @pl.when(~links.same)
     def _():
-        run("up", *range(last))
-
+        run("gate", *range(1, last))
+
+    lined = [1 << step for step in range(n_low)]
     for k in range(CHUNKS):
         rows = pl.ds(k * chunk, chunk)
+        for part in lined:
+            line_copy(part, k).wait_send()
+            if k + 2 < CHUNKS:
+                line_copy(part, k + 2).start()
         total = hidden[rows, :]
-        for step in range(n_low):
-            line_copy(1 << step, k).wait_recv()
-            total = total + line[(1 << step) - 1, rows, :].astype(jnp.float32)
+        for part in lined:
+            line_copy(part, k).wait_recv()
+            total = total + line[part - 1, rows, :].astype(jnp.float32)
         hidden[rows, :] = total
         norm2_v[rows, :] = low(normed(total))
         spread2.own_ready(k)
-
-    @pl.when(~links.same)
-    def _():
-        run("up", last)
-        run("down", *range(last))
+        if k == 0:
+            weights["up"].sent_far()
+            weights["down"].send_far()
+
+        @pl.when(~links.same)
+        def _():
+            if k == 1:
+                run("gate", last)
+                run("up", 0)
+            if k == 2:
+                run("up", *range(1, last))
 
     for k in range(CHUNKS):
+
+        @pl.when(~links.same)
+        def _():
+            if k == 0:
+                run("up", last)
+            if k == 1:
+                run("down", 0)
+            if k == 2:
+                run("down", *range(1, last))
+
+        if k == 1:
+            weights["down"].sent_far()
+
+            @pl.when(~links.same)
+            def _():
+                cot_copy().start()
+
         spread2.pass_on(k)
+
     spread2.wait_near()
     spread2.wait_far()
-    keep.append(pltpu.make_async_copy(norm2_v, norm2, local.at[3]))
+    keep.append(pltpu.make_async_copy(norm2_v, norm2, local.at[7]))
     keep[-1].start()
-
-    @pl.when(links.same)
-    def _():
-        cot_local().wait()
 
     @pl.when(~links.same)
     def _():
         run("down", last)
         cot_copy().wait()
-        for k in range(CHUNKS):
-            swap_copy(k).wait_send()
 
     end_copy.wait_send()
     spread2.finish()
     for weight in weights.values():
         weight.finish()
+    weights["out"].sent_far()
     for part in range(n_parts):
         across_copy(part).wait_send()
     for part, k in line_spots:
-        line_copy(part, k).wait_send()
+        if part & (part - 1):
+            line_copy(part, k).wait_send()
     for made in keep:
         made.wait()
 
@@ -610,7 +631,7 @@
             bf(max(n_parts - 1, 1), own, model),
             pltpu.SemaphoreType.DMA((SEMS,)),
             pltpu.SemaphoreType.DMA((SEMS,)),
-            pltpu.SemaphoreType.DMA((4,)),
+            pltpu.SemaphoreType.DMA((8,)),
         ],
         compiler_params=pltpu.CompilerParams(
             collective_id=0, has_side_effects=True, vmem_limit_bytes=61 * 2**20
@@ -647,18 +668,18 @@
     )(left, right, out)
 
 
-def two_products(left1, right1, left2, right2, out, cols):
+def two_products(left1, right1, left2, right2, out, rows, cols):
     def tile(a, b, c, d, made):
         made[...] = low(dot(a[...], b[...], NT) + dot(c[...], d[...], NT))
 
-    rows, depth = left1.shape
-    held = pl.BlockSpec((rows, depth), lambda j: (0, 0))
-    moving = pl.BlockSpec((cols, depth), lambda j: (j, 0))
+    depth = left1.shape[1]
+    held = pl.BlockSpec((rows, depth), lambda i, j: (i, 0))
+    moving = pl.BlockSpec((cols, depth), lambda i, j: (j, 0))
     pltpu.emit_pipeline(
         tile,
-        grid=(out.shape[1] // cols,),
+        grid=(out.shape[0] // rows, out.shape[1] // cols),
         in_specs=[held, moving, held, moving],
-        out_specs=[pl.BlockSpec((rows, cols), lambda j: (0, j))],
+        out_specs=[pl.BlockSpec((rows, cols), lambda i, j: (i, j))],
     )(left1, right1, left2, right2, out)
 
 
@@ -705,19 +726,23 @@
 
 
 class Sums:
-    def __init__(self, links, mine, other, come, ready, line):
-        self.links, self.mine, self.other = links, mine, other
+    def __init__(self, links, made, come, ready, line):
+        self.links, self.made = links, made
         self.come, self.ready, self.line = come, ready, line
-        n_parts, self.own, _ = mine.shape
+        n_parts, self.own, _ = come.shape
+        self.n_parts = n_parts
         self.chunk = self.own // CHUNKS
         self.spots = [links.take() for _ in range(n_parts)]
         self.line_spots = {
             (part, k): links.take() for part in range(1, n_parts) for k in range(CHUNKS)
         }
 
+    def piece(self, part, other):
+        return self.made.at[pl.ds((part * 2 + other) * self.own, self.own)]
+
     def across(self, part):
         links = self.links
-        return links.copy(self.other.at[part], self.come.at[part], links.across, self.spots[part])
+        return links.copy(self.piece(part, 1), self.come.at[part], links.across, self.spots[part])
 
     def along(self, part, k):
         links = self.links
@@ -731,9 +756,9 @@
     def more(self, part):
         return [part | 1 << k for k in range(part.bit_length(), len(self.links.lower))]
 
-    def far(self, part):
+    def far(self, part, at_once=CHUNKS):
         self.across(part).wait_recv()
-        ins = [self.mine.at[part], self.come.at[part]]
+        ins = [self.piece(part, 0), self.come.at[part]]
         for number in self.more(part):
             for k in range(CHUNKS):
                 self.along(number, k).wait_recv()
@@ -746,22 +771,29 @@
             refs[-1][...] = low(total)
 
         by_rows(make, self.chunk, ins, [self.ready.at[part - 1]])
-        for k in range(CHUNKS):
+        for k in range(CHUNKS if part & (part - 1) else at_once):
             self.along(part, k).start()
 
-    def arrived(self, k):
-        if k == 0:
+    def start_late(self, first):
+        for part in self.more(0):
+            for k in range(first, CHUNKS):
+                self.along(part, k).start()
+
+    def arrived(self, chunks=range(CHUNKS)):
+        if 0 in chunks:
             self.across(0).wait_recv()
         for number in self.more(0):
-            self.along(number, k).wait_recv()
-
-    def terms(self, rows):
-        return [self.mine.at[0, rows], self.come.at[0, rows]] + [
+            for k in chunks:
+                self.along(number, k).wait_recv()
+
+    def terms(self, rows=None):
+        rows = pl.ds(0, self.own) if rows is None else rows
+        return [self.piece(0, 0).at[rows], self.come.at[0, rows]] + [
             self.line.at[number - 1, rows] for number in self.more(0)
         ]
 
     def finish(self):
-        for part in range(self.mine.shape[0]):
+        for part in range(self.n_parts):
             self.across(part).wait_send()
         for part, k in self.line_spots:
             self.along(part, k).wait_send()
@@ -958,9 +990,8 @@
     out_low, d_input, near_down, near_gate, near_up, near_out, near_qkv,
     far_down, far_gate, far_up, far_out, far_qkv,
     cots, act, d_gate, d_up, p_down, p_gate, p_up, p_out, p_qkv, dh, d_hidden, d_att, d_qkv,
-    mine2, other2, come2, ready2, line2, mine3, other3, come3, ready3, line3,
-    mine1, other1, come1, ready1, line1, out_mine, d_mine,
-    come_down, come_gate, come_up, come_out, come_qkv, stage0, stage1, stage_out, send, recv, local, stage_sems,
+    made2, come2, ready2, line2, made3, come3, ready3, line3, made1, come1, ready1, line1, out_mine, d_mine,
+    come_down, come_gate, come_up, come_out, come_qkv, stage0, stage1, stage_out, send, recv, stage_sems,
 ):
     links = Links(places, send, recv)
     own, model = cot.shape
@@ -970,11 +1001,10 @@
     chunk = own // CHUNKS
     trade = {links.core: links.h, links.high: links.c}
     spread_c, spread_d = Spread(links, cots, own), Spread(links, dh, own)
-    sums2 = Sums(links, mine2, other2, come2, ready2, line2)
-    sums3 = Sums(links, mine3, other3, come3, ready3, line3)
-    sums1 = Sums(links, mine1, other1, come1, ready1, line1)
-    swap_spots = [links.take() for _ in range(CHUNKS)]
-    out_spot = links.take()
+    sums2 = Sums(links, made2, come2, ready2, line2)
+    sums3 = Sums(links, made3, come3, ready3, line3)
+    sums1 = Sums(links, made1, come1, ready1, line1)
+    swap_spots, out_spot = [links.take(), links.take()], links.take()
     grad = lambda partial, come, stage, sems, near, far: Gradient(
         links, partial, come, stage, stage_sems.at[sems], near, far
     )
@@ -984,35 +1014,30 @@
     g_out = grad(p_out, come_out, stage_out, 2, near_out, far_out)
     g_qkv = grad(p_qkv, come_qkv, stage1.at[:, :, pl.ds(0, 3 * width)], 1, near_qkv, far_qkv)
 
-    def piece(ref, part, other):
-        return ref.at[pl.ds((part * 2 + other) * own, own)]
-
     near, rest = pl.ds(0, 2 * own), pl.ds(2 * own, 2 * own * (n_parts - 1))
 
-    def trade_start(src, dst, spot):
+    def trade_start(make, ins, src, dst, spot):
         @pl.when(links.same)
         def _():
-            pltpu.make_async_copy(src, dst, recv.at[spot]).start()
+            by_rows(make, chunk, ins, [dst])
 
         @pl.when(~links.same)
         def _():
+            by_rows(make, chunk, ins, [src])
             links.copy(src, dst, trade, spot).start()
 
     def trade_wait(src, dst, spot):
-        @pl.when(links.same)
-        def _():
-            pltpu.make_async_copy(src, dst, recv.at[spot]).wait()
-
         @pl.when(~links.same)
         def _():
             links.copy(src, dst, trade, spot).wait()
 
     links.greet()
-    first = pltpu.make_async_copy(cot, piece(cots, 0, 0), local.at[0])
-    first.start()
-    first.wait()
+    def same_rows(src, dst):
+        dst[...] = src[...]
+
     for k_ in range(CHUNKS):
-        spread_c.own_ready(k_)
+        spread_c.own_ready(k_, cot.at[pl.ds(k_ * chunk, chunk)])
+    by_rows(same_rows, chunk, [cot], [cots.at[pl.ds(0, own)]])
     spread_c.wait_near()
 
     def feed_forward(rows):
@@ -1021,129 +1046,118 @@
             d_up.at[rows], min(512, 2 * own), 256,
         )
 
+    def project_far(sums, make, at_once=CHUNKS):
+        for part in reversed(range(1, n_parts)):
+            for other in (1, 0):
+                rows = pl.ds((part * 2 + other) * own, own)
+                make(rows, sums.made.at[rows])
+                if other:
+                    sums.across(part).start()
+            sums.far(part, at_once)
+
+    def project_near(sums, make):
+        make(near, sums.made.at[near])
+        sums.across(0).start()
+
+    def partials2(rows, goal):
+        two_products(d_gate.at[rows], w_gate, d_up.at[rows], w_up, goal, own, 512)
+
+    def partials1(rows, goal):
+        matmul(NT, d_qkv.at[rows], w_qkv, goal, own, 512)
+
+    def summed(terms):
+        total = terms[0][...].astype(jnp.float32)
+        for term in terms[1:]:
+            total = total + term[...].astype(jnp.float32)
+        return total
+
+    def hidden_back(hid, c, *refs):
+        *terms, wide_out, low_out = refs
+        made = c[...].astype(jnp.float32) + norm_back(hid[...], summed(terms))
+        wide_out[...] = made
+        low_out[...] = low(made)
+
+    def finish_out(hid, *refs):
+        *terms, made = refs
+        made[...] = low(hid[...] + summed(terms))
+
+    def input_back(x, d, *refs):
+        *terms, made = refs
+        made[...] = low(d[...] + norm_back(x[...].astype(jnp.float32), summed(terms)))
+
+    def last_steps(gradient):
+        for step in range(1, gradient.n):
+            gradient.step(step)
+
     feed_forward(near)
     for k_ in range(CHUNKS):
         spread_c.pass_on(k_)
     spread_c.wait_far()
     feed_forward(rest)
+    matmul(NT, act.at[rest], w_down, made3.at[rest], 2 * own, 512)
+    for part in reversed(range(1, n_parts)):
+        sums3.across(part).start()
+    matmul(NT, act.at[near], w_down, made3.at[near], 2 * own, 512)
+    sums3.across(0).start()
+    for part in reversed(range(1, n_parts)):
+        sums3.far(part)
+    project_far(sums2, partials2)
     matmul(TN, cots, act, p_down, 1024, 512)
     g_down.start()
-
-    def partials2(part, other, goal):
-        two_products(
-            piece(d_gate, part, other), w_gate, piece(d_up, part, other), w_up, goal.at[part], 512
-        )
-
-    def each_part(sums, make):
-        for part in reversed(range(n_parts)):
-            make(part, 1, sums.other)
-            sums.across(part).start()
-            make(part, 0, sums.mine)
-            if part:
-                sums.far(part)
-
-    each_part(sums2, partials2)
+    sums3.arrived()
+    trade_start(finish_out, [hidden] + sums3.terms(), out_mine, out_low, out_spot)
+    project_near(sums2, partials2)
+    sums2.arrived()
+    by_rows(
+        hidden_back, chunk, [hidden, cot] + sums2.terms(), [d_hidden, dh.at[pl.ds(0, own)]]
+    )
+    for k_ in range(CHUNKS):
+        spread_d.own_ready(k_)
     g_down.step(0)
     matmul(TN, norm2, d_gate, p_gate, 1024, 512)
     g_gate.start()
-    g_down.step(1)
-    for step in range(2, g_down.n):
-        g_down.step(step)
-
-    def hidden_back(hid, c, *refs):
-        *terms, wide_out, low_out = refs
-        total = terms[0][...].astype(jnp.float32)
-        for term in terms[1:]:
-            total = total + term[...].astype(jnp.float32)
-        made = c[...].astype(jnp.float32) + norm_back(hid[...], total)
-        wide_out[...] = made
-        low_out[...] = low(made)
-
-    for k_ in range(CHUNKS):
-        rows = pl.ds(k_ * chunk, chunk)
-        sums2.arrived(k_)
-        by_rows(
-            hidden_back, chunk // 2, [hidden.at[rows], cot.at[rows]] + sums2.terms(rows),
-            [d_hidden.at[rows], dh.at[rows]],
-        )
-        spread_d.own_ready(k_)
-
+    last_steps(g_down)
     matmul(TN, norm2, d_up, p_up, 1024, 512)
-    g_up.start()
-
-    def partials3(part, other, goal):
-        matmul(NT, piece(act, part, other), w_down, goal.at[part], own, 512)
-
-    for part in reversed(range(n_parts)):
-        partials3(part, 1, other3)
-        sums3.across(part).start()
-        partials3(part, 0, mine3)
     for k_ in range(CHUNKS):
         spread_d.pass_on(k_)
-    g_gate.step(0)
     spread_d.wait_near()
     spread_d.wait_far()
     matmul(NN, dh, w_out, d_att, own, width)
-    for part in reversed(range(1, n_parts)):
-        sums3.far(part)
     matmul(TN, dh, att, p_out, 1024, width)
-    g_out.start()
+    g_gate.step(0)
+    g_up.start()
     d_q, d_k, d_v = (d_qkv.at[:, pl.ds(s * width, width)] for s in range(3))
     half = heads // 2
     attention_back(
         links, q, k, v, d_att, att, lse_ref, cos_ref, sin_ref, end_ref, d_q, d_k, d_v, half, 0
     )
-    for step in range(1, g_gate.n):
-        g_gate.step(step)
+    last_steps(g_gate)
     attention_back(
         links, q, k, v, d_att, att, lse_ref, cos_ref, sin_ref, end_ref, d_q, d_k, d_v, heads - half, half
     )
-
-    def partials1(part, other, goal):
-        matmul(NT, piece(d_qkv, part, other), w_qkv, goal.at[part], own, 512)
-
-    each_part(sums1, partials1)
-
-    def finish_out(hid, *refs):
-        *terms, made = refs
-        total = hid[...]
-        for term in terms:
-            total = total + term[...].astype(jnp.float32)
-        made[...] = low(total)
-
+    first = CHUNKS // 2
+    project_far(sums1, partials1, first)
     g_up.step(0)
-    for k_ in range(CHUNKS):
-        sums3.arrived(k_)
-    by_rows(finish_out, chunk, [hidden] + sums3.terms(pl.ds(0, own)), [out_mine])
+    g_out.start()
+    project_near(sums1, partials1)
+    sums1.start_late(first)
     matmul(TN, norm1, d_qkv, p_qkv, 1024, width)
     g_qkv.start()
-    for step in range(1, g_up.n):
-        g_up.step(step)
+    last_steps(g_up)
     g_out.step(0)
-
-    def input_back(x, d, *refs):
-        *terms, made = refs
-        total = terms[0][...].astype(jnp.float32)
-        for term in terms[1:]:
-            total = total + term[...].astype(jnp.float32)
-        made[...] = low(d[...] + norm_back(x[...].astype(jnp.float32), total))
-
-    for k_ in range(CHUNKS):
-        rows = pl.ds(k_ * chunk, chunk)
-        sums1.arrived(k_)
-        by_rows(
-            input_back, chunk // 2, [x_own.at[rows], d_hidden.at[rows]] + sums1.terms(rows),
-            [d_mine.at[rows]],
+    for n, chunks in enumerate((range(first), range(first, CHUNKS))):
+        rows = pl.ds(chunks[0] * chunk, len(chunks) * chunk)
+        sums1.arrived(chunks)
+        trade_start(
+            input_back, [x_own.at[rows], d_hidden.at[rows]] + sums1.terms(rows), d_mine.at[rows],
+            d_input.at[rows], swap_spots[n],
         )
-        trade_start(d_mine.at[rows], d_input.at[rows], swap_spots[k_])
-    trade_start(out_mine, out_low, out_spot)
-    for step in range(1, g_out.n):
-        g_out.step(step)
-    for step in range(g_qkv.n):
-        g_qkv.step(step)
-    for k_ in range(CHUNKS):
-        rows = pl.ds(k_ * chunk, chunk)
-        trade_wait(d_mine.at[rows], d_input.at[rows], swap_spots[k_])
+    last_steps(g_out)
+    g_qkv.step(0)
+    last_steps(g_qkv)
+    for n in range(2):
+        rows = pl.ds(n * first * chunk, first * chunk)
+        trade_wait(d_mine.at[rows], d_input.at[rows], swap_spots[n])
     trade_wait(out_mine, out_low, out_spot)
     for thing in (spread_c, spread_d, sums1, sums2, sums3, g_down, g_gate, g_up, g_out, g_qkv):
         thing.finish()
@@ -1161,7 +1175,7 @@
     wide = lambda *dims: jax.ShapeDtypeStruct(dims, jnp.float32)
     here, there = pl.BlockSpec(memory_space=pltpu.VMEM), pl.BlockSpec(memory_space=pl.ANY)
     pieces = [shape(rows, cols) for cols in (ff, ff, ff, width, 3 * width)]
-    sums = [shape(n_parts, own, model)] * 3 + [shape(n_parts - 1, own, model)] * 2
+    sums = [shape(length, model), shape(n_parts, own, model)] + [shape(n_parts - 1, own, model)] * 2
     out_shape = (
         [shape(own, model)] * 2
         + pieces * 2
@@ -1190,8 +1204,7 @@
             bf(groups, rows, width),
             pltpu.SemaphoreType.DMA((SEMS,)),
             pltpu.SemaphoreType.DMA((SEMS,)),
-            pltpu.SemaphoreType.DMA((2,)),
-            pltpu.SemaphoreType.DMA((3, groups)),
+                        pltpu.SemaphoreType.DMA((3, groups)),
         ],
         compiler_params=pltpu.CompilerParams(
             collective_id=1, has_side_effects=True, vmem_limit_bytes=61 * 2**20

time: 1080 us -> 966 us (0.89)
  Pallas kernels: 1060 us -> 939 us
    pallas_call x1, Pallas kernels: 692 us -> 572 us  [second_half(): pl.pallas_call(functools.partial(second_kernel, places), in_specs=[there]...]
  transfers between devices with their start and end apart: 1 -> 1, of which waited for: 0 -> 0; matrix products, arithmetic and copies ran while one was open for 0% -> 0% of each run, Pallas kernels for 34% -> 38%
where the time goes in v4:
time: 966 us; the launch traced here: 961 us
  Pallas kernels  939 us (97%)
  other arithmetic  17 us (2%)
    pallas_call x1, Pallas kernels, second_half(): pl.pallas_call(functools.partial(second_kernel, places), in_specs=[there]...  572 us
    pallas_call x1, Pallas kernels, first_half(): pl.pallas_call(functools.partial(first_kernel, places), in_specs=[there,...  367 us
  transfers between devices with their start and end apart: 1, of which 0 were waited for; matrix products, arithmetic and copies ran while one was open for 0% of the time, Pallas kernels for 38%

profile of v4, /device:TPU:1, one launch (start us, length us, event | category | flops | bytes accessed | tf_op | source)
XLA Modules:
  0.0 961.2 jit_solution(9383199913178537969)
XLA Ops:
  0.6 1.4 convert_reduce_fusion.2
  2.0 2.7 iota_select_fusion
  4.7 0.0 copy-start.11
  4.7 0.1 collective-permute-start
  4.8 2.0 pad_maximum_fusion.w_qkv
  6.9 0.0 copy-done.11
  6.9 367.0 %shard_map.196 = (bf16[2048,2048]{1,0:T(8,128)(2,1)}, bf16[2048,1536]{1,0:T(8,128)(2,1)}, bf16[2048,512]{1,0:T(8,128)(2,1)}, bf16[2048,2048]{1,0:T(8,128)(2,1)},...) custom-call(bf16[512,2048]{1,0:T(8,128)(2,1)} %x.1, ...), custom_call_target="tpu_custom_call" | custom-call | flops 17179869184 | bytes 104857600 | tf_op jit(solution)/shard_map/pallas_call | solution.py:614
  373.9 0.0 collective-permute-done
  373.9 0.6 broadcast_select_fusion.end_ref
  374.5 571.9 %shard_map.197 = (bf16[512,2048]{1,0:T(8,128)(2,1)}, bf16[512,2048]{1,0:T(8,128)(2,1)}, bf16[256,2048]{1,0:T(8,128)(2,1)}, bf16[256,2048]{1,0:T(8,128)(2,1)}, bf...) custom-call(bf16[2048,2048]{1,0:T(8,128)(2,1)} %get-tuple-element.36, ...), custom_call_target="tpu_custom_call" | custom-call | flops 154618822656 | bytes 314572800 | tf_op jit(solution)/shard_map/pallas_call | solution.py:1191
  946.4 0.0 copy-start.7
  946.4 0.0 copy-start.8
  946.4 4.2 convert_element_type.45
  950.7 0.0 copy-start.1
  950.7 0.0 copy-done.7
  950.7 0.0 copy-done.8
  950.7 0.2 convert_add_fusion.3
  950.9 1.0 copy-done.1
  951.9 0.3 copy-done.2
  952.2 1.7 convert_add_fusion.2
  953.9 0.0 copy-done.9
  953.9 0.0 copy-done.10
  953.9 0.0 copy-start.5
  953.9 0.0 copy-start.6
  953.9 1.4 fusion
  955.3 0.4 copy-done.3
  955.7 0.5 copy-done.4
  956.2 0.3 copy-done.5
  956.5 0.3 copy-done.6
  956.8 2.8 convert_add_fusion
  959.7 0.0 copy-done
  959.7 1.3 copy.23
  (7 shorter events, 0.0 us)
Async XLA Ops:
  4.7 2.2 copy-start.11
  4.7 369.2 %collective-permute-start = (s32[4,512]{1,0:T(4,128)S(1)}, s32[4,512]{1,0:T(4,128)S(1)}, u32[]{:S(2)}, u32[]{:S(2)}) collective-permute-start(s32[4,512]{1,0:T(4,128)S(1)} %reshape.21.end_mine), channel_id=1, source_target_pairs={{0,4},{4,0},{1,5},{5,1},{2,6},{6,2},{3,7},{7,3},{8,12},{12,8},{9,1... | collective-permute-start | bytes 24584 | tf_op jit(solution)/shard_map/ppermute | solution.py:1232
  946.4 4.3 copy-start.7
  946.4 4.3 copy-start.8
  950.7 1.2 copy-start.1
  950.7 1.5 copy-start.2
  952.2 1.7 copy-start.9
  952.2 1.7 copy-start.10
  953.9 1.8 copy-start.3
  953.9 2.3 copy-start.4
  953.9 2.6 copy-start.5
  953.9 2.9 copy-start.6
  956.8 2.8 copy-start

commit v5 on v4

--- a/solution.py
+++ b/solution.py
@@ -24,16 +24,20 @@
 def low(value):
     return value.astype(jnp.bfloat16)
 
-def allowed_of(first_q, first_k, end_row):
+
+def allowed_of(first_q, first_k, end_row, diagonal):
     blk = end_row.shape[1]
     t = first_q + lax.broadcasted_iota(jnp.int32, (blk, 1), 0)
+    if not diagonal:
+        return t <= end_row
     u = first_k + lax.broadcasted_iota(jnp.int32, (1, blk), 1)
     return (u <= t) & (t <= end_row)
 
 
 MESH = pl.DeviceIdType.MESH
 CHUNKS = 4
-SEMS = 224
+FINE = 8
+SEMS = 320
 MATS = ("qkv", "out", "gate", "up", "down")
 
 
@@ -187,11 +191,11 @@
 
 
 class Spread:
-    def __init__(self, links, full, own):
-        self.links, self.full, self.own, self.chunk = links, full, own, own // CHUNKS
-        self.moves = {}
+    def __init__(self, links, full, own, chunks):
+        self.links, self.full, self.own, self.chunk = links, full, own, own // chunks
+        self.moves, self.chunks = {}, chunks
         n = len(links.lower)
-        for k in range(CHUNKS):
+        for k in range(chunks):
             have = [0]
             for step in range(n):
                 value = 2 ** (n - 1 - step)
@@ -234,11 +238,11 @@
                     self.made(k, goal, None).start()
 
     def wait_near(self):
-        for k in range(CHUNKS):
+        for k in range(self.chunks):
             self.made(k, 0, None).wait_recv()
 
     def wait_far(self):
-        for k in range(CHUNKS):
+        for k in range(self.chunks):
             for part in range(1, self.links.n_parts):
                 self.made(k, part, None).wait_recv()
 
@@ -267,7 +271,7 @@
     own = x.shape[0]
     n_parts, n_pieces = links.n_parts, 2 * links.n_parts
     n_low = len(links.lower)
-    chunk = own // CHUNKS
+    chunk = own // FINE
     heads = q_ref.shape[1] // HD
     width = heads * HD
     weights = {
@@ -279,7 +283,7 @@
         )
     }
     n_steps = len(links.rest)
-    swap_spots = [links.take() for _ in range(CHUNKS)]
+    swap_spots = [links.take() for _ in range(FINE)]
     cot_spot, end_spot = links.take(), links.take()
     trade = {links.core: links.h, links.high: links.c}
 
@@ -298,12 +302,12 @@
         return pltpu.make_async_copy(p_mine.at[0], cot_own, recv.at[cot_spot])
 
     end_copy = links.copy(end_mine, end_other, links.across, end_spot)
-    spread1 = Spread(links, norm1_v, own)
+    spread1 = Spread(links, norm1_v, own, FINE)
     norm2_v = norm1_v
-    spread2 = Spread(links, norm2_v, own)
+    spread2 = Spread(links, norm2_v, own, FINE)
     across_spots = [links.take() for _ in range(n_parts)]
     line_spots = {
-        (part, k): links.take() for part in range(1, n_parts) for k in range(CHUNKS)
+        (part, k): links.take() for part in range(1, n_parts) for k in range(FINE)
     }
 
     rest = []
@@ -320,7 +324,7 @@
 
     @pl.when(links.same)
     def _():
-        for k in range(CHUNKS):
+        for k in range(FINE):
             swap_local(k).start()
         for name in MATS[:2]:
             weights[name].keep_near(weights[name].shard)
@@ -346,7 +350,7 @@
 
     @pl.when(links.same)
     def _():
-        for k in range(CHUNKS):
+        for k in range(FINE):
             swap_local(k).wait()
             norm_chunk(k)
         for name, hold, load in rest:
@@ -366,9 +370,9 @@
         for k in range(2):
             swap_copy(k).start()
         run("qkv", 0)
-        for k in range(CHUNKS):
+        for k in range(FINE):
             swap_copy(k).wait_send()
-            if k + 2 < CHUNKS:
+            if k + 2 < FINE:
                 swap_copy(k + 2).start()
             swap_copy(k).wait_recv()
             norm_chunk(k)
@@ -378,7 +382,7 @@
 
     weights["out"].send_far()
     end_copy.wait_recv()
-    for k in range(CHUNKS):
+    for k in range(FINE):
         spread1.pass_on(k)
 
     keep = [pltpu.make_async_copy(qkv_v, qkv_all, local.at[4])]
@@ -400,9 +404,9 @@
                             value = spin(value, cos_ref[spot, :], sin_ref[spot, :])
                         goal[rows, pl.ds(pl.multiple_of(start + k * HD, HD), HD)] = low(value)
 
-    weights["gate"].send_far()
     spread1.wait_near()
     project((0, 1))
+    weights["gate"].send_far()
 
     @pl.when(links.same)
     def _():
@@ -438,11 +442,11 @@
             rows = pl.ds(pl.multiple_of(i * own, own), own)
             quarter = links.swap_piece(i)
 
-            def step(n, carry):
+            def step(diagonal, n, carry):
                 top, total, acc = carry
                 spot = pl.ds(pl.multiple_of(links.piece(n) * own, own), own)
                 end = jnp.where(links.same, end_mine[pl.ds(n, 1), :], end_other[pl.ds(n, 1), :])
-                allowed = allowed_of(quarter * own, n * own, end)
+                allowed = allowed_of(quarter * own, n * own, end, diagonal)
                 scores = dot(q_ref[rows, cols], k_ref[spot, cols], NT)
                 scores = jnp.where(allowed, scores * (SCALE * LOG2E), NEG)
                 new_top = jnp.maximum(top, jnp.max(scores, axis=1, keepdims=True))
@@ -451,14 +455,15 @@
                 total = total * shrink + jnp.sum(grown, axis=1, keepdims=True)
                 return new_top, total, acc * shrink + dot(low(grown), v_ref[spot, cols])
 
-            top, total, acc = lax.fori_loop(
-                0, quarter + 1, step,
+            carry = lax.fori_loop(
+                0, quarter, functools.partial(step, False),
                 (
                     jnp.full((own, 1), NEG, jnp.float32),
                     jnp.zeros((own, 1), jnp.float32),
                     jnp.zeros((own, HD), jnp.float32),
                 ),
             )
+            top, total, acc = step(True, quarter, carry)
             att_ref[rows, cols] = low(acc / total)
             lse = jnp.broadcast_to(top + jnp.log2(total), (own, HD))
             lse_ref[rows, :] = lse if head == 0 else jnp.where(lanes == head, lse, lse_ref[rows, :])
@@ -511,7 +516,7 @@
         across_copy(part).start()
         out_rows(part * 2, p_mine.at[part])
         across_copy(part).wait_recv()
-        for k in range(CHUNKS):
+        for k in range(FINE):
             rows = pl.ds(k * chunk, chunk)
             total = p_mine[part, rows, :].astype(jnp.float32) + p_come[part, rows, :].astype(jnp.float32)
             if part == 0:
@@ -531,11 +536,11 @@
         run("gate", *range(1, last))
 
     lined = [1 << step for step in range(n_low)]
-    for k in range(CHUNKS):
+    for k in range(FINE):
         rows = pl.ds(k * chunk, chunk)
         for part in lined:
             line_copy(part, k).wait_send()
-            if k + 2 < CHUNKS:
+            if k + 2 < FINE:
                 line_copy(part, k + 2).start()
         total = hidden[rows, :]
         for part in lined:
@@ -550,24 +555,24 @@
 
         @pl.when(~links.same)
         def _():
-            if k == 1:
+            if k == 2:
                 run("gate", last)
                 run("up", 0)
-            if k == 2:
+            if k == 4:
                 run("up", *range(1, last))
 
-    for k in range(CHUNKS):
+    for k in range(FINE):
 
         @pl.when(~links.same)
         def _():
             if k == 0:
                 run("up", last)
-            if k == 1:
+            if k == 2:
                 run("down", 0)
-            if k == 2:
+            if k == 4:
                 run("down", *range(1, last))
 
-        if k == 1:
+        if k == 2:
             weights["down"].sent_far()
 
             @pl.when(~links.same)
@@ -952,9 +957,9 @@
                 rows = pl.ds(pl.multiple_of(i * own, own), own)
                 quarter = links.swap_piece(i)
 
-                def step(n, carry):
+                def step(diagonal, n, carry):
                     spot = pl.ds(pl.multiple_of(links.piece(n) * own, own), own)
-                    allowed = allowed_of(quarter * own, n * own, end_ref[pl.ds(n, 1), :])
+                    allowed = allowed_of(quarter * own, n * own, end_ref[pl.ds(n, 1), :], diagonal)
                     qb, kb, vb, gb = q_ref[rows, :], k_ref[spot, :], v_ref[spot, :], grad_ref[rows, :]
                     scores = dot(qb, kb, NT) * (SCALE * LOG2E)
                     probs = jnp.where(allowed, jnp.exp2(scores - lses[rows, 0:1]), 0.0)
@@ -965,7 +970,8 @@
                     dq_acc[rows, :] += dot(d_scores, kb)
                     return carry
 
-                lax.fori_loop(0, quarter + 1, step, 0)
+                lax.fori_loop(0, quarter, functools.partial(step, False), 0)
+                step(True, quarter, 0)
 
             for number in range(n_pieces):
                 rows = slice(number * own, (number + 1) * own)
@@ -1000,7 +1006,7 @@
     heads = width // HD
     chunk = own // CHUNKS
     trade = {links.core: links.h, links.high: links.c}
-    spread_c, spread_d = Spread(links, cots, own), Spread(links, dh, own)
+    spread_c, spread_d = Spread(links, cots, own, CHUNKS), Spread(links, dh, own, CHUNKS)
     sums2 = Sums(links, made2, come2, ready2, line2)
     sums3 = Sums(links, made3, come3, ready3, line3)
     sums1 = Sums(links, made1, come1, ready1, line1)
@@ -1123,11 +1129,11 @@
     spread_d.wait_near()
     spread_d.wait_far()
     matmul(NN, dh, w_out, d_att, own, width)
-    matmul(TN, dh, att, p_out, 1024, width)
     g_gate.step(0)
     g_up.start()
+    matmul(TN, dh, att, p_out, 1024, width)
     d_q, d_k, d_v = (d_qkv.at[:, pl.ds(s * width, width)] for s in range(3))
-    half = heads // 2
+    half = 1
     attention_back(
         links, q, k, v, d_att, att, lse_ref, cos_ref, sin_ref, end_ref, d_q, d_k, d_v, half, 0
     )
@@ -1136,14 +1142,14 @@
         links, q, k, v, d_att, att, lse_ref, cos_ref, sin_ref, end_ref, d_q, d_k, d_v, heads - half, half
     )
     first = CHUNKS // 2
+    g_up.step(0)
     project_far(sums1, partials1, first)
-    g_up.step(0)
+    last_steps(g_up)
     g_out.start()
     project_near(sums1, partials1)
     sums1.start_late(first)
     matmul(TN, norm1, d_qkv, p_qkv, 1024, width)
     g_qkv.start()
-    last_steps(g_up)
     g_out.step(0)
     for n, chunks in enumerate((range(first), range(first, CHUNKS))):
         rows = pl.ds(chunks[0] * chunk, len(chunks) * chunk)
@@ -1215,16 +1221,40 @@
     )(
         norm2, cot, w_gate, w_up, w_down, w_out, w_qkv, norm1, q, k, v, att, hidden, x_own, lse, cos, sin, end
     )
-    grads = [
-        a.astype(jnp.float32) + b.astype(jnp.float32) for a, b in zip(made[2:7], made[7:12])
-    ]
-    return made[0], made[1], grads
+    return made[:12]
+
+
+def last_kernel(*refs):
+    d_low, near, far = refs[0], refs[1:6], refs[6:11]
+    d_input, g_query, g_key, g_value, g_out, g_gate, g_up, g_down = refs[11:]
+    add = lambda k: near[k][...].astype(jnp.float32) + far[k][...].astype(jnp.float32)
+    d_input[...] = d_low[...].astype(jnp.float32)
+    g_down[...], g_gate[...], g_up[...], g_out[...] = add(0), add(1), add(2), add(3)
+    cols = g_query.shape[1]
+    for k, goal in enumerate((g_query, g_key, g_value)):
+        here = slice(k * cols, (k + 1) * cols)
+        goal[...] = near[4][:, here].astype(jnp.float32) + far[4][:, here].astype(jnp.float32)
+
+
+def last_sums(d_low, near, far, steps):
+    wide = lambda ref, cols: jax.ShapeDtypeStruct((ref.shape[0], cols), jnp.float32)
+    rows = lambda ref: pl.BlockSpec((ref.shape[0] // steps, ref.shape[1]), lambda i: (i, 0))
+    cols = near[3].shape[1]
+    outs = [wide(d_low, d_low.shape[1])] + [wide(near[3], cols)] * 4
+    outs += [wide(near[k], near[k].shape[1]) for k in (1, 2, 0)]
+    return pl.pallas_call(
+        last_kernel,
+        grid=(steps,),
+        in_specs=[rows(ref) for ref in (d_low, *near, *far)],
+        out_specs=[rows(ref) for ref in outs],
+        out_shape=outs,
+        compiler_params=pltpu.CompilerParams(vmem_limit_bytes=61 * 2**20),
+    )(d_low, *near, *far)
 
 
 def body(places, x, segments, padding, w_query, w_key, w_value, w_out, w_gate, w_up, w_down, cot):
     own = x.shape[0]
     length = segments.shape[0]
-    cols = w_query.shape[1]
     same = lax.axis_index(places[1]) == lax.axis_index(places[2])
     counts = [jnp.sum(segments <= number, dtype=jnp.int32) for number in range(3)]
     last = jnp.where(segments == 0, counts[0], jnp.where(segments == 1, counts[1], counts[2])) - 1
@@ -1235,20 +1265,10 @@
     norm1, *fulls, q, k, v, att, lse, x_own, hidden, norm2, cot_own = first_half(
         places, x, end_own, cos, sin, mats, cot
     )
-    output, d_input, (g_down, g_gate, g_up, g_out, g_qkv) = second_half(
+    output, d_low, *terms = second_half(
         places, norm2, cot_own, fulls, norm1, q, k, v, att, hidden, x_own, lse, cos, sin, end
     )
-    return (
-        output,
-        d_input.astype(jnp.float32),
-        g_qkv[:, :cols],
-        g_qkv[:, cols : 2 * cols],
-        g_qkv[:, 2 * cols :],
-        g_out,
-        g_gate,
-        g_up,
-        g_down,
-    )
+    return (output, *last_sums(d_low, terms[:5], terms[5:], 4))
 
 
 def turn_tables(length):

time: 966 us -> 954 us (0.988)
  other arithmetic: 17 us -> 6.68 us
  transfers between devices with their start and end apart: 1 -> 1, of which waited for: 0 -> 0; matrix products, arithmetic and copies ran while one was open for 0% -> 0% of each run, Pallas kernels for 38% -> 39%
where the time goes in v5:
time: 954 us; the launch traced here: 949 us
  Pallas kernels  940 us (99%)
    pallas_call x1, Pallas kernels, second_half(): pl.pallas_call(functools.partial(second_kernel, places), in_specs=[there]...  563 us
    pallas_call x1, Pallas kernels, first_half(): pl.pallas_call(functools.partial(first_kernel, places), in_specs=[there,...  367 us
  transfers between devices with their start and end apart: 1, of which 0 were waited for; matrix products, arithmetic and copies ran while one was open for 0% of the time, Pallas kernels for 39%

profile of v5, /device:TPU:1, one launch (start us, length us, event | category | flops | bytes accessed | tf_op | source)
XLA Modules:
  0.0 948.9 jit_solution(6851242168941526063)
XLA Ops:
  0.6 1.4 convert_reduce_fusion.2
  2.0 2.7 iota_select_fusion
  4.7 0.0 copy-start.1
  4.7 0.1 collective-permute-start
  4.8 2.0 pad_maximum_fusion.w_qkv
  6.9 0.0 copy-done.1
  6.9 367.3 %shard_map.196 = (bf16[2048,2048]{1,0:T(8,128)(2,1)}, bf16[2048,1536]{1,0:T(8,128)(2,1)}, bf16[2048,512]{1,0:T(8,128)(2,1)}, bf16[2048,2048]{1,0:T(8,128)(2,1)},...) custom-call(bf16[512,2048]{1,0:T(8,128)(2,1)} %x.1, ...), custom_call_target="tpu_custom_call" | custom-call | flops 17179869184 | bytes 104857600 | tf_op jit(solution)/shard_map/pallas_call | solution.py:619
  374.2 0.0 collective-permute-done
  374.2 0.6 broadcast_select_fusion.end_ref
  374.8 563.3 %shard_map.197 = (bf16[512,2048]{1,0:T(8,128)(2,1)}, bf16[512,2048]{1,0:T(8,128)(2,1)}, bf16[256,2048]{1,0:T(8,128)(2,1)}, bf16[256,2048]{1,0:T(8,128)(2,1)}, bf...) custom-call(bf16[2048,2048]{1,0:T(8,128)(2,1)} %get-tuple-element.44, ...), custom_call_target="tpu_custom_call" | custom-call | flops 154618822656 | bytes 314572800 | tf_op jit(solution)/shard_map/pallas_call | solution.py:1197
  938.1 0.0 copy-start
  938.1 9.0 shard_map.198
  947.2 0.0 copy-done
  947.2 1.3 copy.23
  (1 shorter events, 0.0 us)
Async XLA Ops:
  4.7 2.2 copy-start.1
  4.7 369.5 %collective-permute-start = (s32[4,512]{1,0:T(4,128)S(1)}, s32[4,512]{1,0:T(4,128)S(1)}, u32[]{:S(2)}, u32[]{:S(2)}) collective-permute-start(s32[4,512]{1,0:T(4,128)S(1)} %reshape.21.end_mine), channel_id=1, source_target_pairs={{0,4},{4,0},{1,5},{5,1},{2,6},{6,2},{3,7},{7,3},{8,12},{12,8},{9,1... | collective-permute-start | bytes 24584 | tf_op jit(solution)/shard_map/ppermute | solution.py:1262
  938.1 9.1 copy-start
